TPU v7x, 128 devices: a whole 4x4x4 slice. The times are simulated.
128 devices in a mesh: blk: 32 (over x, y, core), grp: 4 (over z).
Axes of the slice: x: 4, y: 4, z: 4, core: 2. Of those that a mesh axis runs over, the one named last changes fastest.
Arguments:
- populations: bfloat16 [1024, 19, 32, 1024], P(('blk', 'grp')), may hold values from 0.59765625 to 1.3984375
- solute: float32 [1024, 32, 1024], P(('blk', 'grp')), may hold values from 0 to 2
- solid_fraction: float32 [1024, 32, 1024], P(('blk', 'grp')), may hold values from 0.05 to 0.95
- neighbours: int32 [1024, 6], P(('blk', 'grp')), may hold values from 0 to 1023, as said below
- front_list: int32 [384], P(('blk', 'grp')), may hold values from 0 to 1023, as said below
- redeal_list: int32 [384], P(('blk', 'grp')), may hold values from 0 to 1023, as said below
Outputs:
- new_populations: bfloat16 [1024, 19, 32, 1024], P(('blk', 'grp'))
- new_solute: float32 [1024, 32, 1024], P(('blk', 'grp'))
- new_solid: float32 [1024, 32, 1024], P(('blk', 'grp'))
Inputs may be any that keep to these rules, and one draw needn't show every extreme that they name: `neighbours`: the lists are symmetric: a block is the -x neighbour of its +x neighbour, and likewise for y and z. Every neighbour lies on another device with the same grp index. For each of the three directions, at most 1 block of one device have a neighbour in that direction (across either face) on any one other device, and some pair of devices reaches 1. `front_list`: the 3 entries stored on a device name distinct blocks of that device. Each device sends exactly one of its front blocks to each other device with the same blk index; every target is a block of the receiving device's front_list entries, each reached exactly once, so redeal_list is a permutation of front_list.
All inputs are finite; a program needn't handle non-finite values.
Results may differ from a plain program's by a relative error of at most 0.001.
Values may be sent and summed in bfloat16 or wider, within the bound.
A program may use at most 192 MiB of HBM per device.

v0:
```python
import jax
import jax.numpy as jnp
from jax import lax
from jax.sharding import PartitionSpec as P

VELOCITY = (
    (0, 0, 0),
    (1, 0, 0),
    (-1, 0, 0),
    (0, 1, 0),
    (0, -1, 0),
    (0, 0, 1),
    (0, 0, -1),
    (1, 1, 0),
    (-1, -1, 0),
    (1, -1, 0),
    (-1, 1, 0),
    (1, 0, 1),
    (-1, 0, -1),
    (1, 0, -1),
    (-1, 0, 1),
    (0, 1, 1),
    (0, -1, -1),
    (0, 1, -1),
    (0, -1, 1),
)
WEIGHTS = (1.0 / 3.0,) + (1.0 / 18.0,) * 6 + (1.0 / 36.0,) * 12
OPPOSITE = (0, 2, 1, 4, 3, 6, 5, 8, 7, 10, 9, 12, 11, 14, 13, 16, 15, 18, 17)
PLUS_X = (1, 7, 9, 11, 13)
MINUS_X = (2, 8, 10, 12, 14)
PLUS_Y = (3, 7, 10, 15, 17)
MINUS_Y = (4, 8, 9, 16, 18)
PLUS_Z = (5, 11, 14, 15, 18)
MINUS_Z = (6, 12, 13, 16, 17)
relax_time = 0.8
diffusivity = 0.1
rate_const = 0.5
saturation = 1.0


def face_planes(populations, solute, chosen_plus, chosen_minus, axis_id):
    block_count, velocities, extent, cell_count = populations.shape
    cube_view = populations.reshape(block_count, velocities, extent, extent, extent)
    solute_cube = solute.reshape(block_count, extent, extent, extent)
    top_index = extent - 1
    if axis_id == 0:
        upper_face, lower_face = (cube_view[:, :, top_index], cube_view[:, :, 0])
        solute_upper, solute_lower = (solute_cube[:, top_index], solute_cube[:, 0])
    elif axis_id == 1:
        upper_face, lower_face = (cube_view[:, :, :, top_index], cube_view[:, :, :, 0])
        solute_upper, solute_lower = (solute_cube[:, :, top_index], solute_cube[:, :, 0])
    else:
        upper_face, lower_face = (cube_view[..., top_index], cube_view[..., 0])
        solute_upper, solute_lower = (solute_cube[..., top_index], solute_cube[..., 0])
    upper_face = jnp.stack([upper_face[:, member] for member in chosen_plus], axis=1)
    lower_face = jnp.stack([lower_face[:, member] for member in chosen_minus], axis=1)
    return (
        upper_face.reshape(block_count, len(chosen_plus), cell_count),
        lower_face.reshape(block_count, len(chosen_minus), cell_count),
        solute_upper.reshape(block_count, cell_count),
        solute_lower.reshape(block_count, cell_count),
    )


def edges_y(ghost_xlo, ghost_xhi, extent):
    block_count = ghost_xlo.shape[0]
    lower_view = ghost_xlo.reshape(block_count, 5, extent, extent)
    upper_view = ghost_xhi.reshape(block_count, 5, extent, extent)
    top_index = extent - 1
    rows_upper = jnp.stack([lower_view[:, 1, top_index], upper_view[:, 2, top_index]], axis=1)
    rows_lower = jnp.stack([lower_view[:, 2, 0], upper_view[:, 1, 0]], axis=1)
    return (rows_upper, rows_lower)


def edges_z(ghost_xlo, ghost_xhi, ghost_ylo, ghost_yhi, extent):
    block_count = ghost_xlo.shape[0]
    xlo_view = ghost_xlo.reshape(block_count, 5, extent, extent)
    xhi_view = ghost_xhi.reshape(block_count, 5, extent, extent)
    ylo_view = ghost_ylo.reshape(block_count, 5, extent, extent)
    yhi_view = ghost_yhi.reshape(block_count, 5, extent, extent)
    top_index = extent - 1
    rows_upper = jnp.stack(
        [
            xlo_view[:, 3, :, top_index],
            xhi_view[:, 4, :, top_index],
            ylo_view[:, 3, :, top_index],
            yhi_view[:, 4, :, top_index],
        ],
        axis=1,
    )
    rows_lower = jnp.stack(
        [xlo_view[:, 4, :, 0], xhi_view[:, 3, :, 0], ylo_view[:, 4, :, 0], yhi_view[:, 3, :, 0]],
        axis=1,
    )
    return (rows_upper, rows_lower)


def pull_one(populations, ghosts, direction, extent):
    (
        ghost_xlo,
        ghost_xhi,
        ghost_ylo,
        ghost_yhi,
        rows_ylo,
        rows_yhi,
        ghost_zlo,
        ghost_zhi,
        rows_zlo,
        rows_zhi,
    ) = ghosts
    step_x, step_y, step_z = VELOCITY[direction]
    block_count = populations.shape[0]
    shifted = populations[:, direction]
    if step_x == 1:
        shifted = jnp.concatenate(
            [ghost_xlo[:, PLUS_X.index(direction)][:, None], shifted[:, :-1]], axis=1
        )
    if step_x == -1:
        shifted = jnp.concatenate(
            [shifted[:, 1:], ghost_xhi[:, MINUS_X.index(direction)][:, None]], axis=1
        )
    if step_y != 0:
        if step_y == 1:
            face_plane = ghost_ylo[:, PLUS_Y.index(direction)]
            edge_rows = rows_ylo
        else:
            face_plane = ghost_yhi[:, MINUS_Y.index(direction)]
            edge_rows = rows_yhi
        face_plane = face_plane.reshape(block_count, extent, extent)
        if step_x == 1:
            face_plane = jnp.concatenate([edge_rows[:, 0][:, None], face_plane[:, :-1]], axis=1)
        if step_x == -1:
            face_plane = jnp.concatenate([face_plane[:, 1:], edge_rows[:, 1][:, None]], axis=1)
        if step_y == 1:
            shifted = jnp.concatenate([face_plane, shifted[:, :, :-extent]], axis=2)
        else:
            shifted = jnp.concatenate([shifted[:, :, extent:], face_plane], axis=2)
    if step_z != 0:
        if step_z == 1:
            face_plane = ghost_zlo[:, PLUS_Z.index(direction)]
            edge_rows = rows_zlo
        else:
            face_plane = ghost_zhi[:, MINUS_Z.index(direction)]
            edge_rows = rows_zhi
        face_plane = face_plane.reshape(block_count, extent, extent)
        if step_x == 1:
            face_plane = jnp.concatenate([edge_rows[:, 0][:, None], face_plane[:, :-1]], axis=1)
        if step_x == -1:
            face_plane = jnp.concatenate([face_plane[:, 1:], edge_rows[:, 1][:, None]], axis=1)
        if step_y == 1:
            face_plane = jnp.concatenate(
                [edge_rows[:, 2][:, :, None], face_plane[:, :, :-1]], axis=2
            )
        if step_y == -1:
            face_plane = jnp.concatenate(
                [face_plane[:, :, 1:], edge_rows[:, 3][:, :, None]], axis=2
            )
        spread = jnp.repeat(face_plane, extent, axis=2)
        depth_pos = lax.broadcasted_iota(jnp.int32, shifted.shape, 2) % extent
        if step_z == 1:
            shifted = jnp.where(depth_pos == 0, spread, jnp.roll(shifted, 1, axis=2))
        else:
            shifted = jnp.where(depth_pos == extent - 1, spread, jnp.roll(shifted, -1, axis=2))
    return shifted


def local_update(populations, solute, solid_fraction, ghosts, solute_ghosts):
    block_count, velocities, extent, cell_count = populations.shape
    pulled = [pull_one(populations, ghosts, direction, extent) for direction in range(19)]
    widened = [member.astype(jnp.float32) for member in pulled]
    density = jnp.zeros(solute.shape, jnp.float32)
    moment_x = jnp.zeros(solute.shape, jnp.float32)
    moment_y = jnp.zeros(solute.shape, jnp.float32)
    moment_z = jnp.zeros(solute.shape, jnp.float32)
    for direction in range(19):
        weighted = WEIGHTS[direction] * widened[direction]
        density = density + weighted
        step_x, step_y, step_z = VELOCITY[direction]
        if step_x != 0:
            moment_x = moment_x + step_x * weighted
        if step_y != 0:
            moment_y = moment_y + step_y * weighted
        if step_z != 0:
            moment_z = moment_z + step_z * weighted
    speed_x = moment_x / density
    speed_y = moment_y / density
    speed_z = moment_z / density
    speed_sq = speed_x * speed_x + speed_y * speed_y + speed_z * speed_z
    keep_share = 1.0 - solid_fraction
    collided = []
    for direction in range(19):
        step_x, step_y, step_z = VELOCITY[direction]
        along = step_x * speed_x + step_y * speed_y + step_z * speed_z
        equilibrium = density * (1.0 + 3.0 * along + 4.5 * along * along - 1.5 * speed_sq)
        current = widened[direction]
        relaxed = (
            keep_share * (current + (equilibrium - current) / relax_time)
            + solid_fraction * widened[OPPOSITE[direction]]
        )
        collided.append(relaxed.astype(jnp.bfloat16))
    new_populations = jnp.stack(collided, axis=1)
    solute_xlo, solute_xhi, solute_ylo, solute_yhi, solute_zlo, solute_zhi = solute_ghosts
    below_x = jnp.concatenate([solute_xlo[:, None], solute[:, :-1]], axis=1)
    above_x = jnp.concatenate([solute[:, 1:], solute_xhi[:, None]], axis=1)
    below_y = jnp.concatenate(
        [solute_ylo.reshape(block_count, extent, extent), solute[:, :, :-extent]], axis=2
    )
    above_y = jnp.concatenate(
        [solute[:, :, extent:], solute_yhi.reshape(block_count, extent, extent)], axis=2
    )
    depth_pos = lax.broadcasted_iota(jnp.int32, solute.shape, 2) % extent
    below_z = jnp.where(
        depth_pos == 0,
        jnp.repeat(solute_zlo.reshape(block_count, extent, extent), extent, axis=2),
        jnp.roll(solute, 1, axis=2),
    )
    above_z = jnp.where(
        depth_pos == extent - 1,
        jnp.repeat(solute_zhi.reshape(block_count, extent, extent), extent, axis=2),
        jnp.roll(solute, -1, axis=2),
    )
    laplace = below_x + above_x + below_y + above_y + below_z + above_z - 6.0 * solute
    advect = 0.5 * (
        speed_x * (above_x - below_x)
        + speed_y * (above_y - below_y)
        + speed_z * (above_z - below_z)
    )
    mixed = solute + diffusivity * laplace - advect
    reaction = rate_const * solid_fraction * (1.0 - solid_fraction) * (saturation - mixed)
    return (new_populations, mixed + reaction, solid_fraction - reaction)


def rank_within(peer_of, key_of):
    same_peer = peer_of[:, None] == peer_of[None, :]
    earlier = key_of[None, :] < key_of[:, None]
    return jnp.sum(jnp.where(same_peer & earlier, 1, 0), axis=1).astype(jnp.int32)


def route_plan(owner_blk, source_slot, axis_id, capacity, lanes, lane_index):
    lower_col = 2 * axis_id
    upper_col = 2 * axis_id + 1
    block_count = owner_blk.shape[0]
    slot_ids = jnp.arange(block_count, dtype=jnp.int32)
    out_peer = jnp.concatenate([owner_blk[:, upper_col], owner_blk[:, lower_col]])
    out_key = jnp.concatenate([2 * slot_ids, 2 * slot_ids + 1])
    in_peer = jnp.concatenate([owner_blk[:, lower_col], owner_blk[:, upper_col]])
    in_key = jnp.concatenate([2 * source_slot[:, lower_col], 2 * source_slot[:, upper_col] + 1])
    out_slot = (out_peer * lanes + lane_index) * capacity + rank_within(out_peer, out_key)
    in_slot = (in_peer * lanes + lane_index) * capacity + rank_within(in_peer, in_key)
    return (out_slot, in_slot)


def move_rows(selector, payload):
    flattened = payload.reshape(payload.shape[0], -1)
    if payload.dtype == jnp.bfloat16:
        moved_rows = jnp.dot(
            selector.astype(jnp.bfloat16), flattened, preferred_element_type=jnp.float32
        ).astype(jnp.bfloat16)
    else:
        moved_rows = jnp.dot(
            selector.astype(jnp.float32), flattened, precision=lax.Precision.HIGHEST
        )
    return moved_rows.reshape((selector.shape[0],) + payload.shape[1:])


def pack_faces(pieces, out_slot, slot_total):
    stacked = jnp.concatenate(pieces, axis=0)
    selector = jnp.arange(slot_total, dtype=jnp.int32)[:, None] == out_slot[None, :]
    return move_rows(selector, stacked)


def gather_slots(received, in_slot):
    selector = in_slot[:, None] == jnp.arange(received.shape[0], dtype=jnp.int32)[None, :]
    return move_rows(selector, received)


def body(populations, solute, solid_fraction, neighbours, front_list, redeal_list):
    block_count, velocities, extent, cell_count = populations.shape
    peers = lax.axis_size("blk")
    groups = lax.axis_size("grp")
    my_group = lax.axis_index("grp")
    offset_span = peers // 2 - 1
    capacity = (block_count + offset_span - 1) // offset_span
    owner_blk = neighbours // block_count // groups
    source_slot = neighbours % block_count
    face_sets = (PLUS_X, MINUS_X, PLUS_Y, MINUS_Y, PLUS_Z, MINUS_Z)
    slot_total = peers * capacity
    upper_x, lower_x, sol_upper_x, sol_lower_x = face_planes(
        populations, solute, face_sets[0], face_sets[1], 0
    )
    out_x, in_x = route_plan(owner_blk, source_slot, 0, capacity, 1, 0)
    got_pop, got_sol = (
        lax.all_to_all(
            pack_faces([upper_x, lower_x], out_x, slot_total),
            "blk",
            split_axis=0,
            concat_axis=0,
            tiled=True,
        ),
        lax.all_to_all(
            pack_faces([sol_upper_x, sol_lower_x], out_x, slot_total).astype(jnp.bfloat16),
            "blk",
            split_axis=0,
            concat_axis=0,
            tiled=True,
        ).astype(jnp.float32),
    )
    taken_pop = gather_slots(got_pop, in_x)
    taken_sol = gather_slots(got_sol, in_x)
    ghost_xlo = taken_pop[:block_count]
    ghost_xhi = taken_pop[block_count:]
    solute_xlo, solute_xhi = (taken_sol[:block_count], taken_sol[block_count:])

    def trade_with_rows(axis_id, rows_upper, rows_lower):
        upper_face, lower_face, sol_upper, sol_lower = face_planes(
            populations, solute, face_sets[2 * axis_id], face_sets[2 * axis_id + 1], axis_id
        )
        out_slot, in_slot = route_plan(owner_blk, source_slot, axis_id, capacity, 1, 0)
        got_faces, got_solute, got_rows = (
            lax.all_to_all(
                pack_faces([upper_face, lower_face], out_slot, slot_total),
                "blk",
                split_axis=0,
                concat_axis=0,
                tiled=True,
            ),
            lax.all_to_all(
                pack_faces([sol_upper, sol_lower], out_slot, slot_total).astype(jnp.bfloat16),
                "blk",
                split_axis=0,
                concat_axis=0,
                tiled=True,
            ).astype(jnp.float32),
            lax.all_to_all(
                pack_faces([rows_upper, rows_lower], out_slot, slot_total),
                "blk",
                split_axis=0,
                concat_axis=0,
                tiled=True,
            ),
        )
        faces_in = gather_slots(got_faces, in_slot)
        solute_in = gather_slots(got_solute, in_slot)
        rows_in = gather_slots(got_rows, in_slot)
        return (
            faces_in[:block_count],
            faces_in[block_count:],
            rows_in[:block_count],
            rows_in[block_count:],
            solute_in[:block_count],
            solute_in[block_count:],
        )

    rows_upper_y, rows_lower_y = edges_y(ghost_xlo, ghost_xhi, extent)
    ghost_ylo, ghost_yhi, rows_ylo, rows_yhi, solute_ylo, solute_yhi = trade_with_rows(
        1, rows_upper_y, rows_lower_y
    )
    rows_upper_z, rows_lower_z = edges_z(ghost_xlo, ghost_xhi, ghost_ylo, ghost_yhi, extent)
    ghost_zlo, ghost_zhi, rows_zlo, rows_zhi, solute_zlo, solute_zhi = trade_with_rows(
        2, rows_upper_z, rows_lower_z
    )
    ghosts = (
        ghost_xlo,
        ghost_xhi,
        ghost_ylo,
        ghost_yhi,
        rows_ylo,
        rows_yhi,
        ghost_zlo,
        ghost_zhi,
        rows_zlo,
        rows_zhi,
    )
    solute_ghosts = (solute_xlo, solute_xhi, solute_ylo, solute_yhi, solute_zlo, solute_zhi)
    collided, reacted, dissolved = local_update(
        populations, solute, solid_fraction, ghosts, solute_ghosts
    )
    moves_here = front_list.shape[0]
    front_slot = front_list % block_count
    dest_group = redeal_list // block_count % groups
    dest_slot = redeal_list % block_count
    group_ids = jnp.arange(groups, dtype=jnp.int32)
    match_out = dest_group[None, :] == group_ids[:, None]
    has_out = jnp.any(match_out, axis=1)
    entry_pick = jnp.sum(
        jnp.where(match_out, jnp.arange(moves_here, dtype=jnp.int32)[None, :], 0), axis=1
    )
    chosen_slot = jnp.take(front_slot, entry_pick)
    send_solute = jnp.where(has_out[:, None, None], jnp.take(reacted, chosen_slot, axis=0), 0.0)
    send_solid = jnp.where(has_out[:, None, None], jnp.take(dissolved, chosen_slot, axis=0), 0.0)
    send_place = jnp.where(has_out, jnp.take(dest_slot, entry_pick), 0)[:, None]
    got_solute, got_solid, got_place = (
        lax.all_to_all(send_solute, "grp", split_axis=0, concat_axis=0, tiled=True),
        lax.all_to_all(send_solid, "grp", split_axis=0, concat_axis=0, tiled=True),
        lax.all_to_all(send_place, "grp", split_axis=0, concat_axis=0, tiled=True),
    )
    incoming = group_ids != my_group
    hit_match = (
        got_place[:, 0][None, :] == jnp.arange(block_count, dtype=jnp.int32)[:, None]
    ) & incoming[None, :]
    landed = jnp.any(hit_match, axis=1)
    from_group = jnp.sum(jnp.where(hit_match, group_ids[None, :], 0), axis=1)
    new_solute = jnp.where(landed[:, None, None], jnp.take(got_solute, from_group, axis=0), reacted)
    new_solid = jnp.where(landed[:, None, None], jnp.take(got_solid, from_group, axis=0), dissolved)
    new_populations = jnp.where(landed[:, None, None, None], jnp.ones_like(collided), collided)
    return (new_populations, new_solute, new_solid)


def solution(mesh):
    return jax.shard_map(
        body,
        mesh=mesh,
        in_specs=(
            P(("blk", "grp"), None, None, None),
            P(("blk", "grp"), None, None),
            P(("blk", "grp"), None, None),
            P(("blk", "grp"), None),
            P(("blk", "grp")),
            P(("blk", "grp")),
        ),
        out_specs=(
            P(("blk", "grp"), None, None, None),
            P(("blk", "grp"), None, None),
            P(("blk", "grp"), None, None),
        ),
        check_vma=False,
    )
```

profile of v0, /device:TPU:1, one launch (start us, length us, event | category | flops | bytes accessed | tf_op | source)
XLA Modules:
  0.0 490.6 jit_solution(4094803039097432288)
XLA Ops:
  2.9 5.9 %all-to-all-start = ((s32[4,1,1]{2,1,0:T(1,128)}), s32[4,1,1]{2,1,0:T(1,128)S(1)}, u32[]{:S(2)}, u32[]{:S(2)}) async-start(s32[4,1,1]{2,1,0:T(1,128)} %copy.289), calls=%async_computation | async-start | bytes 4096 | tf_op jit(solution)/shard_map/all_to_all | solution.py:395
  8.7 46.3 %reshape.336 = bf16[8,19,32,32,32]{4,3,2,1,0:T(8,128)(2,1)} reshape(bf16[8,19,32,1024]{3,2,1,0:T(8,128)(2,1)} %param.12) | data formatting | bytes 19922944 | tf_op jit(solution)/shard_map/reshape | solution.py:43
  55.1 3.6 slice_bitcast_fusion.1
  58.7 10.0 %fusion.287 = (bf16[8,19,32,1,32]{4,3,2,1,0:T(2,128)(2,1)S(1)}, bf16[8,19,32,1,32]{4,3,2,1,0:T(2,128)(2,1)S(1)}) fusion(bf16[8,19,32,32,32]{4,3,2,1,0:T(8,128)(2,1)} %reshape.336), kind=kLoop, calls=%fused_computation.600 | loop fusion | bytes 1245184 | tf_op jit(solution)/shard_map/slice | solution.py:50
  71.7 56.3 %slice_reduce_fusion.1 = (bf16[8,19,32,32]{3,2,1,0:T(8,128)(2,1)S(1)}, bf16[8,19,32,32]{3,2,1,0:T(8,128)(2,1)S(1)}) fusion(bf16[8,19,32,32,32]{4,3,2,1,0:T(8,128)(2,1)} %reshape.336), kind=kLoop, calls=%fused_computation.7 | loop fusion | bytes 1245184 | tf_op jit(solution)/shard_map/slice | solution.py:53
  130.7 6.8 %slice_bitcast_fusion.2 = (bf16[8,32,1024]{2,1,0:T(8,128)(2,1)}, bf16[8,32,1024]{2,1,0:T(8,128)(2,1)}, bf16[8,32,1024]{2,1,0:T(8,128)(2,1)S(1)}, bf16[8,32,1024]...) fusion(bf16[8,19,32,1024]{3,2,1,0:T(8,128)(2,1)} %param.12), kind=kLoop, calls=%fused_computation.402 | loop fusion | bytes 18874368 | tf_op jit(solution)/shard_map/squeeze | solution.py:113
  137.5 2.9 reshape.363
  140.4 6.8 %slice_reduce_fusion.3 = (f32[8,32,32]{2,1,0:T(8,128)S(1)}, f32[8,32,32]{2,1,0:T(8,128)S(1)}) fusion(f32[8,32,32,32]{3,2,1,0:T(8,128)} %reshape.363), kind=kLoop, calls=%fused_computation.16 | loop fusion | bytes 131072 | tf_op jit(solution)/shard_map/slice | solution.py:54
  147.3 3.0 slice_reduce_fusion.5
  210.6 8.0 %all-to-all-start.8 = ((bf16[32,2,512]{2,1,0:T(2,128)(2,1)}), bf16[32,2,512]{2,1,0:T(2,128)(2,1)S(1)}, u32[]{:S(2)}, u32[]{:S(2)}) async-start(bf16[32,2,512]{2,1,0:T(2,128)(2,1)} %reshape.466), calls=%async_computation.8 | async-start | bytes 131072 | tf_op jit(solution)/shard_map/all_to_all | solution.py:327
  220.6 5.4 %all-to-all-done.8 = bf16[32,2,512]{2,1,0:T(2,128)(2,1)S(1)} async-done(((bf16[32,2,512]{2,1,0:T(2,128)(2,1)}), bf16[32,2,512]{2,1,0:T(2,128)(2,1)S(1)}, u32[]{:S(2)}, u32[]{:S(2)}) %all-to-all-start.8) | async-done | bytes 65568 | tf_op jit(solution)/shard_map/all_to_all | solution.py:327
  226.0 3.9 all-to-all-start.7
  230.2 7.2 %all-to-all-done.7 = bf16[32,2,512]{2,1,0:T(2,128)(2,1)S(1)} async-done(((bf16[32,2,512]{2,1,0:T(2,128)(2,1)}), bf16[32,2,512]{2,1,0:T(2,128)(2,1)S(1)}, u32[]{:S(2)}, u32[]{:S(2)}) %all-to-all-start.7) | async-done | bytes 65568 | tf_op jit(solution)/shard_map/all_to_all | solution.py:327
  237.4 3.9 all-to-all-start.6
  241.6 7.2 %all-to-all-done.6 = bf16[32,2,512]{2,1,0:T(2,128)(2,1)S(1)} async-done(((bf16[32,2,512]{2,1,0:T(2,128)(2,1)}), bf16[32,2,512]{2,1,0:T(2,128)(2,1)S(1)}, u32[]{:S(2)}, u32[]{:S(2)}) %all-to-all-start.6) | async-done | bytes 65568 | tf_op jit(solution)/shard_map/all_to_all | solution.py:300
  248.8 3.9 all-to-all-start.1
  253.1 2.6 broadcast_in_dim.236
  255.7 4.6 reshape.367
  260.4 2.6 broadcast_in_dim.237
  263.0 4.6 reshape.369
  270.4 7.5 %all-to-all-start.2 = ((bf16[32,5,1024]{2,1,0:T(8,128)(2,1)}), bf16[32,5,1024]{2,1,0:T(8,128)(2,1)S(1)}, u32[]{:S(2)}, u32[]{:S(2)}) async-start(bf16[32,5,1024]{2,1,0:T(8,128)(2,1)} %reshape.339), calls=%async_computation.2 | async-start | bytes 1048576 | tf_op jit(solution)/shard_map/all_to_all | solution.py:320
  279.5 10.0 %all-to-all-done.2 = bf16[32,5,1024]{2,1,0:T(8,128)(2,1)S(1)} async-done(((bf16[32,5,1024]{2,1,0:T(8,128)(2,1)}), bf16[32,5,1024]{2,1,0:T(8,128)(2,1)S(1)}, u32[]{:S(2)}, u32[]{:S(2)}) %all-to-all-start.2) | async-done | bytes 327712 | tf_op jit(solution)/shard_map/all_to_all | solution.py:320
  289.5 3.7 all-to-all-start.3
  295.1 9.7 %all-to-all-done.3 = bf16[32,5,1024]{2,1,0:T(8,128)(2,1)S(1)} async-done(((bf16[32,5,1024]{2,1,0:T(8,128)(2,1)}), bf16[32,5,1024]{2,1,0:T(8,128)(2,1)S(1)}, u32[]{:S(2)}, u32[]{:S(2)}) %all-to-all-start.3) | async-done | bytes 327712 | tf_op jit(solution)/shard_map/all_to_all | solution.py:320
  306.2 3.6 all-to-all-start.4
  326.4 2.9 reshape.343
  330.7 2.9 reshape.344
  333.6 7.7 %all-to-all-start.5 = ((bf16[32,4,32]{2,1,0:T(4,128)(2,1)}), bf16[32,4,32]{2,1,0:T(4,128)(2,1)S(1)}, u32[]{:S(2)}, u32[]{:S(2)}) async-start(bf16[32,4,32]{2,1,0:T(4,128)(2,1)} %reshape.353), calls=%async_computation.5 | async-start | bytes 65536 | tf_op jit(solution)/shard_map/all_to_all | solution.py:334
  341.7 6.7 %all-to-all-done.5 = bf16[32,4,32]{2,1,0:T(4,128)(2,1)S(1)} async-done(((bf16[32,4,32]{2,1,0:T(4,128)(2,1)}), bf16[32,4,32]{2,1,0:T(4,128)(2,1)S(1)}, u32[]{:S(2)}, u32[]{:S(2)}) %all-to-all-start.5) | async-done | bytes 8224 | tf_op jit(solution)/shard_map/all_to_all | solution.py:334
  350.9 2.9 reshape.362
  356.1 2.9 reshape.361
  360.5 2.9 reshape.359
  364.7 2.9 reshape.358
  369.0 2.9 reshape.357
  374.1 2.9 reshape.355
  379.1 3.1 reshape.356
  385.3 2.9 reshape.360
  388.2 19.1 %fusion.196 = (f32[8,32,1024]{2,1,0:T(8,128)}, f32[8,32,1024]{2,1,0:T(8,128)S(1)}, f32[8,32,1024]{2,1,0:T(8,128)S(1)}, f32[8,32,1024]{2,1,0:T(8,128)S(1)}, f32[8...) fusion(f32[8,32,1024]{2,1,0:T(8,128)S(1)} %copy-done, ...), kind=kLoop, calls=%fused_computation.347 | loop fusion | flops 63963136 | bytes 38348800 | tf_op jit(solution)/shard_map/sub | solution.py:230
  408.5 2.7 gather_fusion.2
  411.3 2.7 gather_fusion.4
  416.4 4.9 all-to-all-start.10
  421.4 3.5 bitcast_dynamic-update-slice_fusion.18
  424.9 3.6 bitcast_dynamic-update-slice_fusion.17
  459.4 4.2 all-to-all-start.9
  463.7 8.7 %broadcast_select_fusion = bf16[8,19,32,1024]{3,2,0,1:T(8,128)(2,1)} fusion(bf16[8,19,32,1024]{3,2,0,1:T(8,128)(2,1)} %bitcast_dynamic-update-slice_fusion, pred[8]{0:T(512)(128)(4,1)S(1)} %copy-done.48), kind=kLoop, calls=%fused_computation.8 | loop fusion | flops 4980736 | bytes 19922952 | tf_op jit(solution)/shard_map/jit(_where)/select_n | solution.py:405
  472.4 10.2 %copy.348 = bf16[8,19,32,1024]{3,2,1,0:T(8,128)(2,1)} copy(bf16[8,19,32,1024]{3,2,0,1:T(8,128)(2,1)} %broadcast_select_fusion) | data formatting | bytes 19922944
  482.5 2.8 gather_fusion.5
  487.0 3.4 select_select_fusion
  (379 shorter events, 148.9 us)
Async XLA Ops:
  1.4 53.6 %copy-start.45 = (s32[4]{0:T(128)}, s32[4]{0:T(128)S(1)}, u32[]{:S(2)}) copy-start(s32[4]{0:T(128)S(1)} %select_reduce_fusion.7) | copy-start | bytes 52
  1.5 53.5 %copy-start.47 = (pred[4]{0:T(512)(128)(4,1)}, pred[4]{0:T(512)(128)(4,1)S(1)}, u32[]{:S(2)}) copy-start(pred[4]{0:T(512)(128)(4,1)S(1)} %fusion.261) | copy-start | bytes 16
  2.9 207.7 %all-to-all-start = ((s32[4,1,1]{2,1,0:T(1,128)}), s32[4,1,1]{2,1,0:T(1,128)S(1)}, u32[]{:S(2)}, u32[]{:S(2)}) async-start(s32[4,1,1]{2,1,0:T(1,128)} %copy.289), calls=%async_computation | async-start | bytes 4096 | tf_op jit(solution)/shard_map/all_to_all | solution.py:395
  128.7 8.8 %copy-start.3 = (f32[8,32,1024]{2,1,0:T(8,128)S(1)}, f32[8,32,1024]{2,1,0:T(8,128)}, u32[]{:S(2)}) copy-start(f32[8,32,1024]{2,1,0:T(8,128)} %param.13) | copy-start | bytes 3145732
  137.5 66.5 %copy-start.27 = (bf16[8,32,1024]{2,1,0:T(8,128)(2,1)}, bf16[8,32,1024]{2,1,0:T(8,128)(2,1)S(1)}, u32[]{:S(2)}) copy-start(bf16[8,32,1024]{2,1,0:T(8,128)(2,1)S(1)} %get-tuple-element.82) | copy-start | bytes 1572868
  137.5 67.2 %copy-start.26 = (bf16[8,32,1024]{2,1,0:T(8,128)(2,1)}, bf16[8,32,1024]{2,1,0:T(8,128)(2,1)S(1)}, u32[]{:S(2)}) copy-start(bf16[8,32,1024]{2,1,0:T(8,128)(2,1)S(1)} %get-tuple-element.72) | copy-start | bytes 1572868
  137.5 173.7 %copy-start.14 = (bf16[8,32,1024]{2,1,0:T(8,128)(2,1)}, bf16[8,32,1024]{2,1,0:T(8,128)(2,1)S(1)}, u32[]{:S(2)}) copy-start(bf16[8,32,1024]{2,1,0:T(8,128)(2,1)S(1)} %get-tuple-element.74) | copy-start | bytes 1572868
  140.4 11.5 %copy-start.28 = (bf16[8,32,1024]{2,1,0:T(8,128)(2,1)S(1)}, bf16[8,32,1024]{2,1,0:T(8,128)(2,1)}, u32[]{:S(2)}) copy-start(bf16[8,32,1024]{2,1,0:T(8,128)(2,1)} %get-tuple-element.81) | copy-start | bytes 1572868
  147.3 14.8 %copy-start.40 = (s32[8,6]{1,0:T(8,128)S(1)}, s32[8,6]{1,0:T(8,128)}, u32[]{:S(2)}) copy-start(s32[8,6]{1,0:T(8,128)} %param.15) | copy-start | bytes 580
  155.4 25.8 %copy-start.31 = (bf16[8,2,32,32]{3,2,1,0:T(8,128)(2,1)S(1)}, bf16[8,2,32,32]{3,2,1,0:T(8,128)(2,1)}, u32[]{:S(2)}) copy-start(bf16[8,2,32,32]{3,2,1,0:T(8,128)(2,1)} %slice.914) | copy-start | bytes 98308
  160.3 47.6 %copy-start.29 = (bf16[8,32,1024]{2,1,0:T(8,128)(2,1)S(1)}, bf16[8,32,1024]{2,1,0:T(8,128)(2,1)}, u32[]{:S(2)}) copy-start(bf16[8,32,1024]{2,1,0:T(8,128)(2,1)} %get-tuple-element.73) | copy-start | bytes 1572868
  165.6 43.2 %copy-start.50 = (s32[3]{0:T(128)S(1)}, s32[3]{0:T(128)}, u32[]{:S(2)}) copy-start(s32[3]{0:T(128)} %param.16) | copy-start | bytes 40
  169.1 40.4 %copy-start.46 = (s32[4]{0:T(128)S(1)}, s32[4]{0:T(128)}, u32[]{:S(2)}) copy-start(s32[4]{0:T(128)} %copy-done.45) | copy-start | bytes 52
  180.9 112.5 %copy-start.43 = (s32[16]{0:T(128)}, s32[16]{0:T(128)S(1)}, u32[]{:S(2)}) copy-start(s32[16]{0:T(128)S(1)} %add.648) | copy-start | bytes 196
  181.1 60.2 %copy-start.41 = (s32[16]{0:T(128)}, s32[16]{0:T(128)S(1)}, u32[]{:S(2)}) copy-start(s32[16]{0:T(128)S(1)} %add.655) | copy-start | bytes 196
  186.5 123.6 %copy-start.15 = (bf16[8,31,1024]{2,1,0:T(8,128)(2,1)}, bf16[8,31,1024]{2,1,0:T(8,128)(2,1)S(1)}, u32[]{:S(2)}) copy-start(bf16[8,31,1024]{2,1,0:T(8,128)(2,1)S(1)} %slice.972) | copy-start | bytes 1523716
  210.6 15.4 %all-to-all-start.8 = ((bf16[32,2,512]{2,1,0:T(2,128)(2,1)}), bf16[32,2,512]{2,1,0:T(2,128)(2,1)S(1)}, u32[]{:S(2)}, u32[]{:S(2)}) async-start(bf16[32,2,512]{2,1,0:T(2,128)(2,1)} %reshape.466), calls=%async_computation.8 | async-start | bytes 131072 | tf_op jit(solution)/shard_map/all_to_all | solution.py:327
  226.0 11.4 %all-to-all-start.7 = ((bf16[32,2,512]{2,1,0:T(2,128)(2,1)}), bf16[32,2,512]{2,1,0:T(2,128)(2,1)S(1)}, u32[]{:S(2)}, u32[]{:S(2)}) async-start(bf16[32,2,512]{2,1,0:T(2,128)(2,1)} %reshape.468), calls=%async_computation.7 | async-start | bytes 131072 | tf_op jit(solution)/shard_map/all_to_all | solution.py:327
  237.4 11.4 %all-to-all-start.6 = ((bf16[32,2,512]{2,1,0:T(2,128)(2,1)}), bf16[32,2,512]{2,1,0:T(2,128)(2,1)S(1)}, u32[]{:S(2)}, u32[]{:S(2)}) async-start(bf16[32,2,512]{2,1,0:T(2,128)(2,1)} %reshape.470), calls=%async_computation.6 | async-start | bytes 131072 | tf_op jit(solution)/shard_map/all_to_all | solution.py:300
  248.8 21.6 %all-to-all-start.1 = ((bf16[32,5,1024]{2,1,0:T(8,128)(2,1)}), bf16[32,5,1024]{2,1,0:T(8,128)(2,1)S(1)}, u32[]{:S(2)}, u32[]{:S(2)}) async-start(bf16[32,5,1024]{2,1,0:T(8,128)(2,1)} %reshape.337), calls=%async_computation.1 | async-start | bytes 1048576 | tf_op jit(solution)/shard_map/all_to_all | solution.py:293
  260.4 44.6 %copy-start.42 = (s32[16]{0:T(128)S(1)}, s32[16]{0:T(128)}, u32[]{:S(2)}) copy-start(s32[16]{0:T(128)} %copy-done.41) | copy-start | bytes 196
  270.4 19.1 %all-to-all-start.2 = ((bf16[32,5,1024]{2,1,0:T(8,128)(2,1)}), bf16[32,5,1024]{2,1,0:T(8,128)(2,1)S(1)}, u32[]{:S(2)}, u32[]{:S(2)}) async-start(bf16[32,5,1024]{2,1,0:T(8,128)(2,1)} %reshape.339), calls=%async_computation.2 | async-start | bytes 1048576 | tf_op jit(solution)/shard_map/all_to_all | solution.py:320
  289.5 15.3 %all-to-all-start.3 = ((bf16[32,5,1024]{2,1,0:T(8,128)(2,1)}), bf16[32,5,1024]{2,1,0:T(8,128)(2,1)S(1)}, u32[]{:S(2)}, u32[]{:S(2)}) async-start(bf16[32,5,1024]{2,1,0:T(8,128)(2,1)} %reshape.341), calls=%async_computation.3 | async-start | bytes 1048576 | tf_op jit(solution)/shard_map/all_to_all | solution.py:320
  293.6 47.7 %copy-start.44 = (s32[16]{0:T(128)S(1)}, s32[16]{0:T(128)}, u32[]{:S(2)}) copy-start(s32[16]{0:T(128)} %copy-done.43) | copy-start | bytes 196
  306.2 27.3 %all-to-all-start.4 = ((bf16[32,2,32]{2,1,0:T(2,128)(2,1)}), bf16[32,2,32]{2,1,0:T(2,128)(2,1)S(1)}, u32[]{:S(2)}, u32[]{:S(2)}) async-start(bf16[32,2,32]{2,1,0:T(2,128)(2,1)} %reshape.348), calls=%async_computation.4 | async-start | bytes 32768 | tf_op jit(solution)/shard_map/all_to_all | solution.py:334
  309.9 15.0 %copy-start.38 = (bf16[8,1,1024]{2,1,0:T(2,128)(2,1)}, bf16[8,1,1024]{2,1,0:T(2,128)(2,1)S(1)}, u32[]{:S(2)}) copy-start(bf16[8,1,1024]{2,1,0:T(2,128)(2,1)S(1)} %copy.388) | copy-start | bytes 49156
  310.0 15.0 %copy-start.39 = (bf16[8,1,1024]{2,1,0:T(2,128)(2,1)}, bf16[8,1,1024]{2,1,0:T(2,128)(2,1)S(1)}, u32[]{:S(2)}) copy-start(bf16[8,1,1024]{2,1,0:T(2,128)(2,1)S(1)} %copy.389) | copy-start | bytes 49156
  333.6 14.8 %all-to-all-start.5 = ((bf16[32,4,32]{2,1,0:T(4,128)(2,1)}), bf16[32,4,32]{2,1,0:T(4,128)(2,1)S(1)}, u32[]{:S(2)}, u32[]{:S(2)}) async-start(bf16[32,4,32]{2,1,0:T(4,128)(2,1)} %reshape.353), calls=%async_computation.5 | async-start | bytes 65536 | tf_op jit(solution)/shard_map/all_to_all | solution.py:334
  367.7 20.5 %copy-start = (f32[8,32,1024]{2,1,0:T(8,128)S(1)}, f32[8,32,1024]{2,1,0:T(8,128)}, u32[]{:S(2)}) copy-start(f32[8,32,1024]{2,1,0:T(8,128)} %param.14) | copy-start | bytes 3145732
  416.4 43.0 %all-to-all-start.10 = ((f32[4,32,1024]{2,1,0:T(8,128)}), f32[4,32,1024]{2,1,0:T(8,128)}, u32[]{:S(2)}, u32[]{:S(2)}) async-start(f32[4,32,1024]{2,1,0:T(8,128)} %get-tuple-element.179), calls=%async_computation.10 | async-start | bytes 1048576 | tf_op jit(solution)/shard_map/all_to_all | solution.py:394
  421.3 7.2 %copy-start.1 = (f32[8,32,1024]{2,1,0:T(8,128)S(1)}, f32[8,32,1024]{2,1,0:T(8,128)}, u32[]{:S(2)}) copy-start(f32[8,32,1024]{2,1,0:T(8,128)} %get-tuple-element.49) | copy-start | bytes 3145732
  421.3 7.2 %copy-start.2 = (f32[8,32,1024]{2,1,0:T(8,128)S(1)}, f32[8,32,1024]{2,1,0:T(8,128)}, u32[]{:S(2)}) copy-start(f32[8,32,1024]{2,1,0:T(8,128)} %get-tuple-element.50) | copy-start | bytes 3145732
  421.3 7.2 %copy-start.9 = (bf16[8,32,1024]{2,1,0:T(8,128)(2,1)S(1)}, bf16[8,32,1024]{2,1,0:T(8,128)(2,1)}, u32[]{:S(2)}) copy-start(bf16[8,32,1024]{2,1,0:T(8,128)(2,1)} %get-tuple-element.86) | copy-start | bytes 1572868
  421.4 7.2 %copy-start.11 = (bf16[8,31,1024]{2,1,0:T(8,128)(2,1)S(1)}, bf16[8,31,1024]{2,1,0:T(8,128)(2,1)}, u32[]{:S(2)}) copy-start(bf16[8,31,1024]{2,1,0:T(8,128)(2,1)} %slice.891) | copy-start | bytes 1523716
  421.4 7.2 %copy-start.36 = (bf16[8,1,1024]{2,1,0:T(2,128)(2,1)S(1)}, bf16[8,1,1024]{2,1,0:T(2,128)(2,1)}, u32[]{:S(2)}) copy-start(bf16[8,1,1024]{2,1,0:T(2,128)(2,1)} %copy.357) | copy-start | bytes 49156
  421.4 7.2 %copy-start.37 = (bf16[8,1,1024]{2,1,0:T(2,128)(2,1)S(1)}, bf16[8,1,1024]{2,1,0:T(2,128)(2,1)}, u32[]{:S(2)}) copy-start(bf16[8,1,1024]{2,1,0:T(2,128)(2,1)} %copy.360) | copy-start | bytes 49156
  421.4 8.9 %copy-start.8 = (bf16[8,32,1024]{2,1,0:T(8,128)(2,1)S(1)}, bf16[8,32,1024]{2,1,0:T(8,128)(2,1)}, u32[]{:S(2)}) copy-start(bf16[8,32,1024]{2,1,0:T(8,128)(2,1)} %get-tuple-element.84) | copy-start | bytes 1572868
  421.4 8.9 %copy-start.10 = (bf16[8,32,992]{2,1,0:T(8,128)(2,1)S(1)}, bf16[8,32,992]{2,1,0:T(8,128)(2,1)}, u32[]{:S(2)}) copy-start(bf16[8,32,992]{2,1,0:T(8,128)(2,1)} %slice.908) | copy-start | bytes 1523716
  432.1 5.1 %copy-start.7 = (bf16[8,31,1024]{2,1,0:T(8,128)(2,1)S(1)}, bf16[8,31,1024]{2,1,0:T(8,128)(2,1)}, u32[]{:S(2)}) copy-start(bf16[8,31,1024]{2,1,0:T(8,128)(2,1)} %slice.938) | copy-start | bytes 1523716
  432.1 5.1 %copy-start.34 = (bf16[8,1,1024]{2,1,0:T(2,128)(2,1)S(1)}, bf16[8,1,1024]{2,1,0:T(2,128)(2,1)}, u32[]{:S(2)}) copy-start(bf16[8,1,1024]{2,1,0:T(2,128)(2,1)} %copy.369) | copy-start | bytes 49156
  432.1 5.1 %copy-start.35 = (bf16[8,1,1024]{2,1,0:T(2,128)(2,1)S(1)}, bf16[8,1,1024]{2,1,0:T(2,128)(2,1)}, u32[]{:S(2)}) copy-start(bf16[8,1,1024]{2,1,0:T(2,128)(2,1)} %copy.372) | copy-start | bytes 49156
  443.9 5.6 %copy-start.20 = (bf16[8,32,1024]{2,1,0:T(8,128)(2,1)S(1)}, bf16[8,32,1024]{2,1,0:T(8,128)(2,1)}, u32[]{:S(2)}) copy-start(bf16[8,32,1024]{2,1,0:T(8,128)(2,1)} %get-tuple-element.56) | copy-start | bytes 1572868
  443.9 5.6 %copy-start.21 = (bf16[8,32,1024]{2,1,0:T(8,128)(2,1)S(1)}, bf16[8,32,1024]{2,1,0:T(8,128)(2,1)}, u32[]{:S(2)}) copy-start(bf16[8,32,1024]{2,1,0:T(8,128)(2,1)} %get-tuple-element.57) | copy-start | bytes 1572868
  456.1 7.5 %copy-start.48 = (pred[8]{0:T(512)(128)(4,1)S(1)}, pred[8]{0:T(512)(128)(4,1)}, u32[]{:S(2)}) copy-start(pred[8]{0:T(512)(128)(4,1)} %fusion.263) | copy-start | bytes 28
  459.4 25.9 %all-to-all-start.9 = ((f32[4,32,1024]{2,1,0:T(8,128)}), f32[4,32,1024]{2,1,0:T(8,128)S(1)}, u32[]{:S(2)}, u32[]{:S(2)}) async-start(f32[4,32,1024]{2,1,0:T(8,128)} %get-tuple-element.180), calls=%async_computation.9 | async-start | bytes 1048576 | tf_op jit(solution)/shard_map/all_to_all | solution.py:393
  472.4 14.6 %copy-start.12 = (f32[8,32,1024]{2,1,0:T(8,128)S(1)}, f32[8,32,1024]{2,1,0:T(8,128)}, u32[]{:S(2)}) copy-start(f32[8,32,1024]{2,1,0:T(8,128)} %get-tuple-element.45) | copy-start | bytes 3145732
  472.4 14.6 %copy-start.13 = (f32[8,32,1024]{2,1,0:T(8,128)S(1)}, f32[8,32,1024]{2,1,0:T(8,128)}, u32[]{:S(2)}) copy-start(f32[8,32,1024]{2,1,0:T(8,128)} %fusion.197) | copy-start | bytes 3145732
  472.4 14.6 %copy-start.49 = (pred[8]{0:T(512)(128)(4,1)S(1)}, pred[8]{0:T(512)(128)(4,1)}, u32[]{:S(2)}) copy-start(pred[8]{0:T(512)(128)(4,1)} %compare_and_fusion.3) | copy-start | bytes 28
  (14 other events, 62.0 us)
where the time goes:
time: 500 us; the launch traced here: 491 us
  local copies, waits for them, and re-layouts  292 us (58%)
  other arithmetic  90.2 us (18%)
  starting transfers between devices  57.2 us (11%)
  waiting for transfers between devices  46.1 us (9%)
    slice x1, local copies, waits for them, and re-layouts, face_planes(): upper_face, lower_face = (cube_view[..., top_index], cube_view[..., 0])  56.3 us
    reshape x1, local copies, waits for them, and re-layouts, face_planes(): populations.reshape(block_count, velocities, extent, extent, extent)  46.3 us
    unnamed x18, other arithmetic  36.2 us
    unnamed x151, local copies, waits for them, and re-layouts  31.8 us
    reshape x10, local copies, waits for them, and re-layouts, pull_one(): spread = jnp.repeat(face_plane, extent, axis=2)  29.6 us
    all_to_all x2, waiting for transfers between devices, trade_with_rows(): lax.all_to_all(pack_faces([upper_face, lower_face], out_slot, slot_total)...  19.6 us
    sub x1, other arithmetic, local_update(): return (new_populations, mixed + reaction, solid_fraction - reaction)  19.1 us
    all_to_all x2, waiting for transfers between devices, trade_with_rows(): lax.all_to_all(pack_faces([sol_upper, sol_lower], out_slot, slot_total).a...  12.6 us
  transfers between devices with their start and end apart: 11, of which 6 were waited for; matrix products, arithmetic and copies ran while one was open for 63% of the time, Pallas kernels for 0%

commit v1 on v0

v1 whole, which is shorter than its diff:
```python
import jax
import jax.numpy as jnp
from jax import lax
from jax.experimental import pallas as pl
from jax.experimental.pallas import tpu as pltpu
from jax.sharding import PartitionSpec as P

VELOCITY = (
    (0, 0, 0), (1, 0, 0), (-1, 0, 0), (0, 1, 0), (0, -1, 0), (0, 0, 1), (0, 0, -1),
    (1, 1, 0), (-1, -1, 0), (1, -1, 0), (-1, 1, 0), (1, 0, 1), (-1, 0, -1), (1, 0, -1),
    (-1, 0, 1), (0, 1, 1), (0, -1, -1), (0, 1, -1), (0, -1, 1),
)
LEAVES = (
    ((2, 8, 10, 12, 14), (1, 7, 9, 11, 13)),
    ((4, 8, 9, 16, 18), (3, 7, 10, 15, 17)),
    ((6, 12, 13, 16, 17), (5, 11, 14, 15, 18)),
)
FETCH = (6, 12, 13, 16, 17, 5, 11, 14, 15, 18, 4, 8, 9, 3, 7, 10, 2, 1)
SLOTS = 8
S = 32
CELLS = S * S
PEERS = 32
GROUPS = 4
F32, BF16, I32 = jnp.float32, jnp.bfloat16, jnp.int32
relax_time = 0.8
diffusivity = 0.1
rate_const = 0.5
saturation = 1.0


def iota(shape, dim):
    return lax.broadcasted_iota(I32, shape, dim)


def dot(a, b):
    return jnp.dot(a, b, preferred_element_type=F32)


def exchange_kernel(pop_hbm, sol_ref, nbr, inv, redeal, gx_ref, gy_ref, gz_ref, table_ref,
                    pop, fx, fy, fz, sa, sb, se, ra, rb, re, ex, mine, fetch_sem, send_sem, recv_sem,
                    table_send, table_recv):
    me = lax.axis_index("blk")
    grp = lax.axis_index("grp")

    def fetch(direction):
        return pltpu.make_async_copy(pop_hbm.at[:, direction], pop.at[direction], fetch_sem.at[direction])

    for direction in FETCH:
        fetch(direction).start()

    barrier = pltpu.get_barrier_semaphore()

    @pl.loop(1, PEERS)
    def _(k):
        pl.semaphore_signal(barrier, inc=1, device_id={"blk": (me + k) % PEERS}, device_id_type=pl.DeviceIdType.MESH)

    for k in range(1, GROUPS):
        pl.semaphore_signal(barrier, inc=1, device_id={"grp": (grp + k) % GROUPS}, device_id_type=pl.DeviceIdType.MESH)

    lane_of = iota((8, 128), 1)
    mine[...] = jnp.where(lane_of == 0, redeal[0], jnp.where(lane_of == 1, redeal[1], redeal[2]))

    deep, lane = iota((CELLS, 128), 0), iota((CELLS, 128), 1) % S
    pick = [jnp.where(deep == lane * S + z, 1.0, 0.0).astype(BF16) for z in (0, S - 1)]
    wide, lane = iota((128, 128), 0), iota((128, 128), 1) % S
    pick_y = [jnp.where(wide == lane + first, 1.0, 0.0).astype(BF16) for first in (0, 128 - S)]
    quarter = iota((SLOTS * S, 128), 1) // S

    def spread_items(parts, later):
        low = jnp.where(quarter == 0, parts[0], jnp.where(quarter == 1, parts[1], jnp.where(quarter == 2, parts[2], parts[3])))
        high = jnp.where(quarter == later, parts[4], parts[5])
        return low.reshape(SLOTS, S, 128).astype(BF16), high.reshape(SLOTS, S, 128).astype(BF16)

    fetched = set()

    def ready(directions):
        for direction in directions:
            if direction not in fetched:
                fetched.add(direction)
                fetch(direction).wait()

    sol = sol_ref[...].reshape(SLOTS * S, CELLS).astype(BF16)
    for side in range(2):
        ready(LEAVES[2][side])
        parts = [dot(pop[d].reshape(SLOTS * S, CELLS), pick[side]) for d in LEAVES[2][side]] + [dot(sol, pick[side])]
        low, high = spread_items(parts, 2)
        fz[:, side, :, 0:128] = low
        fz[:, side, :, 128:256] = high
    for side in range(2):
        ready(LEAVES[1][side])
        at = slice(CELLS - 128, CELLS) if side else slice(0, 128)
        parts = [dot(pop[d, :, :, at].reshape(SLOTS * S, 128), pick_y[side]) for d in LEAVES[1][side]]
        parts.append(dot(sol[:, at], pick_y[side]))
        low, high = spread_items(parts, 0)
        fy[:, side, :, 0:128] = low
        fy[:, side, :, 128:256] = high
    for side in range(2):
        ready(LEAVES[0][side])

        @pl.loop(0, SLOTS)
        def _(slot):
            if side:
                rows = [pop[d, slot, 16:32, :].astype(F32)[15:16] for d in LEAVES[0][side]]
                rows.append(sol_ref[slot, 31:32, :])
            else:
                rows = [pop[d, slot, 0:16, :].astype(F32)[0:1] for d in LEAVES[0][side]]
                rows.append(sol_ref[slot, 0:1, :])
            rows.append(jnp.zeros((2, CELLS), F32))
            rows = jnp.concatenate(rows, axis=0)
            fx[slot, side] = jnp.concatenate([rows[:, :512], rows[:, 512:]], axis=0).astype(BF16)

    pl.semaphore_wait(barrier, PEERS - 1 + GROUPS - 1)

    def send(src, dst, which, peer):
        return pltpu.make_async_remote_copy(
            src_ref=src.at[peer], dst_ref=dst.at[me], send_sem=send_sem.at[which], recv_sem=recv_sem.at[which],
            device_id={"blk": peer}, device_id_type=pl.DeviceIdType.MESH)

    def all_of(src, dst, which):
        return pltpu.make_async_remote_copy(
            src_ref=src.at[pl.ds(0, PEERS - 1)], dst_ref=dst.at[pl.ds(0, PEERS - 1)], send_sem=send_sem.at[which],
            recv_sem=recv_sem.at[which], device_id={"blk": (me + 1) % PEERS}, device_id_type=pl.DeviceIdType.MESH)

    def table_copy(k):
        return pltpu.make_async_remote_copy(
            src_ref=mine, dst_ref=table_ref.at[grp], send_sem=table_send.at[k], recv_sem=table_recv.at[k],
            device_id={"grp": (grp + k) % GROUPS}, device_id_type=pl.DeviceIdType.MESH)

    left = iota((S, 128), 1) < 64

    @pl.loop(1, PEERS)
    def _(k):
        peer = (me + k) % PEERS
        at_x, at_y, at_z = inv[0, peer], inv[1, peer], inv[2, peer]
        y_part = fy[at_y // 2, at_y % 2]
        z_part = fz[at_z // 2, at_z % 2]
        mixed = jnp.where(left, y_part[:, 128:].astype(F32), z_part[:, 128:].astype(F32)).astype(BF16)
        sa[peer, :, 0:512] = fx[at_x // 2, at_x % 2]
        sa[peer, :, 512:640] = y_part[0:16, 0:128]
        sa[peer, :, 640:768] = mixed[0:16]
        sa[peer, :, 768:896] = y_part[16:32, 0:128]
        sa[peer, :, 896:1024] = mixed[16:32]
        sb[peer] = z_part[:, 0:128]
        send(sa, ra, 0, peer).start()

    @pl.loop(1, PEERS)
    def _(k):
        send(sb, rb, 1, (me + k) % PEERS).start()

    for k in range(1, GROUPS):
        table_copy(k).start()

    all_of(sa, ra, 0).wait_recv()

    def owner(slot, face):
        return nbr[slot, face] // (SLOTS * GROUPS)

    @pl.loop(0, SLOTS)
    def _(slot):
        halves = []
        for side in range(2):
            part = ra[owner(slot, side), :, 0:512].astype(F32)
            halves.append(jnp.concatenate([part[0:8], part[8:16]], axis=1))
        gx_ref[slot] = jnp.concatenate(halves, axis=0).astype(BF16)
        for side in range(2):
            peer = owner(slot, 2 + side)
            gy_ref[slot, side, 0:16, :] = ra[peer, :, 512:768]
            gy_ref[slot, side, 16:32, :] = ra[peer, :, 768:1024]

    ghosts = gx_ref[...].reshape(SLOTS * 16, CELLS)
    ex[0] = dot(ghosts, pick[0]).reshape(SLOTS, 16, 128)
    ex[1] = dot(ghosts, pick[1]).reshape(SLOTS, 16, 128)
    ex[2] = dot(ghosts[:, 0:128], pick_y[0]).reshape(SLOTS, 16, 128)
    ex[3] = dot(ghosts[:, CELLS - 128:], pick_y[1]).reshape(SLOTS, 16, 128)
    row32, lane32 = iota((S, 128), 0), iota((S, 128), 1)
    first = lane32[0:1] < 64

    @pl.loop(0, SLOTS)
    def _(slot):
        y_lo = gy_ref[slot, 0].astype(F32)
        y_hi = gy_ref[slot, 1].astype(F32)
        for side in range(2):
            if side:
                y_row = jnp.where(first, ex[3, slot, 1:2], ex[3, slot, 10:11])
                z_row = jnp.where(first, ex[1, slot, 3:4], ex[1, slot, 12:13])
                third, fourth = y_lo[:, 127:128], y_hi[:, 159:160]
            else:
                y_row = jnp.where(first, ex[2, slot, 9:10], ex[2, slot, 2:3])
                z_row = jnp.where(first, ex[0, slot, 11:12], ex[0, slot, 4:5])
                third, fourth = y_hi[:, 96:97], y_lo[:, 128:129]
            cols = jnp.where(lane32 == 96, third, fourth)
            fy[slot, side, :, 0:128] = jnp.broadcast_to(y_row, (S, 128)).astype(BF16)
            fz[slot, side, :, 0:128] = jnp.where(lane32 < 96, z_row, cols).astype(BF16)

    top = (row32 < 16) & (lane32 < 96)

    @pl.loop(1, PEERS)
    def _(k):
        peer = (me + k) % PEERS
        at_y, at_z = inv[1, peer], inv[2, peer]
        se[peer] = jnp.where(top, fy[at_y // 2, at_y % 2, :, 0:128].astype(F32),
                             fz[at_z // 2, at_z % 2, :, 0:128].astype(F32)).astype(BF16)
        send(se, re, 2, peer).start()

    all_of(sb, rb, 1).wait_recv()
    all_of(se, re, 2).wait_recv()
    item = lane32 // S
    lane = lane32 % S

    @pl.loop(0, SLOTS)
    def _(slot):
        for side in range(2):
            down, up = (1, 2) if side == 0 else (2, 1)
            edge = re[owner(slot, 2 + side), 0:16, :].astype(F32)[0:1]
            plane = gy_ref[slot, side, :, 0:128].astype(F32)
            plane = jnp.where(item == down, jnp.concatenate([edge, plane[:S - 1]], axis=0),
                              jnp.where(item == up, jnp.concatenate([plane[1:], edge], axis=0), plane))
            gy_ref[slot, side, :, 0:128] = plane.astype(BF16)
            peer = owner(slot, 4 + side)
            edges = re[peer].astype(F32)
            edge = edges[16:17]
            plane = rb[peer].astype(F32)
            late = jnp.concatenate([ra[peer, :, 640:768], ra[peer, :, 896:1024]], axis=0).astype(F32)
            third, fourth = edges[:, 96:97], edges[:, 97:98]
            if side == 0:
                moved = jnp.where(lane == 0, third, pltpu.roll(plane, 1, 1))
                moved_late = jnp.where(lane == S - 1, fourth, pltpu.roll(late, 127, 1))
            else:
                moved = jnp.where(lane == S - 1, third, pltpu.roll(plane, 127, 1))
                moved_late = jnp.where(lane == 0, fourth, pltpu.roll(late, 1, 1))
            plane = jnp.where(item == down, jnp.concatenate([edge, plane[:S - 1]], axis=0),
                              jnp.where(item == up, jnp.concatenate([plane[1:], edge], axis=0),
                                        jnp.where(item == 3, moved, plane)))
            gz_ref[slot, side, :, 0:128] = plane.astype(BF16)
            gz_ref[slot, side, :, 128:256] = jnp.where(item == 2, moved_late, late).astype(BF16)

    all_of(sa, ra, 0).wait_send()
    all_of(sb, rb, 1).wait_send()
    all_of(se, re, 2).wait_send()
    for k in range(1, GROUPS):
        table_copy(k).wait()


def exchange(populations, solute, neighbours, inverse, redeal_list):
    vmem, smem, anywhere = (pl.BlockSpec(memory_space=m) for m in (pltpu.VMEM, pltpu.SMEM, pl.ANY))
    return pl.pallas_call(
        exchange_kernel,
        out_shape=(
            jax.ShapeDtypeStruct((SLOTS, 16, CELLS), BF16),
            jax.ShapeDtypeStruct((SLOTS, 2, S, 256), BF16),
            jax.ShapeDtypeStruct((SLOTS, 2, S, 256), BF16),
            jax.ShapeDtypeStruct((GROUPS, 8, 128), I32),
        ),
        in_specs=[anywhere, vmem, smem, smem, smem],
        out_specs=(vmem, vmem, vmem, vmem),
        scratch_shapes=[
            pltpu.VMEM((19, SLOTS, S, CELLS), BF16),
            pltpu.VMEM((SLOTS, 2, 16, 512), BF16),
            pltpu.VMEM((SLOTS, 2, S, 256), BF16),
            pltpu.VMEM((SLOTS, 2, S, 256), BF16),
            pltpu.VMEM((PEERS, 16, 1024), BF16),
            pltpu.VMEM((PEERS, S, 128), BF16),
            pltpu.VMEM((PEERS, S, 128), BF16),
            pltpu.VMEM((PEERS, 16, 1024), BF16),
            pltpu.VMEM((PEERS, S, 128), BF16),
            pltpu.VMEM((PEERS, S, 128), BF16),
            pltpu.VMEM((4, SLOTS, 16, 128), F32),
            pltpu.VMEM((8, 128), I32),
            pltpu.SemaphoreType.DMA((19,)),
            pltpu.SemaphoreType.DMA((3,)),
            pltpu.SemaphoreType.DMA((3,)),
            pltpu.SemaphoreType.DMA((GROUPS,)),
            pltpu.SemaphoreType.DMA((GROUPS,)),
        ],
        compiler_params=pltpu.CompilerParams(collective_id=0, has_side_effects=True, vmem_limit_bytes=48 * 2**20),
        cost_estimate=pl.CostEstimate(flops=10**9, bytes_accessed=12 * 10**6, transcendentals=0),
        name="exchange",
    )(populations, solute, neighbours, inverse, redeal_list)


def pull_block(pop, sol, gx, gy, gz, spread, pulled, grads):
    lane = iota((S, CELLS), 1)
    depth = lane % S
    lane128 = iota((S, 128), 1)
    part = lane128 // S
    x_rows = gx[...].astype(F32)
    y_tiles = [[gy[side, :, 128 * t:128 * t + 128].astype(F32) for t in range(2)] for side in range(2)]
    stack = []
    for side in range(2):
        for item in range(6):
            tile = gz[side, :, 0:128] if item < 4 else gz[side, :, 128:256]
            quarter = item if item < 4 else item - 2
            stack.append(jnp.where(part == quarter, tile.astype(F32), 0.0).astype(BF16))
    z_all = dot(jnp.concatenate(stack, axis=0), spread[...])

    def z_ghost(side, item):
        at = (side * 6 + item) * S
        return z_all[at:at + S]

    def y_merge(block, side, item, cz):
        tile = y_tiles[side][item // 4]
        start = (item % 4) * S
        target = 0 if side == 0 else 128 - S
        shift = (target + cz - start) % 128
        if shift:
            tile = pltpu.roll(tile, shift, 1)
        if side == 0:
            return jnp.concatenate([jnp.where(lane128 < S, tile, block[:, 0:128]), block[:, 128:]], axis=1)
        return jnp.concatenate([block[:, :CELLS - 128], jnp.where(lane128 >= 128 - S, tile, block[:, CELLS - 128:])], axis=1)

    def shift_x(block, side, item):
        row = x_rows[side * 8 + item:side * 8 + item + 1]
        if side == 0:
            return jnp.concatenate([row, block[:S - 1]], axis=0)
        return jnp.concatenate([block[1:], row], axis=0)

    for d, (cx, cy, cz) in enumerate(VELOCITY):
        block = pop[d].astype(F32)
        if cx:
            side = 0 if cx == 1 else 1
            block = shift_x(block, side, LEAVES[0][1 - side].index(d))
        shift = (S * cy + cz) % CELLS
        if shift:
            block = pltpu.roll(block, shift, 1)
        if cy:
            side = 0 if cy == 1 else 1
            block = y_merge(block, side, LEAVES[1][1 - side].index(d), cz)
        if cz:
            side = 0 if cz == 1 else 1
            edge = 0 if cz == 1 else S - 1
            block = jnp.where(depth == edge, z_ghost(side, LEAVES[2][1 - side].index(d)), block)
        pulled[d] = block
    here = sol[...]
    below, above = shift_x(here, 0, 5), shift_x(here, 1, 5)
    total = below + above
    grads[1] = above - below
    below = y_merge(pltpu.roll(here, S, 1), 0, 5, 0)
    above = y_merge(pltpu.roll(here, CELLS - S, 1), 1, 5, 0)
    total = total + below + above
    grads[2] = above - below
    below = jnp.where(depth == 0, z_ghost(0, 5), pltpu.roll(here, 1, 1))
    above = jnp.where(depth == S - 1, z_ghost(1, 5), pltpu.roll(here, CELLS - 1, 1))
    grads[3] = above - below
    grads[0] = total + below + above - 6.0 * here


def update(pulled, grads, sol, solid, rows, lanes, put):
    f = [pulled[d, rows, lanes] for d in range(19)]
    pair_sum = [f[i] + f[i + 1] for i in range(1, 19, 2)]
    pair_dif = [f[i] - f[i + 1] for i in range(1, 19, 2)]
    straight = pair_sum[0] + pair_sum[1] + pair_sum[2]
    slanted = (pair_sum[3] + pair_sum[4]) + (pair_sum[5] + pair_sum[6]) + (pair_sum[7] + pair_sum[8])
    density = f[0] * (1.0 / 3.0) + straight * (1.0 / 18.0) + slanted * (1.0 / 36.0)
    dif = pair_dif
    over = 1.0 / density
    over36 = over * (1.0 / 36.0)
    ux = (2.0 * dif[0] + ((dif[3] + dif[4]) + (dif[5] + dif[6]))) * over36
    uy = (2.0 * dif[1] + ((dif[3] - dif[4]) + (dif[7] + dif[8]))) * over36
    uz = (2.0 * dif[2] + ((dif[5] - dif[6]) + (dif[7] - dif[8]))) * over36
    amount = solid[rows, lanes]
    keep = 1.0 - amount
    if put is not None:
        scale = (1.0 / relax_time) * keep * density
        base = scale - (1.5 * scale) * (ux * ux + uy * uy + uz * uz)
        curve, slope = 4.5 * scale, 3.0 * scale
        rest = (1.0 / relax_time - 1.0) * keep
        even_part, odd_part = 0.5 * (amount - rest), 0.5 * (amount + rest)
        put(0, base + (amount - rest) * f[0])
        along_all = (ux, uy, uz, ux + uy, ux - uy, ux + uz, ux - uz, uy + uz, uy - uz)
        for pair in range(9):
            along = along_all[pair]
            even = base + (curve * along) * along + even_part * pair_sum[pair]
            odd = slope * along - odd_part * pair_dif[pair]
            put(2 * pair + 1, even + odd)
            put(2 * pair + 2, even - odd)
    mixed = (sol[rows, lanes] + diffusivity * grads[0, rows, lanes]
             - 0.5 * (ux * grads[1, rows, lanes] + uy * grads[2, rows, lanes] + uz * grads[3, rows, lanes]))
    reaction = rate_const * amount * keep * (saturation - mixed)
    return mixed + reaction, amount - reaction


def make_spread(spread):
    deep, lane = iota((128, CELLS), 0), iota((128, CELLS), 1)
    spread[...] = jnp.where(deep % S == lane // S, 1.0, 0.0).astype(BF16)


def chunks(body):
    @pl.loop(0, 16)
    def _(step):
        rows = pl.ds(pl.multiple_of((step // 8) * 16, 16), 16)
        lanes = pl.ds(pl.multiple_of((step % 8) * 128, 128), 128)
        body(rows, lanes)


def front_kernel(front, redeal, pop, sol, solid, gx, gy, gz, send1, send2, send3, ones_ref, spread, pulled, grads):
    step = pl.program_id(0)

    @pl.when(step == 0)
    def _():
        make_spread(spread)

    ones_ref[...] = jnp.ones(ones_ref.shape, BF16)
    pull_block(pop.at[0], sol.at[0], gx.at[0], gy.at[0], gz.at[0], spread, pulled, grads)
    for target, ref in enumerate((send1, send2, send3)):
        @pl.when(step == target)
        def _():
            def one(rows, lanes):
                ref[0, rows, lanes], ref[1, rows, lanes] = update(pulled, grads, sol.at[0], solid.at[0], rows, lanes, None)

            chunks(one)


def rest_kernel(front, pop, sol, solid, gx, gy, gz, old_ref, new_pop, new_sol, new_solid, spread, pulled, grads):
    @pl.when(pl.program_id(0) == 0)
    def _():
        make_spread(spread)

    pull_block(pop.at[0], sol.at[0], gx.at[0], gy.at[0], gz.at[0], spread, pulled, grads)

    def one(rows, lanes):
        def put(direction, value):
            new_pop[0, direction, rows, lanes] = value.astype(BF16)

        new_sol[0, rows, lanes], new_solid[0, rows, lanes] = update(
            pulled, grads, sol.at[0], solid.at[0], rows, lanes, put)

    chunks(one)


def front_slot(step, front, redeal):
    group = front[0] // SLOTS % GROUPS
    slot = front[0] % SLOTS
    for entry in range(1, 3):
        ahead = (redeal[entry] // SLOTS % GROUPS - group + GROUPS) % GROUPS
        slot = jnp.where(ahead == step + 1, front[entry] % SLOTS, slot)
    return slot


def rest_slot(step, front):
    a, b, c = (front[entry] % SLOTS for entry in range(3))
    low, high = jnp.minimum(a, b), jnp.maximum(a, b)
    mid, high = jnp.minimum(high, c), jnp.maximum(high, c)
    low, mid = jnp.minimum(low, mid), jnp.maximum(low, mid)
    slot = step
    for taken in (low, mid, high):
        slot = slot + jnp.where(slot >= taken, 1, 0)
    return slot


def block_specs(pick):
    shapes = ((1, 19, S, CELLS), (1, S, CELLS), (1, S, CELLS), (1, 16, CELLS), (1, 2, S, 256), (1, 2, S, 256))
    return [pl.BlockSpec(shape, lambda step, *refs, n=len(shape): (pick(step, *refs),) + (0,) * (n - 1)) for shape in shapes]


WORK = [
    pltpu.VMEM((128, CELLS), BF16),
    pltpu.VMEM((19, S, CELLS), F32),
    pltpu.VMEM((4, S, CELLS), F32),
]


def front_update(front, redeal, populations, solute, solid_fraction, gx, gy, gz):
    specs = block_specs(front_slot)
    sent = pl.BlockSpec((2, S, CELLS), lambda *_: (0, 0, 0))
    return pl.pallas_call(
        front_kernel,
        out_shape=tuple(jax.ShapeDtypeStruct((2, S, CELLS), F32) for _ in range(3))
        + (jax.ShapeDtypeStruct(populations.shape, BF16),),
        grid_spec=pltpu.PrefetchScalarGridSpec(
            num_scalar_prefetch=2, grid=(3,), in_specs=specs, out_specs=(sent, sent, sent, specs[0]),
            scratch_shapes=WORK),
        compiler_params=pltpu.CompilerParams(vmem_limit_bytes=40 * 2**20),
        cost_estimate=pl.CostEstimate(flops=2 * 10**7, bytes_accessed=9 * 10**6, transcendentals=0),
        name="front",
    )(front, redeal, populations, solute, solid_fraction, gx, gy, gz)


def rest_update(front, populations, solute, solid_fraction, gx, gy, gz, new_populations):
    specs = block_specs(rest_slot)
    return pl.pallas_call(
        rest_kernel,
        out_shape=(
            jax.ShapeDtypeStruct(populations.shape, BF16),
            jax.ShapeDtypeStruct(solute.shape, F32),
            jax.ShapeDtypeStruct(solute.shape, F32),
        ),
        grid_spec=pltpu.PrefetchScalarGridSpec(
            num_scalar_prefetch=1, grid=(5,), in_specs=specs + [pl.BlockSpec(memory_space=pl.ANY)],
            out_specs=tuple(specs[:3]), scratch_shapes=WORK),
        input_output_aliases={7: 0},
        compiler_params=pltpu.CompilerParams(vmem_limit_bytes=40 * 2**20),
        cost_estimate=pl.CostEstimate(flops=10**8, bytes_accessed=16 * 10**6, transcendentals=0),
        name="rest",
    )(front, populations, solute, solid_fraction, gx, gy, gz, new_populations)


def place_kernel(front, table, got1, got2, got3, old_sol, old_solid, new_sol, new_solid):
    for k, got in enumerate((got1, got2, got3)):
        @pl.when(pl.program_id(0) == k)
        def _():
            new_sol[0] = got[0]
            new_solid[0] = got[1]


def place_slot(step, front, table):
    group = front[0] // SLOTS % GROUPS
    source = (group + GROUPS - 1 - step) % GROUPS
    slot = table[source, 0] % SLOTS
    for entry in range(1, 3):
        place = table[source, entry]
        slot = jnp.where(place // SLOTS % GROUPS == group, place % SLOTS, slot)
    return slot


def place_front(front, table, received, new_solute, new_solid):
    whole = pl.BlockSpec((2, S, CELLS), lambda *_: (0, 0, 0))
    landed = pl.BlockSpec((1, S, CELLS), lambda *refs: (place_slot(*refs), 0, 0))
    anywhere = pl.BlockSpec(memory_space=pl.ANY)
    return pl.pallas_call(
        place_kernel,
        out_shape=tuple(jax.ShapeDtypeStruct(new_solute.shape, F32) for _ in range(2)),
        grid_spec=pltpu.PrefetchScalarGridSpec(
            num_scalar_prefetch=2, grid=(3,), in_specs=[whole] * 3 + [anywhere] * 2, out_specs=(landed, landed)),
        input_output_aliases={5: 0, 6: 1},
        cost_estimate=pl.CostEstimate(flops=0, bytes_accessed=2 * 10**6, transcendentals=0),
        name="place",
    )(front, table, *received, new_solute, new_solid)


def body(populations, solute, solid_fraction, neighbours, front_list, redeal_list):
    owner = (neighbours // (SLOTS * GROUPS)).reshape(SLOTS, 3, 2)
    face = 2 * jnp.arange(SLOTS, dtype=I32)[:, None, None] + jnp.arange(2, dtype=I32)[None, None, :]
    hits = owner[..., None] == jnp.arange(PEERS, dtype=I32)
    inverse = jnp.sum(jnp.where(hits, face[..., None], 0), axis=(0, 2), dtype=I32)
    gx, gy, gz, table = exchange(populations, solute, neighbours, inverse, redeal_list)
    *sent, new_populations = front_update(front_list, redeal_list, populations, solute, solid_fraction, gx, gy, gz)
    received = [
        lax.ppermute(sent[k], "grp", [(g, (g + k + 1) % GROUPS) for g in range(GROUPS)]) for k in range(GROUPS - 1)
    ]
    new_populations, new_solute, new_solid = rest_update(
        front_list, populations, solute, solid_fraction, gx, gy, gz, new_populations)
    new_solute, new_solid = place_front(front_list, table[:, 0, :8], received, new_solute, new_solid)
    return new_populations, new_solute, new_solid


def solution(mesh):
    deal = ("blk", "grp")
    return jax.shard_map(
        body,
        mesh=mesh,
        in_specs=(P(deal, None, None, None), P(deal, None, None), P(deal, None, None), P(deal, None), P(deal), P(deal)),
        out_specs=(P(deal, None, None, None), P(deal, None, None), P(deal, None, None)),
        check_vma=False,
    )
```

time: 500 us -> 70.1 us (0.14); the launches traced: 491 us -> 69.9 us
  local copies, waits for them, and re-layouts: 292 us -> 5.35 us
  other arithmetic: 90.2 us -> 0.8 us
  Pallas kernels: 0 us -> 57.3 us
  starting transfers between devices: 57.2 us -> 5.75 us
  waiting for transfers between devices: 46.1 us -> 0.01 us
    slice x62 -> x1, local copies, waits for them, and re-layouts: 109 us -> 0.58 us  [body(): table[:, 0, :8]]
    reshape x31 -> x0, local copies, waits for them, and re-layouts: 95.8 us -> none  [the longest x1 46.3 us: face_planes(): populations.reshape(block_count, velocities, extent, extent, extent)]
    pallas_call x0 -> x4, Pallas kernels: none -> 57.3 us  [the longest x1 34.9 us: exchange(): pl.pallas_call(exchange_kernel, out_shape=(jax.ShapeDtypeStruct((SLOTS, 1...]
    all_to_all x11 -> x0, starting transfers between devices: 57.2 us -> none  [the longest x2 11.9 us: trade_with_rows(): lax.all_to_all(pack_faces([sol_upper, sol_lower], out_slot, slot_total).a...]
    all_to_all x11 -> x0, waiting for transfers between devices: 46.1 us -> none  [the longest x2 19.6 us: trade_with_rows(): lax.all_to_all(pack_faces([upper_face, lower_face], out_slot, slot_total)...]
    unnamed x18 -> x0, other arithmetic: 36.2 us -> none
    unnamed x151 -> x18, local copies, waits for them, and re-layouts: 31.8 us -> 4.68 us
    sub x1 -> x0, other arithmetic: 19.1 us -> none  [local_update(): return (new_populations, mixed + reaction, solid_fraction - reaction)]
  transfers between devices with their start and end apart: 11 -> 3, of which waited for: 6 -> 0; matrix products, arithmetic and copies ran while one was open for 63% -> 1% of each run, Pallas kernels for 0% -> 17%
where the time goes in v1:
time: 70.1 us; the launch traced here: 69.9 us
  Pallas kernels  57.3 us (82%)
  starting transfers between devices  5.75 us (8%)
  local copies, waits for them, and re-layouts  5.35 us (8%)
  other arithmetic  0.8 us (1%)
  between operations  0.72 us (1%)
    pallas_call x1, Pallas kernels, exchange(): pl.pallas_call(exchange_kernel, out_shape=(jax.ShapeDtypeStruct((SLOTS, 1...  34.9 us
    pallas_call x1, Pallas kernels, rest_update(): pl.pallas_call(rest_kernel, out_shape=(jax.ShapeDtypeStruct(populations.s...  12.2 us
    pallas_call x1, Pallas kernels, front_update(): pl.pallas_call(front_kernel, out_shape=tuple((jax.ShapeDtypeStruct((2, S,...  6.64 us
    ppermute x3, starting transfers between devices, body(): lax.ppermute(sent[k], 'grp', [(g, (g + k + 1) % GROUPS) for g in range(GR...  5.75 us
    unnamed x18, local copies, waits for them, and re-layouts  4.68 us
    pallas_call x1, Pallas kernels, place_front(): pl.pallas_call(place_kernel, out_shape=tuple((jax.ShapeDtypeStruct(new_so...  3.57 us
  transfers between devices with their start and end apart: 3, of which 0 were waited for; matrix products, arithmetic and copies ran while one was open for 1% of the time, Pallas kernels for 17%

profile of v1, /device:TPU:1, one launch (start us, length us, event | category | flops | bytes accessed | tf_op | source)
XLA Modules:
  0.0 69.9 jit_solution(14812839045315425164)
XLA Ops:
  0.6 0.0 copy-start.4
  0.7 0.7 add_select_fusion
  1.4 0.1 copy.14
  1.5 0.0 copy-start
  1.5 0.1 select_reduce_fusion.inv
  1.6 0.0 copy-start.1
  1.6 1.4 %copy-done.1 = f32[8,32,1024]{2,1,0:T(8,128)S(1)} copy-done((f32[8,32,1024]{2,1,0:T(8,128)S(1)}, f32[8,32,1024]{2,1,0:T(8,128)}, u32[]{:S(2)}) %copy-start.1) | copy-done | bytes 1048600
  2.9 0.0 copy-start.3
  2.9 0.9 %copy-done.3 = s32[8,6]{1,0:T(8,128)S(1)} copy-done((s32[8,6]{1,0:T(8,128)S(1)}, s32[8,6]{1,0:T(8,128)}, u32[]{:S(2)}) %copy-start.3) | copy-done | bytes 216
  3.9 0.0 copy-start.5
  3.9 0.9 %copy-done.5 = s32[3]{0:T(128)S(1)} copy-done((s32[3]{0:T(128)S(1)}, s32[3]{0:T(128)}, u32[]{:S(2)}) %copy-start.5) | copy-done | bytes 36
  4.8 0.0 copy-start.2
  4.8 34.9 %exchange.1 = (bf16[8,16,1024]{2,1,0:T(8,128)(2,1)S(1)}, bf16[8,2,32,256]{3,2,1,0:T(8,128)(2,1)S(1)}, bf16[8,2,32,256]{3,2,1,0:T(8,128)(2,1)S(1)}, s32[4,8,128]{2,1,0:T(8,128)S(1)}) custom-call(bf16[8,19,32,1024]{3,2,1,0:T(8,128)(2,1)} %pop.3, f32[8,32,1024]{2,1,0:T(8,128)S(1)} %copy-done.1, s32[8,6]{1,0:T(8,128)S(1)} %copy-done.3, ...), custom_call_target="tpu_custom_call" | custom-call | flops 1000000000 | bytes 12000000 | tf_op jit(solution)/shard_map/exchange/pallas_call | solution.py:246
  39.7 0.0 copy-done.4
  39.7 0.0 copy-done
  39.7 0.0 copy-done.2
  39.7 6.6 %front.4 = (f32[2,32,1024]{2,1,0:T(8,128)S(1)}, f32[2,32,1024]{2,1,0:T(8,128)S(1)}, f32[2,32,1024]{2,1,0:T(8,128)S(1)}, bf16[8,19,32,1024]{3,2,1,0:T(8,128)(2,1)}) custom-call(s32[3]{0:T(128)S(1)} %copy-done.4, s32[3]{0:T(128)S(1)} %copy-done.5, bf16[8,19,32,1024]{3,2,1,0:T(8,128)(2,1)S(1)} %copy-done, f32[8,32,1024]{2,1,0:T(8,128)S(1)} %copy-done.1, ...), custom_call_target="tpu_custom_call" | custom-call | flops 20000000 | bytes 9000000 | tf_op jit(solution)/shard_map/front/pallas_call | solution.py:465
  46.4 1.7 %collective-permute-start = (f32[2,32,1024]{2,1,0:T(8,128)S(1)}, f32[2,32,1024]{2,1,0:T(8,128)S(1)}, u32[]{:S(2)}, u32[]{:S(2)}) collective-permute-start(f32[2,32,1024]{2,1,0:T(8,128)S(1)} %get-tuple-element.22), channel_id=1, source_target_pairs={{0,1},{1,2},{2,3},{3,0},{4,5},{5,6},{6,7},{7,4},{8,9},{9,10},{10,1... | collective-permute-start | bytes 786440 | tf_op jit(solution)/shard_map/ppermute | solution.py:538
  48.1 3.3 %collective-permute-start.1 = (f32[2,32,1024]{2,1,0:T(8,128)S(1)}, f32[2,32,1024]{2,1,0:T(8,128)S(1)}, u32[]{:S(2)}, u32[]{:S(2)}) collective-permute-start(f32[2,32,1024]{2,1,0:T(8,128)S(1)} %get-tuple-element.23), channel_id=1, source_target_pairs={{0,2},{1,3},{2,0},{3,1},{4,6},{5,7},{6,4},{7,5},{8,10},{9,11},{10,... | collective-permute-start | bytes 786440 | tf_op jit(solution)/shard_map/ppermute | solution.py:538
  51.4 0.7 %collective-permute-start.2 = (f32[2,32,1024]{2,1,0:T(8,128)S(1)}, f32[2,32,1024]{2,1,0:T(8,128)S(1)}, u32[]{:S(2)}, u32[]{:S(2)}) collective-permute-start(f32[2,32,1024]{2,1,0:T(8,128)S(1)} %get-tuple-element.24), channel_id=1, source_target_pairs={{0,3},{1,0},{2,1},{3,2},{4,7},{5,4},{6,5},{7,6},{8,11},{9,8},{10,9... | collective-permute-start | bytes 786440 | tf_op jit(solution)/shard_map/ppermute | solution.py:538
  52.1 0.6 slice.3
  52.7 12.2 %rest.1 = (bf16[8,19,32,1024]{3,2,1,0:T(8,128)(2,1)}, f32[8,32,1024]{2,1,0:T(8,128)}, f32[8,32,1024]{2,1,0:T(8,128)}) custom-call(s32[3]{0:T(128)S(1)} %copy-done.4, bf16[8,19,32,1024]{3,2,1,0:T(8,128)(2,1)S(1)} %copy-done, f32[8,32,1024]{2,1,0:T(8,128)S(1)} %copy-done.1, f32[8,32,1024]{2,1,0:T(8,128)S(1)} %copy-done.2, ...), custom_call_target="tpu_custom_call", output_to_operand_aliasing={{0}: (7, {})} | custom-call | flops 100000000 | bytes 16000000 | tf_op jit(solution)/shard_map/rest/pallas_call | solution.py:480
  64.9 0.0 collective-permute-done.got1
  64.9 0.0 copy-start.6
  64.9 0.0 collective-permute-done.1.got2
  64.9 0.0 copy-start.7
  64.9 0.0 collective-permute-done.2.got3
  64.9 0.7 %copy-done.7 = f32[2,32,1024]{2,1,0:T(8,128)} copy-done((f32[2,32,1024]{2,1,0:T(8,128)}, f32[2,32,1024]{2,1,0:T(8,128)S(1)}, u32[]{:S(2)}) %copy-start.7) | copy-done | bytes 262168
  65.6 0.0 copy-start.8
  65.6 0.7 %copy-done.8 = f32[2,32,1024]{2,1,0:T(8,128)} copy-done((f32[2,32,1024]{2,1,0:T(8,128)}, f32[2,32,1024]{2,1,0:T(8,128)S(1)}, u32[]{:S(2)}) %copy-start.8) | copy-done | bytes 262168
  66.3 0.0 copy-done.6
  66.3 3.6 %place.1 = (f32[8,32,1024]{2,1,0:T(8,128)}, f32[8,32,1024]{2,1,0:T(8,128)}) custom-call(s32[3]{0:T(128)} %front.7, s32[4,8]{1,0:T(4,128)} %bitcast.3, f32[2,32,1024]{2,1,0:T(8,128)} %copy-done.6, f32[2,32,1024]{2,1,0:T(8,128)} %copy-done.7, f32[2,32,1024]{2,1,0:T(8,128)} %copy-done.8, ...), custom_call_target="tpu_custom_call", output_to_operand_aliasing={{0}: (5, {}), {1}: (6, {})} | custom-call | bytes 2000000 | tf_op jit(solution)/shard_map/place/pallas_call | solution.py:519
  (3 shorter events, 0.0 us)
Async XLA Ops:
  0.6 39.1 %copy-start.4 = (s32[3]{0:T(128)S(1)}, s32[3]{0:T(128)}, u32[]{:S(2)}) copy-start(s32[3]{0:T(128)} %front.7) | copy-start | bytes 40
  1.5 38.2 %copy-start = (bf16[8,19,32,1024]{3,2,1,0:T(8,128)(2,1)S(1)}, bf16[8,19,32,1024]{3,2,1,0:T(8,128)(2,1)}, u32[]{:S(2)}) copy-start(bf16[8,19,32,1024]{3,2,1,0:T(8,128)(2,1)} %pop.3) | copy-start | bytes 29884420
  1.6 1.4 %copy-start.1 = (f32[8,32,1024]{2,1,0:T(8,128)S(1)}, f32[8,32,1024]{2,1,0:T(8,128)}, u32[]{:S(2)}) copy-start(f32[8,32,1024]{2,1,0:T(8,128)} %sol.3) | copy-start | bytes 3145732
  2.9 0.9 %copy-start.3 = (s32[8,6]{1,0:T(8,128)S(1)}, s32[8,6]{1,0:T(8,128)}, u32[]{:S(2)}) copy-start(s32[8,6]{1,0:T(8,128)} %nbr.1) | copy-start | bytes 580
  3.9 0.9 %copy-start.5 = (s32[3]{0:T(128)S(1)}, s32[3]{0:T(128)}, u32[]{:S(2)}) copy-start(s32[3]{0:T(128)} %redeal.3) | copy-start | bytes 40
  4.8 34.9 %copy-start.2 = (f32[8,32,1024]{2,1,0:T(8,128)S(1)}, f32[8,32,1024]{2,1,0:T(8,128)}, u32[]{:S(2)}) copy-start(f32[8,32,1024]{2,1,0:T(8,128)} %solid.3) | copy-start | bytes 3145732
  46.4 18.5 %collective-permute-start = (f32[2,32,1024]{2,1,0:T(8,128)S(1)}, f32[2,32,1024]{2,1,0:T(8,128)S(1)}, u32[]{:S(2)}, u32[]{:S(2)}) collective-permute-start(f32[2,32,1024]{2,1,0:T(8,128)S(1)} %get-tuple-element.22), channel_id=1, source_target_pairs={{0,1},{1,2},{2,3},{3,0},{4,5},{5,6},{6,7},{7,4},{8,9},{9,10},{10,1... | collective-permute-start | bytes 786440 | tf_op jit(solution)/shard_map/ppermute | solution.py:538
  48.1 16.8 %collective-permute-start.1 = (f32[2,32,1024]{2,1,0:T(8,128)S(1)}, f32[2,32,1024]{2,1,0:T(8,128)S(1)}, u32[]{:S(2)}, u32[]{:S(2)}) collective-permute-start(f32[2,32,1024]{2,1,0:T(8,128)S(1)} %get-tuple-element.23), channel_id=1, source_target_pairs={{0,2},{1,3},{2,0},{3,1},{4,6},{5,7},{6,4},{7,5},{8,10},{9,11},{10,... | collective-permute-start | bytes 786440 | tf_op jit(solution)/shard_map/ppermute | solution.py:538
  51.4 13.5 %collective-permute-start.2 = (f32[2,32,1024]{2,1,0:T(8,128)S(1)}, f32[2,32,1024]{2,1,0:T(8,128)S(1)}, u32[]{:S(2)}, u32[]{:S(2)}) collective-permute-start(f32[2,32,1024]{2,1,0:T(8,128)S(1)} %get-tuple-element.24), channel_id=1, source_target_pairs={{0,3},{1,0},{2,1},{3,2},{4,7},{5,4},{6,5},{7,6},{8,11},{9,8},{10,9... | collective-permute-start | bytes 786440 | tf_op jit(solution)/shard_map/ppermute | solution.py:538
  64.9 1.4 %copy-start.6 = (f32[2,32,1024]{2,1,0:T(8,128)}, f32[2,32,1024]{2,1,0:T(8,128)S(1)}, u32[]{:S(2)}) copy-start(f32[2,32,1024]{2,1,0:T(8,128)S(1)} %collective-permute-done.got1) | copy-start | bytes 786436
  64.9 0.7 %copy-start.7 = (f32[2,32,1024]{2,1,0:T(8,128)}, f32[2,32,1024]{2,1,0:T(8,128)S(1)}, u32[]{:S(2)}) copy-start(f32[2,32,1024]{2,1,0:T(8,128)S(1)} %collective-permute-done.1.got2) | copy-start | bytes 786436
  65.6 0.7 %copy-start.8 = (f32[2,32,1024]{2,1,0:T(8,128)}, f32[2,32,1024]{2,1,0:T(8,128)S(1)}, u32[]{:S(2)}) copy-start(f32[2,32,1024]{2,1,0:T(8,128)S(1)} %collective-permute-done.2.got3) | copy-start | bytes 786436

commit v2 on v1

v2 whole, which is shorter than its diff:
```python
import jax
import jax.numpy as jnp
from jax import lax
from jax.experimental import pallas as pl
from jax.experimental.pallas import tpu as pltpu
from jax.sharding import PartitionSpec as P

VELOCITY = (
    (0, 0, 0), (1, 0, 0), (-1, 0, 0), (0, 1, 0), (0, -1, 0), (0, 0, 1), (0, 0, -1),
    (1, 1, 0), (-1, -1, 0), (1, -1, 0), (-1, 1, 0), (1, 0, 1), (-1, 0, -1), (1, 0, -1),
    (-1, 0, 1), (0, 1, 1), (0, -1, -1), (0, 1, -1), (0, -1, 1),
)
LEAVES = (
    ((2, 8, 10, 12, 14), (1, 7, 9, 11, 13)),
    ((4, 8, 9, 16, 18), (3, 7, 10, 15, 17)),
    ((6, 12, 13, 16, 17), (5, 11, 14, 15, 18)),
)
FETCH = (2, 8, 10, 12, 14, 1, 7, 9, 11, 13, 15, 16, 17, 18, 3, 4, 6, 5)
SLOTS = 8
S = 32
CELLS = S * S
PEERS = 32
GROUPS = 4
F32, BF16, I32 = jnp.float32, jnp.bfloat16, jnp.int32
relax_time = 0.8
diffusivity = 0.1
rate_const = 0.5
saturation = 1.0


def iota(shape, dim):
    return lax.broadcasted_iota(I32, shape, dim)


def dot(a, b):
    return jnp.dot(a, b, preferred_element_type=F32)


def exchange_kernel(pop_hbm, sol_hbm, nbr_hbm, redeal_hbm, gx_ref, gy_ref, gz_ref, table_ref,
                    pop, sol_ref, xr, fx, fy, fz, lx, ly, ey, ez, s1, s2, s3, r1, r2, r3, mine, inv_vmem,
                    nbr, inv, redeal, fetch_sem, small_sem, send_sem, recv_sem, table_send, table_recv):
    me = lax.axis_index("blk")
    grp = lax.axis_index("grp")

    def fetch(direction):
        return pltpu.make_async_copy(pop_hbm.at[:, direction], pop.at[direction], fetch_sem.at[direction])

    nbr_copy = pltpu.make_async_copy(nbr_hbm, nbr, small_sem.at[0])
    redeal_copy = pltpu.make_async_copy(redeal_hbm, redeal, small_sem.at[1])
    inv_copy = pltpu.make_async_copy(inv_vmem, inv, small_sem.at[2])
    sol_copy = pltpu.make_async_copy(sol_hbm, sol_ref, small_sem.at[3])
    nbr_copy.start()
    redeal_copy.start()
    sol_copy.start()
    for direction in FETCH:
        fetch(direction).start()

    barrier = pltpu.get_barrier_semaphore()

    @pl.loop(1, PEERS)
    def _(k):
        pl.semaphore_signal(barrier, inc=1, device_id={"blk": (me + k) % PEERS}, device_id_type=pl.DeviceIdType.MESH)

    for k in range(1, GROUPS):
        pl.semaphore_signal(barrier, inc=1, device_id={"grp": (grp + k) % GROUPS}, device_id_type=pl.DeviceIdType.MESH)

    deep, lane = iota((CELLS, 128), 0), iota((CELLS, 128), 1) % S
    pick = [jnp.where(deep == lane * S + z, 1.0, 0.0).astype(BF16) for z in (0, S - 1)]
    wide, lane = iota((128, 128), 0), iota((128, 128), 1) % S
    pick_y = [jnp.where(wide == lane + first, 1.0, 0.0).astype(BF16) for first in (0, 128 - S)]

    nbr_copy.wait()
    redeal_copy.wait()

    def owner(slot, face):
        return nbr[slot, face] // (SLOTS * GROUPS)

    row8, lane8 = iota((8, 128), 0), iota((8, 128), 1)
    found = jnp.zeros((8, 128), I32)
    for axis in range(3):
        hit = jnp.zeros((8, 128), I32)
        for slot in range(SLOTS):
            for side in range(2):
                hit = jnp.where(lane8 == owner(slot, 2 * axis + side), 2 * slot + side, hit)
        found = jnp.where(row8 == axis, hit, found)
    inv_vmem[...] = found
    inv_copy.start()
    lane1 = iota((1, 128), 1)
    mine[...] = jnp.where(lane1 == 0, redeal[0], jnp.where(lane1 == 1, redeal[1], redeal[2]))
    sol_copy.wait()

    fetched = set()

    def ready(directions):
        for direction in directions:
            if direction not in fetched:
                fetched.add(direction)
                fetch(direction).wait()

    ready(LEAVES[0][0] + LEAVES[0][1])

    @pl.loop(0, SLOTS)
    def _(slot):
        faces = []
        for side in range(2):
            at, row = (16, 15) if side else (0, 0)
            rows = [pop[d, slot, at:at + 16, :].astype(F32)[row:row + 1] for d in LEAVES[0][side]]
            rows.append(sol_ref[slot, at + row:at + row + 1, :])
            rows.append(jnp.zeros((2, CELLS), F32))
            rows = jnp.concatenate(rows, axis=0)
            fx[2 * slot + side] = jnp.concatenate([rows[:, :512], rows[:, 512:]], axis=0).astype(BF16)
            faces.append(rows)
        xr[slot] = jnp.concatenate(faces, axis=0).astype(BF16)

    faces = xr[...].reshape(SLOTS * 16, CELLS)
    z_low, z_top = dot(faces, pick[0]), dot(faces, pick[1])
    y_low, y_top = dot(faces[:, 0:128], pick_y[0]), dot(faces[:, CELLS - 128:], pick_y[1])
    quarter1 = lane1 // S
    ready((15, 16, 17, 18))
    high = slice(CELLS - 128, CELLS)
    lane16 = iota((16, 128), 1)

    def across(d, at, z):
        one = jnp.where(lane16 == z, 1.0, 0.0).astype(BF16)
        tile = pop[d, :, :, at].reshape(SLOTS * S, 128)
        return lax.dot_general(one, tile, (((1,), (1,)), ((), ())), preferred_element_type=F32)

    y_lines = ((across(16, slice(0, 128), 0), across(18, slice(0, 128), S - 1)),
               (across(15, high, 127), across(17, high, 128 - S)))
    for slot in range(SLOTS):
        for side in range(2):
            row = slot * 16 + side * 8
            four = (y_top, y_low, z_top, z_low) if side else (y_low, y_top, z_low, z_top)
            four = [part[row + 1 + i:row + 2 + i] for i, part in enumerate(four)]
            line = jnp.where(quarter1 == 0, four[0], jnp.where(quarter1 == 1, four[1], jnp.where(quarter1 == 2, four[2], four[3])))
            lx[2 * slot + side] = jnp.broadcast_to(line, (16, 128)).astype(BF16)
            tiles = [part[:, 128 * (slot // 4):128 * (slot // 4) + 128] for part in y_lines[side]]
            shift = (128 - S * (slot % 4)) % 128
            if shift:
                tiles[0] = pltpu.roll(tiles[0], shift, 1)
            shift = (shift + S) % 128
            if shift:
                tiles[1] = pltpu.roll(tiles[1], shift, 1)
            ly[2 * slot + side] = jnp.where(lane16 < S, tiles[0], tiles[1]).astype(BF16)

    inv_copy.wait()
    pl.semaphore_wait(barrier, PEERS - 1 + GROUPS - 1)

    def send(src, dst, which, peer):
        return pltpu.make_async_remote_copy(
            src_ref=src.at[peer], dst_ref=dst.at[me], send_sem=send_sem.at[which], recv_sem=recv_sem.at[which],
            device_id={"blk": peer}, device_id_type=pl.DeviceIdType.MESH)

    def all_of(src, dst, which):
        return pltpu.make_async_remote_copy(
            src_ref=src.at[pl.ds(0, PEERS - 1)], dst_ref=dst.at[pl.ds(0, PEERS - 1)], send_sem=send_sem.at[which],
            recv_sem=recv_sem.at[which], device_id={"blk": (me + 1) % PEERS}, device_id_type=pl.DeviceIdType.MESH)

    def table_copy(k):
        return pltpu.make_async_remote_copy(
            src_ref=mine, dst_ref=table_ref.at[grp], send_sem=table_send.at[k], recv_sem=table_recv.at[k],
            device_id={"grp": (grp + k) % GROUPS}, device_id_type=pl.DeviceIdType.MESH)

    upper8 = iota((16, 128), 0) < 8

    @pl.loop(1, PEERS)
    def _(k):
        peer = (me + k) % PEERS
        s1[peer] = jnp.where(upper8, lx[inv[0, peer]].astype(F32), ly[inv[1, peer]].astype(F32)).astype(BF16)
        send(s1, r1, 0, peer).start()

    for k in range(1, GROUPS):
        table_copy(k).start()

    quarter = iota((SLOTS * S, 128), 1) // S

    def place_items(into, side, parts, later):
        low = jnp.where(quarter == 0, parts[0], jnp.where(quarter == 1, parts[1], jnp.where(quarter == 2, parts[2], parts[3])))
        late = jnp.where(quarter == later, parts[4], parts[5])
        low, late = low.reshape(SLOTS, S, 128).astype(BF16), late.reshape(SLOTS, S, 128).astype(BF16)
        for slot in range(SLOTS):
            into[2 * slot + side, :, 0:128] = low[slot]
            into[2 * slot + side, :, 128:256] = late[slot]

    sol = sol_ref[...].reshape(SLOTS * S, CELLS).astype(BF16)
    for side in range(2):
        ready(LEAVES[1][side])
        at = high if side else slice(0, 128)
        parts = [dot(pop[d, :, :, at].reshape(SLOTS * S, 128), pick_y[side]) for d in LEAVES[1][side]]
        parts.append(dot(sol[:, at], pick_y[side]))
        place_items(fy, side, parts, 0)
    for side in range(2):
        ready(LEAVES[2][side])
        parts = [dot(pop[d].reshape(SLOTS * S, CELLS), pick[side]) for d in LEAVES[2][side]] + [dot(sol, pick[side])]
        place_items(fz, side, parts, 2)

    left = iota((S, 128), 1) < 64

    @pl.loop(1, PEERS)
    def _(k):
        peer = (me + k) % PEERS
        y_part, z_part = fy[inv[1, peer]], fz[inv[2, peer]]
        s2[peer, :, 0:128] = y_part[:, 0:128]
        s2[peer, :, 128:256] = jnp.where(left, y_part[:, 128:].astype(F32), z_part[:, 128:].astype(F32)).astype(BF16)
        s2[peer, :, 256:384] = z_part[:, 0:128]
        send(s2, r2, 1, peer).start()

    all_of(s1, r1, 0).wait_recv()

    def lines(face, row):
        return jnp.concatenate([r1[owner(slot, face)].astype(F32)[row:row + 1] for slot in range(SLOTS)], axis=0)

    x_lo, x_hi, y_lo, y_hi = lines(0, 0), lines(1, 0), lines(2, 8), lines(3, 8)
    quarter8 = lane8 // S
    back = [pltpu.roll(part, 128 - S, 1) for part in (x_lo, x_hi, y_lo, y_hi)]
    x_lo, x_hi = pltpu.roll(x_lo, S, 1), pltpu.roll(x_hi, S, 1)

    def four_of(one, two, three, zero):
        return jnp.where(quarter8 == 1, one, jnp.where(quarter8 == 2, two, jnp.where(quarter8 == 3, three, zero)))

    y_rows = (jnp.where(quarter8 == 1, x_hi, x_lo), jnp.where(quarter8 == 1, x_lo, x_hi))
    z_rows = (four_of(back[1], back[0], back[3], back[2]), four_of(back[0], back[1], back[2], back[3]))
    for slot in range(SLOTS):
        for side in range(2):
            ey[2 * slot + side] = jnp.broadcast_to(y_rows[side][slot:slot + 1], (16, 128))
            ez[2 * slot + side] = jnp.broadcast_to(z_rows[side][slot:slot + 1], (16, 128))
    row16 = iota((16, 128), 0)

    @pl.loop(1, PEERS)
    def _(k):
        peer = (me + k) % PEERS
        part = fx[inv[0, peer]]
        first = jnp.where(row16 == 6, ey[inv[1, peer]], jnp.where(row16 == 7, ez[inv[2, peer]], part[:, 0:128].astype(F32)))
        s3[peer, :, 0:128] = first.astype(BF16)
        s3[peer, :, 128:512] = part[:, 128:512]
        send(s3, r3, 2, peer).start()

    all_of(s2, r2, 1).wait_recv()
    row32, lane32 = iota((S, 128), 0), iota((S, 128), 1)
    item = lane32 // S

    def shift_rows(plane, down, up):
        return jnp.where(item == down, pltpu.roll(plane, 1, 0), jnp.where(item == up, pltpu.roll(plane, S - 1, 0), plane))

    @pl.loop(0, SLOTS)
    def _(slot):
        for side in range(2):
            down, up = (1, 2) if side == 0 else (2, 1)
            peer = owner(slot, 2 + side)
            gy_ref[slot, side, :, 0:128] = shift_rows(r2[peer, :, 0:128].astype(F32), down, up).astype(BF16)
            gy_ref[slot, side, :, 128:256] = r2[peer, :, 128:256]
            peer = owner(slot, 4 + side)
            plane, late = r2[peer, :, 256:384].astype(F32), r2[peer, :, 128:256].astype(F32)
            turn = 1 if side == 0 else 127
            plane = jnp.where(item == 3, pltpu.roll(plane, turn, 1), shift_rows(plane, down, up))
            gz_ref[slot, side, :, 0:128] = plane.astype(BF16)
            gz_ref[slot, side, :, 128:256] = jnp.where(item == 2, pltpu.roll(late, 128 - turn, 1), late).astype(BF16)

    all_of(s3, r3, 2).wait_recv()

    @pl.loop(0, SLOTS)
    def _(slot):
        halves = []
        for side in range(2):
            part = r3[owner(slot, side)].astype(F32)
            halves.append(jnp.concatenate([part[0:8], part[8:16]], axis=1))
        gx_ref[slot] = jnp.concatenate(halves, axis=0).astype(BF16)
        for side in range(2):
            down, up = (1, 2) if side == 0 else (2, 1)
            ends = ((item == down) & (row32 == 0)) | ((item == up) & (row32 == S - 1))
            edge = r3[owner(slot, 2 + side), :, 0:128].astype(F32)[6:7]
            plane = gy_ref[slot, side, :, 0:128].astype(F32)
            gy_ref[slot, side, :, 0:128] = jnp.where(ends, edge, plane).astype(BF16)
            edge = r3[owner(slot, 4 + side), :, 0:128].astype(F32)[7:8]
            third = jnp.sum(jnp.where(lane32 == row32 + 96, edge, 0.0), axis=1, keepdims=True)
            fourth = jnp.sum(jnp.where(lane32 == row32, edge, 0.0), axis=1, keepdims=True)
            plane, late = gz_ref[slot, side, :, 0:128].astype(F32), gz_ref[slot, side, :, 128:256].astype(F32)
            at3, at4 = (96, 95) if side == 0 else (127, 64)
            gz_ref[slot, side, :, 0:128] = jnp.where(ends, edge, jnp.where(lane32 == at3, third, plane)).astype(BF16)
            gz_ref[slot, side, :, 128:256] = jnp.where(lane32 == at4, fourth, late).astype(BF16)

    all_of(s1, r1, 0).wait_send()
    all_of(s2, r2, 1).wait_send()
    all_of(s3, r3, 2).wait_send()
    for k in range(1, GROUPS):
        table_copy(k).wait()


def exchange(populations, solute, neighbours, redeal_list):
    vmem, hbm = (pl.BlockSpec(memory_space=m) for m in (pltpu.VMEM, pltpu.HBM))
    return pl.pallas_call(
        exchange_kernel,
        out_shape=(
            jax.ShapeDtypeStruct((SLOTS, 16, CELLS), BF16),
            jax.ShapeDtypeStruct((SLOTS, 2, S, 256), BF16),
            jax.ShapeDtypeStruct((SLOTS, 2, S, 256), BF16),
            jax.ShapeDtypeStruct((GROUPS, 1, 128), I32),
        ),
        in_specs=[hbm] * 4,
        out_specs=(vmem, vmem, vmem, vmem),
        scratch_shapes=[
            pltpu.VMEM((19, SLOTS, S, CELLS), BF16),
            pltpu.VMEM((SLOTS, S, CELLS), F32),
            pltpu.VMEM((SLOTS, 16, CELLS), BF16),
            pltpu.VMEM((2 * SLOTS, 16, 512), BF16),
            pltpu.VMEM((2 * SLOTS, S, 256), BF16),
            pltpu.VMEM((2 * SLOTS, S, 256), BF16),
            pltpu.VMEM((2 * SLOTS, 16, 128), BF16),
            pltpu.VMEM((2 * SLOTS, 16, 128), BF16),
            pltpu.VMEM((2 * SLOTS, 16, 128), F32),
            pltpu.VMEM((2 * SLOTS, 16, 128), F32),
            pltpu.VMEM((PEERS, 16, 128), BF16),
            pltpu.VMEM((PEERS, S, 384), BF16),
            pltpu.VMEM((PEERS, 16, 512), BF16),
            pltpu.VMEM((PEERS, 16, 128), BF16),
            pltpu.VMEM((PEERS, S, 384), BF16),
            pltpu.VMEM((PEERS, 16, 512), BF16),
            pltpu.VMEM((1, 128), I32),
            pltpu.VMEM((8, 128), I32),
            pltpu.SMEM((SLOTS, 6), I32),
            pltpu.SMEM((8, 128), I32),
            pltpu.SMEM((3,), I32),
            pltpu.SemaphoreType.DMA((19,)),
            pltpu.SemaphoreType.DMA((4,)),
            pltpu.SemaphoreType.DMA((3,)),
            pltpu.SemaphoreType.DMA((3,)),
            pltpu.SemaphoreType.DMA((GROUPS,)),
            pltpu.SemaphoreType.DMA((GROUPS,)),
        ],
        compiler_params=pltpu.CompilerParams(collective_id=0, has_side_effects=True, vmem_limit_bytes=28 * 2**20),
        cost_estimate=pl.CostEstimate(flops=10**9, bytes_accessed=12 * 10**6, transcendentals=0),
        name="exchange",
    )(*(pltpu.with_memory_space_constraint(a, pltpu.HBM) for a in (populations, solute, neighbours, redeal_list)))


def pull_block(pop, sol, gx, gy, gz, spread, pulled, grads):
    lane = iota((S, CELLS), 1)
    depth = lane % S
    lane128 = iota((S, 128), 1)
    part = lane128 // S
    x_rows = gx[...].astype(F32)
    y_tiles = [[gy[side, :, 128 * t:128 * t + 128].astype(F32) for t in range(2)] for side in range(2)]
    stack = []
    for side in range(2):
        for item in range(6):
            tile = gz[side, :, 0:128] if item < 4 else gz[side, :, 128:256]
            quarter = item if item < 4 else item - 2
            stack.append(jnp.where(part == quarter, tile.astype(F32), 0.0).astype(BF16))
    z_all = dot(jnp.concatenate(stack, axis=0), spread[...])

    def z_ghost(side, item):
        at = (side * 6 + item) * S
        return z_all[at:at + S]

    def y_merge(block, side, item, cz):
        tile = y_tiles[side][item // 4]
        start = (item % 4) * S
        target = 0 if side == 0 else 128 - S
        shift = (target + cz - start) % 128
        if shift:
            tile = pltpu.roll(tile, shift, 1)
        if side == 0:
            return jnp.concatenate([jnp.where(lane128 < S, tile, block[:, 0:128]), block[:, 128:]], axis=1)
        return jnp.concatenate([block[:, :CELLS - 128], jnp.where(lane128 >= 128 - S, tile, block[:, CELLS - 128:])], axis=1)

    def shift_x(block, side, item):
        row = x_rows[side * 8 + item:side * 8 + item + 1]
        if side == 0:
            return jnp.concatenate([row, block[:S - 1]], axis=0)
        return jnp.concatenate([block[1:], row], axis=0)

    for d, (cx, cy, cz) in enumerate(VELOCITY):
        block = pop[d].astype(F32)
        if cx:
            side = 0 if cx == 1 else 1
            block = shift_x(block, side, LEAVES[0][1 - side].index(d))
        shift = (S * cy + cz) % CELLS
        if shift:
            block = pltpu.roll(block, shift, 1)
        if cy:
            side = 0 if cy == 1 else 1
            block = y_merge(block, side, LEAVES[1][1 - side].index(d), cz)
        if cz:
            side = 0 if cz == 1 else 1
            edge = 0 if cz == 1 else S - 1
            block = jnp.where(depth == edge, z_ghost(side, LEAVES[2][1 - side].index(d)), block)
        pulled[d] = block
    here = sol[...]
    below, above = shift_x(here, 0, 5), shift_x(here, 1, 5)
    total = below + above
    grads[1] = above - below
    below = y_merge(pltpu.roll(here, S, 1), 0, 5, 0)
    above = y_merge(pltpu.roll(here, CELLS - S, 1), 1, 5, 0)
    total = total + below + above
    grads[2] = above - below
    below = jnp.where(depth == 0, z_ghost(0, 5), pltpu.roll(here, 1, 1))
    above = jnp.where(depth == S - 1, z_ghost(1, 5), pltpu.roll(here, CELLS - 1, 1))
    grads[3] = above - below
    grads[0] = total + below + above - 6.0 * here


def update(pulled, grads, sol, solid, rows, lanes, put):
    f = [pulled[d, rows, lanes] for d in range(19)]
    pair_sum = [f[i] + f[i + 1] for i in range(1, 19, 2)]
    pair_dif = [f[i] - f[i + 1] for i in range(1, 19, 2)]
    straight = pair_sum[0] + pair_sum[1] + pair_sum[2]
    slanted = (pair_sum[3] + pair_sum[4]) + (pair_sum[5] + pair_sum[6]) + (pair_sum[7] + pair_sum[8])
    density = f[0] * (1.0 / 3.0) + straight * (1.0 / 18.0) + slanted * (1.0 / 36.0)
    dif = pair_dif
    over = 1.0 / density
    over36 = over * (1.0 / 36.0)
    ux = (2.0 * dif[0] + ((dif[3] + dif[4]) + (dif[5] + dif[6]))) * over36
    uy = (2.0 * dif[1] + ((dif[3] - dif[4]) + (dif[7] + dif[8]))) * over36
    uz = (2.0 * dif[2] + ((dif[5] - dif[6]) + (dif[7] - dif[8]))) * over36
    amount = solid[rows, lanes]
    keep = 1.0 - amount
    if put is not None:
        scale = (1.0 / relax_time) * keep * density
        base = scale - (1.5 * scale) * (ux * ux + uy * uy + uz * uz)
        curve, slope = 4.5 * scale, 3.0 * scale
        rest = (1.0 / relax_time - 1.0) * keep
        even_part, odd_part = 0.5 * (amount - rest), 0.5 * (amount + rest)
        put(0, base + (amount - rest) * f[0])
        along_all = (ux, uy, uz, ux + uy, ux - uy, ux + uz, ux - uz, uy + uz, uy - uz)
        for pair in range(9):
            along = along_all[pair]
            even = base + (curve * along) * along + even_part * pair_sum[pair]
            odd = slope * along - odd_part * pair_dif[pair]
            put(2 * pair + 1, even + odd)
            put(2 * pair + 2, even - odd)
    mixed = (sol[rows, lanes] + diffusivity * grads[0, rows, lanes]
             - 0.5 * (ux * grads[1, rows, lanes] + uy * grads[2, rows, lanes] + uz * grads[3, rows, lanes]))
    reaction = rate_const * amount * keep * (saturation - mixed)
    return mixed + reaction, amount - reaction


def make_spread(spread):
    deep, lane = iota((128, CELLS), 0), iota((128, CELLS), 1)
    spread[...] = jnp.where(deep % S == lane // S, 1.0, 0.0).astype(BF16)


def chunks(body):
    for row in range(0, S, 16):
        for lane in range(0, CELLS, 128):
            body(slice(row, row + 16), slice(lane, lane + 128))


def front_kernel(front, redeal, pop, sol, solid, gx, gy, gz, send1, send2, send3, ones_ref, spread, pulled, grads):
    step = pl.program_id(0)

    @pl.when(step == 0)
    def _():
        make_spread(spread)

    ones_ref[...] = jnp.ones(ones_ref.shape, BF16)
    pull_block(pop.at[0], sol.at[0], gx.at[0], gy.at[0], gz.at[0], spread, pulled, grads)
    for target, ref in enumerate((send1, send2, send3)):
        @pl.when(step == target)
        def _():
            def one(rows, lanes):
                ref[0, rows, lanes], ref[1, rows, lanes] = update(pulled, grads, sol.at[0], solid.at[0], rows, lanes, None)

            chunks(one)


def rest_kernel(front, pop, sol, solid, gx, gy, gz, old_ref, new_pop, new_sol, new_solid, spread, pulled, grads):
    @pl.when(pl.program_id(0) == 0)
    def _():
        make_spread(spread)

    pull_block(pop.at[0], sol.at[0], gx.at[0], gy.at[0], gz.at[0], spread, pulled, grads)

    def one(rows, lanes):
        def put(direction, value):
            new_pop[0, direction, rows, lanes] = value.astype(BF16)

        new_sol[0, rows, lanes], new_solid[0, rows, lanes] = update(
            pulled, grads, sol.at[0], solid.at[0], rows, lanes, put)

    chunks(one)


def front_slot(step, front, redeal):
    group = front[0] // SLOTS % GROUPS
    slot = front[0] % SLOTS
    for entry in range(1, 3):
        ahead = (redeal[entry] // SLOTS % GROUPS - group + GROUPS) % GROUPS
        slot = jnp.where(ahead == step + 1, front[entry] % SLOTS, slot)
    return slot


def rest_slot(step, front):
    a, b, c = (front[entry] % SLOTS for entry in range(3))
    low, high = jnp.minimum(a, b), jnp.maximum(a, b)
    mid, high = jnp.minimum(high, c), jnp.maximum(high, c)
    low, mid = jnp.minimum(low, mid), jnp.maximum(low, mid)
    slot = step
    for taken in (low, mid, high):
        slot = slot + jnp.where(slot >= taken, 1, 0)
    return slot


def block_specs(pick):
    shapes = ((1, 19, S, CELLS), (1, S, CELLS), (1, S, CELLS), (1, 16, CELLS), (1, 2, S, 256), (1, 2, S, 256))
    return [pl.BlockSpec(shape, lambda step, *refs, n=len(shape): (pick(step, *refs),) + (0,) * (n - 1)) for shape in shapes]


WORK = [
    pltpu.VMEM((128, CELLS), BF16),
    pltpu.VMEM((19, S, CELLS), F32),
    pltpu.VMEM((4, S, CELLS), F32),
]


def front_update(front, redeal, populations, solute, solid_fraction, gx, gy, gz):
    specs = block_specs(front_slot)
    sent = pl.BlockSpec((2, S, CELLS), lambda *_: (0, 0, 0))
    return pl.pallas_call(
        front_kernel,
        out_shape=tuple(jax.ShapeDtypeStruct((2, S, CELLS), F32) for _ in range(3))
        + (jax.ShapeDtypeStruct(populations.shape, BF16),),
        grid_spec=pltpu.PrefetchScalarGridSpec(
            num_scalar_prefetch=2, grid=(3,), in_specs=specs, out_specs=(sent, sent, sent, specs[0]),
            scratch_shapes=WORK),
        compiler_params=pltpu.CompilerParams(vmem_limit_bytes=20 * 2**20),
        cost_estimate=pl.CostEstimate(flops=2 * 10**7, bytes_accessed=9 * 10**6, transcendentals=0),
        name="front",
    )(front, redeal, populations, solute, solid_fraction, gx, gy, gz)


def rest_update(front, populations, solute, solid_fraction, gx, gy, gz, new_populations):
    specs = block_specs(rest_slot)
    return pl.pallas_call(
        rest_kernel,
        out_shape=(
            jax.ShapeDtypeStruct(populations.shape, BF16),
            jax.ShapeDtypeStruct(solute.shape, F32),
            jax.ShapeDtypeStruct(solute.shape, F32),
        ),
        grid_spec=pltpu.PrefetchScalarGridSpec(
            num_scalar_prefetch=1, grid=(5,), in_specs=specs + [pl.BlockSpec(memory_space=pl.ANY)],
            out_specs=tuple(specs[:3]), scratch_shapes=WORK),
        input_output_aliases={7: 0},
        compiler_params=pltpu.CompilerParams(vmem_limit_bytes=20 * 2**20),
        cost_estimate=pl.CostEstimate(flops=10**8, bytes_accessed=16 * 10**6, transcendentals=0),
        name="rest",
    )(front, populations, solute, solid_fraction, gx, gy, gz, new_populations)


def place_kernel(front, table, got1, got2, got3, old_sol, old_solid, new_sol, new_solid, sems):
    group = front[0] // SLOTS % GROUPS
    copies = []
    for k, got in enumerate((got1, got2, got3)):
        source = (group + GROUPS - 1 - k) % GROUPS
        slot = table[source, 0, 0] % SLOTS
        for entry in range(1, 3):
            place = table[source, 0, entry]
            slot = jnp.where(place // SLOTS % GROUPS == group, place % SLOTS, slot)
        copies.append(pltpu.make_async_copy(got.at[0], new_sol.at[slot], sems.at[k, 0]))
        copies.append(pltpu.make_async_copy(got.at[1], new_solid.at[slot], sems.at[k, 1]))
    for copy in copies:
        copy.start()
    for copy in copies:
        copy.wait()


def place_front(front, table, received, new_solute, new_solid):
    smem, vmem, anywhere = (pl.BlockSpec(memory_space=m) for m in (pltpu.SMEM, pltpu.VMEM, pl.ANY))
    return pl.pallas_call(
        place_kernel,
        out_shape=tuple(jax.ShapeDtypeStruct(new_solute.shape, F32) for _ in range(2)),
        in_specs=[smem, smem] + [vmem] * 3 + [anywhere] * 2,
        out_specs=(anywhere, anywhere),
        input_output_aliases={5: 0, 6: 1},
        scratch_shapes=[pltpu.SemaphoreType.DMA((3, 2))],
        compiler_params=pltpu.CompilerParams(vmem_limit_bytes=2 * 2**20),
        cost_estimate=pl.CostEstimate(flops=0, bytes_accessed=2 * 10**6, transcendentals=0),
        name="place",
    )(front, table, *received, new_solute, new_solid)


def body(populations, solute, solid_fraction, neighbours, front_list, redeal_list):
    gx, gy, gz, table = exchange(populations, solute, neighbours, redeal_list)
    *sent, new_populations = front_update(front_list, redeal_list, populations, solute, solid_fraction, gx, gy, gz)
    received = [
        lax.ppermute(sent[k], "grp", [(g, (g + k + 1) % GROUPS) for g in range(GROUPS)]) for k in range(GROUPS - 1)
    ]
    new_populations, new_solute, new_solid = rest_update(
        front_list, populations, solute, solid_fraction, gx, gy, gz, new_populations)
    new_solute, new_solid = place_front(front_list, table, received, new_solute, new_solid)
    return new_populations, new_solute, new_solid


def solution(mesh):
    deal = ("blk", "grp")
    return jax.shard_map(
        body,
        mesh=mesh,
        in_specs=(P(deal, None, None, None), P(deal, None, None), P(deal, None, None), P(deal, None), P(deal), P(deal)),
        out_specs=(P(deal, None, None, None), P(deal, None, None), P(deal, None, None)),
        check_vma=False,
    )
```

time: 70.1 us -> 55.6 us (0.79)
  Pallas kernels: 57.3 us -> 47.8 us
  local copies, waits for them, and re-layouts: 5.35 us -> 1.24 us
  other arithmetic: 0.8 us -> 0 us
    pallas_call x1, Pallas kernels: 34.9 us -> 29.7 us  [exchange(): pl.pallas_call(exchange_kernel, out_shape=(jax.ShapeDtypeStruct((SLOTS, 1...]
    unnamed x18 -> x10, local copies, waits for them, and re-layouts: 4.68 us -> 1.24 us
    pallas_call x1, Pallas kernels: 3.57 us -> 1.54 us  [place_front(): pl.pallas_call(place_kernel, out_shape=tuple((jax.ShapeDtypeStruct(new_so...]
    pallas_call x1, Pallas kernels: 6.64 us -> 5.37 us  [front_update(): pl.pallas_call(front_kernel, out_shape=tuple((jax.ShapeDtypeStruct((2, S,...]
    pallas_call x1, Pallas kernels: 12.2 us -> 11.3 us  [rest_update(): pl.pallas_call(rest_kernel, out_shape=(jax.ShapeDtypeStruct(populations.s...]
  transfers between devices with their start and end apart: 3 -> 3, of which waited for: 0 -> 0; matrix products, arithmetic and copies ran while one was open for 1% -> 0% of each run, Pallas kernels for 17% -> 20%
where the time goes in v2:
time: 55.6 us; the launch traced here: 55.5 us
  Pallas kernels  47.8 us (86%)
  starting transfers between devices  5.68 us (10%)
  local copies, waits for them, and re-layouts  1.24 us (2%)
  between operations  0.72 us (1%)
    pallas_call x1, Pallas kernels, exchange(): pl.pallas_call(exchange_kernel, out_shape=(jax.ShapeDtypeStruct((SLOTS, 1...  29.7 us
    pallas_call x1, Pallas kernels, rest_update(): pl.pallas_call(rest_kernel, out_shape=(jax.ShapeDtypeStruct(populations.s...  11.3 us
    ppermute x3, starting transfers between devices, body(): lax.ppermute(sent[k], 'grp', [(g, (g + k + 1) % GROUPS) for g in range(GR...  5.68 us
    pallas_call x1, Pallas kernels, front_update(): pl.pallas_call(front_kernel, out_shape=tuple((jax.ShapeDtypeStruct((2, S,...  5.37 us
    pallas_call x1, Pallas kernels, place_front(): pl.pallas_call(place_kernel, out_shape=tuple((jax.ShapeDtypeStruct(new_so...  1.54 us
    unnamed x10, local copies, waits for them, and re-layouts  1.24 us
  transfers between devices with their start and end apart: 3, of which 0 were waited for; matrix products, arithmetic and copies ran while one was open for 0% of the time, Pallas kernels for 20%

profile of v2, /device:TPU:1, one launch (start us, length us, event | category | flops | bytes accessed | tf_op | source)
XLA Modules:
  0.0 55.5 jit_solution(1932562253392542277)
XLA Ops:
  0.6 0.0 copy-start.1
  0.6 0.0 copy-start
  0.7 0.0 copy-start.4
  0.7 0.0 copy-start.3
  0.7 29.7 %exchange.1 = (bf16[8,16,1024]{2,1,0:T(8,128)(2,1)S(1)}, bf16[8,2,32,256]{3,2,1,0:T(8,128)(2,1)S(1)}, bf16[8,2,32,256]{3,2,1,0:T(8,128)(2,1)S(1)}, s32[4,1,128]{2,1,0:T(1,128)S(1)}) custom-call(bf16[8,19,32,1024]{3,2,1,0:T(8,128)(2,1)} %pop.3, f32[8,32,1024]{2,1,0:T(8,128)} %sol.3, s32[8,6]{1,0:T(8,128)} %nbr_hbm.1, s32[3]{0:T(128)} %redeal.1), custom_call_target="tpu_custom_call" | custom-call | flops 1000000000 | bytes 12000000 | tf_op jit(solution)/shard_map/exchange/pallas_call | solution.py:291
  30.3 0.0 copy-done.1
  30.4 0.0 copy-done
  30.4 0.0 copy-done.4
  30.4 0.0 copy-done.3
  30.4 0.0 copy-start.2
  30.4 1.2 %copy-done.2 = f32[8,32,1024]{2,1,0:T(8,128)S(1)} copy-done((f32[8,32,1024]{2,1,0:T(8,128)S(1)}, f32[8,32,1024]{2,1,0:T(8,128)}, u32[]{:S(2)}) %copy-start.2) | copy-done | bytes 1048600
  31.6 5.4 %front.4 = (f32[2,32,1024]{2,1,0:T(8,128)S(1)}, f32[2,32,1024]{2,1,0:T(8,128)S(1)}, f32[2,32,1024]{2,1,0:T(8,128)S(1)}, bf16[8,19,32,1024]{3,2,1,0:T(8,128)(2,1)}) custom-call(s32[3]{0:T(128)S(1)} %copy-done.3, s32[3]{0:T(128)S(1)} %copy-done.4, bf16[8,19,32,1024]{3,2,1,0:T(8,128)(2,1)S(1)} %copy-done, f32[8,32,1024]{2,1,0:T(8,128)S(1)} %copy-done.1, ...), custom_call_target="tpu_custom_call" | custom-call | flops 20000000 | bytes 9000000 | tf_op jit(solution)/shard_map/front/pallas_call | solution.py:518
  37.0 1.6 %collective-permute-start = (f32[2,32,1024]{2,1,0:T(8,128)S(1)}, f32[2,32,1024]{2,1,0:T(8,128)S(1)}, u32[]{:S(2)}, u32[]{:S(2)}) collective-permute-start(f32[2,32,1024]{2,1,0:T(8,128)S(1)} %get-tuple-element.22), channel_id=1, source_target_pairs={{0,1},{1,2},{2,3},{3,0},{4,5},{5,6},{6,7},{7,4},{8,9},{9,10},{10,1... | collective-permute-start | bytes 786440 | tf_op jit(solution)/shard_map/ppermute | solution.py:586
  38.6 3.3 %collective-permute-start.1 = (f32[2,32,1024]{2,1,0:T(8,128)S(1)}, f32[2,32,1024]{2,1,0:T(8,128)S(1)}, u32[]{:S(2)}, u32[]{:S(2)}) collective-permute-start(f32[2,32,1024]{2,1,0:T(8,128)S(1)} %get-tuple-element.23), channel_id=1, source_target_pairs={{0,2},{1,3},{2,0},{3,1},{4,6},{5,7},{6,4},{7,5},{8,10},{9,11},{10,... | collective-permute-start | bytes 786440 | tf_op jit(solution)/shard_map/ppermute | solution.py:586
  41.9 0.7 %collective-permute-start.2 = (f32[2,32,1024]{2,1,0:T(8,128)S(1)}, f32[2,32,1024]{2,1,0:T(8,128)S(1)}, u32[]{:S(2)}, u32[]{:S(2)}) collective-permute-start(f32[2,32,1024]{2,1,0:T(8,128)S(1)} %get-tuple-element.24), channel_id=1, source_target_pairs={{0,3},{1,0},{2,1},{3,2},{4,7},{5,4},{6,5},{7,6},{8,11},{9,8},{10,9... | collective-permute-start | bytes 786440 | tf_op jit(solution)/shard_map/ppermute | solution.py:586
  42.7 11.3 %rest.1 = (bf16[8,19,32,1024]{3,2,1,0:T(8,128)(2,1)}, f32[8,32,1024]{2,1,0:T(8,128)}, f32[8,32,1024]{2,1,0:T(8,128)}) custom-call(s32[3]{0:T(128)S(1)} %copy-done.3, bf16[8,19,32,1024]{3,2,1,0:T(8,128)(2,1)S(1)} %copy-done, f32[8,32,1024]{2,1,0:T(8,128)S(1)} %copy-done.1, f32[8,32,1024]{2,1,0:T(8,128)S(1)} %copy-done.2, ...), custom_call_target="tpu_custom_call", output_to_operand_aliasing={{0}: (7, {})} | custom-call | flops 100000000 | bytes 16000000 | tf_op jit(solution)/shard_map/rest/pallas_call | solution.py:533
  53.9 0.0 collective-permute-done.got1
  53.9 0.0 collective-permute-done.1.got2
  53.9 0.0 collective-permute-done.2.got3
  53.9 1.5 %place.1 = (f32[8,32,1024]{2,1,0:T(8,128)}, f32[8,32,1024]{2,1,0:T(8,128)}) custom-call(s32[3]{0:T(128)S(1)} %copy-done.3, s32[4,1,128]{2,1,0:T(1,128)S(1)} %get-tuple-element.21.table, f32[2,32,1024]{2,1,0:T(8,128)S(1)} %collective-permute-done.got1, f32[2,32,1024]{2,1,0:T(8,128)S(1)} %collective-permute-done.1.got2, ...), custom_call_target="tpu_custom_call", output_to_operand_aliasing={{0}: (5, {}), {1}: (6, {})} | custom-call | bytes 2000000 | tf_op jit(solution)/shard_map/place/pallas_call | solution.py:569
Async XLA Ops:
  0.6 29.7 %copy-start.1 = (f32[8,32,1024]{2,1,0:T(8,128)S(1)}, f32[8,32,1024]{2,1,0:T(8,128)}, u32[]{:S(2)}) copy-start(f32[8,32,1024]{2,1,0:T(8,128)} %sol.3) | copy-start | bytes 3145732
  0.6 29.7 %copy-start = (bf16[8,19,32,1024]{3,2,1,0:T(8,128)(2,1)S(1)}, bf16[8,19,32,1024]{3,2,1,0:T(8,128)(2,1)}, u32[]{:S(2)}) copy-start(bf16[8,19,32,1024]{3,2,1,0:T(8,128)(2,1)} %pop.3) | copy-start | bytes 29884420
  0.7 29.7 %copy-start.4 = (s32[3]{0:T(128)S(1)}, s32[3]{0:T(128)}, u32[]{:S(2)}) copy-start(s32[3]{0:T(128)} %redeal.1) | copy-start | bytes 40
  0.7 29.7 %copy-start.3 = (s32[3]{0:T(128)S(1)}, s32[3]{0:T(128)}, u32[]{:S(2)}) copy-start(s32[3]{0:T(128)} %front.7) | copy-start | bytes 40
  30.4 1.2 %copy-start.2 = (f32[8,32,1024]{2,1,0:T(8,128)S(1)}, f32[8,32,1024]{2,1,0:T(8,128)}, u32[]{:S(2)}) copy-start(f32[8,32,1024]{2,1,0:T(8,128)} %solid.3) | copy-start | bytes 3145732
  37.0 17.0 %collective-permute-start = (f32[2,32,1024]{2,1,0:T(8,128)S(1)}, f32[2,32,1024]{2,1,0:T(8,128)S(1)}, u32[]{:S(2)}, u32[]{:S(2)}) collective-permute-start(f32[2,32,1024]{2,1,0:T(8,128)S(1)} %get-tuple-element.22), channel_id=1, source_target_pairs={{0,1},{1,2},{2,3},{3,0},{4,5},{5,6},{6,7},{7,4},{8,9},{9,10},{10,1... | collective-permute-start | bytes 786440 | tf_op jit(solution)/shard_map/ppermute | solution.py:586
  38.6 15.3 %collective-permute-start.1 = (f32[2,32,1024]{2,1,0:T(8,128)S(1)}, f32[2,32,1024]{2,1,0:T(8,128)S(1)}, u32[]{:S(2)}, u32[]{:S(2)}) collective-permute-start(f32[2,32,1024]{2,1,0:T(8,128)S(1)} %get-tuple-element.23), channel_id=1, source_target_pairs={{0,2},{1,3},{2,0},{3,1},{4,6},{5,7},{6,4},{7,5},{8,10},{9,11},{10,... | collective-permute-start | bytes 786440 | tf_op jit(solution)/shard_map/ppermute | solution.py:586
  41.9 12.0 %collective-permute-start.2 = (f32[2,32,1024]{2,1,0:T(8,128)S(1)}, f32[2,32,1024]{2,1,0:T(8,128)S(1)}, u32[]{:S(2)}, u32[]{:S(2)}) collective-permute-start(f32[2,32,1024]{2,1,0:T(8,128)S(1)} %get-tuple-element.24), channel_id=1, source_target_pairs={{0,3},{1,0},{2,1},{3,2},{4,7},{5,4},{6,5},{7,6},{8,11},{9,8},{10,9... | collective-permute-start | bytes 786440 | tf_op jit(solution)/shard_map/ppermute | solution.py:586

commit v3 on v2

v3 whole, which is shorter than its diff:
```python
import jax
import jax.numpy as jnp
from jax import lax
from jax.experimental import pallas as pl
from jax.experimental.pallas import tpu as pltpu
from jax.sharding import PartitionSpec as P

VELOCITY = (
    (0, 0, 0), (1, 0, 0), (-1, 0, 0), (0, 1, 0), (0, -1, 0), (0, 0, 1), (0, 0, -1),
    (1, 1, 0), (-1, -1, 0), (1, -1, 0), (-1, 1, 0), (1, 0, 1), (-1, 0, -1), (1, 0, -1),
    (-1, 0, 1), (0, 1, 1), (0, -1, -1), (0, 1, -1), (0, -1, 1),
)
LEAVES = (
    ((2, 8, 10, 12, 14), (1, 7, 9, 11, 13)),
    ((4, 8, 9, 16, 18), (3, 7, 10, 15, 17)),
    ((6, 12, 13, 16, 17), (5, 11, 14, 15, 18)),
)
FETCH = (2, 8, 10, 12, 14, 1, 7, 9, 11, 13, 15, 16, 17, 18, 3, 4, 6, 5, 0)
SLOTS = 8
S = 32
CELLS = S * S
PEERS = 32
GROUPS = 4
TURNS = ((0, 1), (0, -1), (1, 0), (-1, 0), (1, 1), (-1, -1), (1, -1), (-1, 1))
WIDE = 256
F32, BF16, I32 = jnp.float32, jnp.bfloat16, jnp.int32
relax_time = 0.8
diffusivity = 0.1
rate_const = 0.5
saturation = 1.0


def iota(shape, dim):
    return lax.broadcasted_iota(I32, shape, dim)


def lane_shift(direction):
    return (S * VELOCITY[direction][1] + VELOCITY[direction][2]) % CELLS


def dot(a, b):
    return jnp.dot(a, b, preferred_element_type=F32)


def react(mixed, amount):
    reaction = rate_const * amount * (1.0 - amount) * (saturation - mixed)
    return mixed + reaction, amount - reaction


def front_slot(step, front, redeal):
    group = front[0] // SLOTS % GROUPS
    slot = front[0] % SLOTS
    for entry in range(1, 3):
        ahead = (redeal[entry] // SLOTS % GROUPS - group + GROUPS) % GROUPS
        slot = jnp.where(ahead == step + 1, front[entry] % SLOTS, slot)
    return slot


def rest_slot(step, front):
    a, b, c = (front[entry] % SLOTS for entry in range(3))
    low, high = jnp.minimum(a, b), jnp.maximum(a, b)
    mid, high = jnp.minimum(high, c), jnp.maximum(high, c)
    low, mid = jnp.minimum(low, mid), jnp.maximum(low, mid)
    slot = step
    for taken in (low, mid, high):
        slot = slot + jnp.where(slot >= taken, 1, 0)
    return slot


def place_slot(step, front, table):
    group = front[0] // SLOTS % GROUPS
    slot = table[step, 0, 0] % SLOTS
    for entry in range(1, 3):
        place = table[step, 0, entry]
        slot = jnp.where(place // SLOTS % GROUPS == group, place % SLOTS, slot)
    return slot


def exchange_kernel(pop_hbm, sol_hbm, solid_hbm, nbr_hbm, front_hbm, redeal_hbm,
                    moved, flow, fresh, got_mixed, got_solid, table_ref,
                    sol_ref, solid_ref, xr, fx, fy, fz, lx, ly, ey, ez, s1, s2, s3, r1, r2, r3, mine, inv_vmem,
                    keep, spread, ghost, grads, out_mixed, out_solid,
                    nbr, inv, front, redeal, fetch_sem, small_sem, send_sem, recv_sem, grp_send, grp_recv):
    me = lax.axis_index("blk")
    grp = lax.axis_index("grp")

    def fetch(direction):
        return pltpu.make_async_copy(pop_hbm.at[:, direction], moved.at[:, direction], fetch_sem.at[direction])

    nbr_copy = pltpu.make_async_copy(nbr_hbm, nbr, small_sem.at[0])
    redeal_copy = pltpu.make_async_copy(redeal_hbm, redeal, small_sem.at[1])
    inv_copy = pltpu.make_async_copy(inv_vmem, inv, small_sem.at[2])
    sol_copy = pltpu.make_async_copy(sol_hbm, sol_ref, small_sem.at[3])
    front_copy = pltpu.make_async_copy(front_hbm, front, small_sem.at[4])
    solid_copy = pltpu.make_async_copy(solid_hbm, solid_ref, small_sem.at[5])
    nbr_copy.start()
    redeal_copy.start()
    front_copy.start()
    sol_copy.start()
    for direction in FETCH:
        fetch(direction).start()

    solid_copy.start()
    barrier = pltpu.get_barrier_semaphore()

    @pl.loop(1, PEERS)
    def _(k):
        pl.semaphore_signal(barrier, inc=1, device_id={"blk": (me + k) % PEERS}, device_id_type=pl.DeviceIdType.MESH)

    for k in range(1, GROUPS):
        pl.semaphore_signal(barrier, inc=1, device_id={"grp": (grp + k) % GROUPS}, device_id_type=pl.DeviceIdType.MESH)

    deep, lane = iota((CELLS, 128), 0), iota((CELLS, 128), 1) % S
    pick = [jnp.where(deep == lane * S + z, 1.0, 0.0).astype(BF16) for z in (0, S - 1)]
    wide, lane = iota((128, 128), 0), iota((128, 128), 1) % S
    pick_y = [jnp.where(wide == lane + first, 1.0, 0.0).astype(BF16) for first in (0, 128 - S)]

    nbr_copy.wait()
    redeal_copy.wait()
    front_copy.wait()

    def owner(slot, face):
        return nbr[slot, face] // (SLOTS * GROUPS)

    row8, lane8 = iota((8, 128), 0), iota((8, 128), 1)
    found = jnp.zeros((8, 128), I32)
    for axis in range(3):
        hit = jnp.zeros((8, 128), I32)
        for slot in range(SLOTS):
            for side in range(2):
                hit = jnp.where(lane8 == owner(slot, 2 * axis + side), 2 * slot + side, hit)
        found = jnp.where(row8 == axis, hit, found)
    inv_vmem[...] = found
    inv_copy.start()
    lane1 = iota((1, 128), 1)
    mine[...] = jnp.where(lane1 == 0, redeal[0], jnp.where(lane1 == 1, redeal[1], redeal[2]))
    sol_copy.wait()

    fetched = set()

    def ready(directions):
        for direction in directions:
            if direction not in fetched:
                fetched.add(direction)
                fetch(direction).wait()

    ready(LEAVES[0][0] + LEAVES[0][1])

    @pl.loop(0, SLOTS)
    def _(slot):
        faces = []
        for side in range(2):
            at, row = (16, 15) if side else (0, 0)
            rows = [moved[slot, d, at:at + 16, :].astype(F32)[row:row + 1] for d in LEAVES[0][side]]
            rows.append(sol_ref[slot, at + row:at + row + 1, :])
            rows.append(jnp.zeros((2, CELLS), F32))
            rows = jnp.concatenate(rows, axis=0)
            faces.append(rows)
        xr[slot] = jnp.concatenate(faces, axis=0).astype(BF16)

    faces = xr[...].reshape(SLOTS * 16, CELLS)
    z_low, z_top = dot(faces, pick[0]), dot(faces, pick[1])
    y_low, y_top = dot(faces[:, 0:128], pick_y[0]), dot(faces[:, CELLS - 128:], pick_y[1])
    quarter1 = lane1 // S
    ready((15, 16, 17, 18))
    high = slice(CELLS - 128, CELLS)
    lane16 = iota((16, 128), 1)

    def across(d, at, z):
        one = jnp.where(lane16 == z, 1.0, 0.0).astype(BF16)
        tile = moved[:, d, :, at].reshape(SLOTS * S, 128)
        return lax.dot_general(one, tile, (((1,), (1,)), ((), ())), preferred_element_type=F32)

    y_lines = ((across(16, slice(0, 128), 0), across(18, slice(0, 128), S - 1)),
               (across(15, high, 127), across(17, high, 128 - S)))
    for slot in range(SLOTS):
        for side in range(2):
            row = slot * 16 + side * 8
            four = (y_top, y_low, z_top, z_low) if side else (y_low, y_top, z_low, z_top)
            four = [part[row + 1 + i:row + 2 + i] for i, part in enumerate(four)]
            line = jnp.where(quarter1 == 0, four[0], jnp.where(quarter1 == 1, four[1], jnp.where(quarter1 == 2, four[2], four[3])))
            lx[2 * slot + side] = jnp.broadcast_to(line, (16, 128)).astype(BF16)
            tiles = [part[:, 128 * (slot // 4):128 * (slot // 4) + 128] for part in y_lines[side]]
            shift = (128 - S * (slot % 4)) % 128
            if shift:
                tiles[0] = pltpu.roll(tiles[0], shift, 1)
            shift = (shift + S) % 128
            if shift:
                tiles[1] = pltpu.roll(tiles[1], shift, 1)
            ly[2 * slot + side] = jnp.where(lane16 < S, tiles[0], tiles[1]).astype(BF16)

    inv_copy.wait()
    pl.semaphore_wait(barrier, PEERS - 1 + GROUPS - 1)

    def send(src, dst, which, peer):
        return pltpu.make_async_remote_copy(
            src_ref=src.at[peer], dst_ref=dst.at[me], send_sem=send_sem.at[which], recv_sem=recv_sem.at[which],
            device_id={"blk": peer}, device_id_type=pl.DeviceIdType.MESH)

    def all_of(src, dst, which):
        return pltpu.make_async_remote_copy(
            src_ref=src.at[pl.ds(0, PEERS - 1)], dst_ref=dst.at[pl.ds(0, PEERS - 1)], send_sem=send_sem.at[which],
            recv_sem=recv_sem.at[which], device_id={"blk": (me + 1) % PEERS}, device_id_type=pl.DeviceIdType.MESH)

    def grp_copy(src, dst, which, k):
        return pltpu.make_async_remote_copy(
            src_ref=src, dst_ref=dst, send_sem=grp_send.at[which, k], recv_sem=grp_recv.at[which, k],
            device_id={"grp": (grp + k) % GROUPS}, device_id_type=pl.DeviceIdType.MESH)

    def table_copy(k):
        return grp_copy(mine, table_ref.at[k - 1], 0, k)

    def solid_out(k):
        return grp_copy(out_solid.at[k - 1], got_solid.at[k - 1], 1, k)

    def mixed_out(k):
        return grp_copy(out_mixed.at[k - 1], got_mixed.at[k - 1], 2, k)

    upper8 = iota((16, 128), 0) < 8

    @pl.loop(1, PEERS)
    def _(k):
        peer = (me + k) % PEERS
        s1[peer] = jnp.where(upper8, lx[inv[0, peer]].astype(F32), ly[inv[1, peer]].astype(F32)).astype(BF16)
        send(s1, r1, 0, peer).start()

    for k in range(1, GROUPS):
        table_copy(k).start()

    quarter = iota((SLOTS * S, 128), 1) // S

    def place_items(into, side, parts, later):
        low = jnp.where(quarter == 0, parts[0], jnp.where(quarter == 1, parts[1], jnp.where(quarter == 2, parts[2], parts[3])))
        late = jnp.where(quarter == later, parts[4], parts[5])
        low, late = low.reshape(SLOTS, S, 128).astype(BF16), late.reshape(SLOTS, S, 128).astype(BF16)
        for slot in range(SLOTS):
            into[2 * slot + side, :, 0:128] = low[slot]
            into[2 * slot + side, :, 128:256] = late[slot]

    sol = sol_ref[...].reshape(SLOTS * S, CELLS).astype(BF16)
    for side in range(2):
        ready(LEAVES[1][side])
        at = high if side else slice(0, 128)
        parts = [dot(moved[:, d, :, at].reshape(SLOTS * S, 128), pick_y[side]) for d in LEAVES[1][side]]
        parts.append(dot(sol[:, at], pick_y[side]))
        place_items(fy, side, parts, 0)
    for side in range(2):
        ready(LEAVES[2][side])
        parts = [dot(moved[:, d].reshape(SLOTS * S, CELLS), pick[side]) for d in LEAVES[2][side]] + [dot(sol, pick[side])]
        place_items(fz, side, parts, 2)

    left = iota((S, 128), 1) < 64

    @pl.loop(1, PEERS)
    def _(k):
        peer = (me + k) % PEERS
        y_part, z_part = fy[inv[1, peer]], fz[inv[2, peer]]
        s2[peer, :, 0:128] = y_part[:, 0:128]
        s2[peer, :, 128:256] = jnp.where(left, y_part[:, 128:].astype(F32), z_part[:, 128:].astype(F32)).astype(BF16)
        s2[peer, :, 256:384] = z_part[:, 0:128]
        send(s2, r2, 1, peer).start()

    row8w, lane8w = iota((8, CELLS), 0), iota((8, CELLS), 1)
    for i, (cy, cz) in enumerate(TURNS):
        hold = lane8w >= 0
        if cy:
            hold = hold & ((lane8w >= S) if cy == 1 else (lane8w < CELLS - S))
        if cz:
            hold = hold & (lane8w % S != (0 if cz == 1 else S - 1))
        keep[i] = jnp.where(hold, 1.0, 0.0)

    @pl.loop(0, SLOTS)
    def _(slot):
        for side in range(2):
            rows = xr[slot, 8 * side:8 * side + 8, :].astype(F32)
            turned = rows
            for i, d in enumerate(LEAVES[0][side]):
                shift = lane_shift(d)
                if shift:
                    turned = jnp.where(row8w == i, pltpu.roll(rows, shift, 1) * keep[TURNS.index(VELOCITY[d][1:])], turned)
            fx[2 * slot + side] = jnp.concatenate([turned[:, :512], turned[:, 512:]], axis=0).astype(BF16)

    all_of(s1, r1, 0).wait_recv()

    def lines(face, row):
        return jnp.concatenate([r1[owner(slot, face)].astype(F32)[row:row + 1] for slot in range(SLOTS)], axis=0)

    x_lo, x_hi, y_lo, y_hi = lines(0, 0), lines(1, 0), lines(2, 8), lines(3, 8)
    quarter8 = lane8 // S
    back = [pltpu.roll(part, 128 - S, 1) for part in (x_lo, x_hi, y_lo, y_hi)]
    x_lo, x_hi = pltpu.roll(x_lo, S, 1), pltpu.roll(x_hi, S, 1)

    def four_of(one, two, three, zero):
        return jnp.where(quarter8 == 1, one, jnp.where(quarter8 == 2, two, jnp.where(quarter8 == 3, three, zero)))

    y_rows = (jnp.where(quarter8 == 1, x_hi, x_lo), jnp.where(quarter8 == 1, x_lo, x_hi))
    z_rows = (four_of(back[1], back[0], back[3], back[2]), four_of(back[0], back[1], back[2], back[3]))
    for slot in range(SLOTS):
        for side in range(2):
            ey[2 * slot + side] = jnp.broadcast_to(y_rows[side][slot:slot + 1], (16, 128))
            ez[2 * slot + side] = jnp.broadcast_to(z_rows[side][slot:slot + 1], (16, 128))
    row16 = iota((16, 128), 0)

    @pl.loop(1, PEERS)
    def _(k):
        peer = (me + k) % PEERS
        part = fx[inv[0, peer]]
        first = jnp.where(row16 == 6, ey[inv[1, peer]], jnp.where(row16 == 7, ez[inv[2, peer]], part[:, 0:128].astype(F32)))
        s3[peer, :, 0:128] = first.astype(BF16)
        s3[peer, :, 128:512] = part[:, 128:512]
        send(s3, r3, 2, peer).start()

    ready((0,))
    solid_copy.wait()
    for k in range(1, GROUPS):
        out_solid[k - 1] = solid_ref[front_slot(k - 1, front, redeal)]
        solid_out(k).start()
    deep, lane = iota((128, CELLS), 0), iota((128, CELLS), 1)
    for side in range(2):
        spread[side] = jnp.where((deep % S == lane // S) & (lane % S == (S - 1) * side), 1.0, 0.0).astype(BF16)
    row8w = iota((8, CELLS), 0)
    depth8w = lane8w % S

    def without_row(block, step):
        if step == 1:
            return jnp.concatenate([jnp.where(row8w == 0, 0.0, block[:8]), block[8:]], axis=0)
        return jnp.concatenate([block[:S - 8], jnp.where(row8w == 7, 0.0, block[S - 8:])], axis=0)

    def masked(block, turn):
        tall = keep[TURNS.index(turn)]
        return block * jnp.concatenate([tall] * 4, axis=0)

    @pl.loop(0, SLOTS)
    def _(slot):
        for d, (step, cy, cz) in enumerate(VELOCITY):
            shift = lane_shift(d)
            if d:
                block = moved[slot, d].astype(F32)
                if step:
                    block = without_row(pltpu.roll(block, step % S, 0), step)
                if shift:
                    block = masked(pltpu.roll(block, shift, 1), (cy, cz))
                moved[slot, d] = block.astype(BF16)
        here = sol_ref[slot]
        below, above = without_row(pltpu.roll(here, 1, 0), 1), without_row(pltpu.roll(here, S - 1, 0), -1)
        total = below + above
        grads[slot, 1] = above - below
        below, above = masked(pltpu.roll(here, S, 1), (1, 0)), masked(pltpu.roll(here, CELLS - S, 1), (-1, 0))
        total = total + below + above
        grads[slot, 2] = above - below
        below, above = masked(pltpu.roll(here, 1, 1), (0, 1)), masked(pltpu.roll(here, CELLS - 1, 1), (0, -1))
        grads[slot, 3] = above - below
        grads[slot, 0] = here + diffusivity * (total + below + above - 6.0 * here)

    all_of(s2, r2, 1).wait_recv()
    all_of(s3, r3, 2).wait_recv()
    row32, lane32 = iota((S, 128), 0), iota((S, 128), 1)
    item = lane32 // S
    depth32 = lane32 % S
    row16w = iota((16, CELLS), 0)

    def shift_rows(plane, down, up, edge):
        from_low = jnp.where(row32 == 0, edge, pltpu.roll(plane, 1, 0))
        from_high = jnp.where(row32 == S - 1, edge, pltpu.roll(plane, S - 1, 0))
        return jnp.where(item == down, from_low, jnp.where(item == up, from_high, plane))

    @pl.loop(0, SLOTS)
    def _(slot):
        for side in range(2):
            enter = LEAVES[0][1 - side]
            part = r3[owner(slot, side)].astype(F32)
            rows = jnp.concatenate([part[0:8], part[8:16]], axis=1)
            at, hit = (0, row16w == 0) if side == 0 else (16, row16w == 15)
            for i, d in enumerate(enter):
                moved[slot, d, at:at + 16, :] += jnp.where(hit, rows[i:i + 1], 0.0).astype(BF16)
            at, hit, sign = (0, row8w == 0, -1.0) if side == 0 else (S - 8, row8w == 7, 1.0)
            extra = jnp.where(hit, rows[5:6], 0.0)
            grads[slot, 0, at:at + 8, :] += diffusivity * extra
            grads[slot, 1, at:at + 8, :] += sign * extra

            enter = LEAVES[1][1 - side]
            down, up = (1, 2) if side == 0 else (2, 1)
            peer = owner(slot, 2 + side)
            edge = r3[peer, :, 0:128].astype(F32)[6:7]
            tiles = (shift_rows(r2[peer, :, 0:128].astype(F32), down, up, edge), r2[peer, :, 128:256].astype(F32))
            first = 0 if side == 0 else 128 - S
            at = 0 if side == 0 else CELLS - 128
            for i in range(6):
                cz = VELOCITY[enter[i]][2] if i < 5 else 0
                shift = (first + cz - (i % 4) * S) % 128
                tile = tiles[i // 4]
                if shift:
                    tile = pltpu.roll(tile, shift, 1)
                hit = item == first // S
                if cz:
                    hit = hit & (depth32 != (0 if cz == 1 else S - 1))
                tile = jnp.where(hit, tile, 0.0)
                if i < 5:
                    moved[slot, enter[i], :, at:at + 128] += tile.astype(BF16)
                else:
                    grads[slot, 0, :, at:at + 128] += diffusivity * tile
                    grads[slot, 2, :, at:at + 128] += sign * tile

            enter = LEAVES[2][1 - side]
            peer = owner(slot, 4 + side)
            edge = r3[peer, :, 0:128].astype(F32)[7:8]
            third = jnp.sum(jnp.where(lane32 == row32 + 96, edge, 0.0), axis=1, keepdims=True)
            fourth = jnp.sum(jnp.where(lane32 == row32, edge, 0.0), axis=1, keepdims=True)
            plane, late = r2[peer, :, 256:384].astype(F32), r2[peer, :, 128:256].astype(F32)
            turn, at3, at4 = (1, 96, 95) if side == 0 else (127, 127, 64)
            turned = jnp.where(lane32 == at3, third, pltpu.roll(plane, turn, 1))
            turned_late = jnp.where(lane32 == at4, fourth, pltpu.roll(late, 128 - turn, 1))
            plane = jnp.where(item == 3, turned, shift_rows(plane, down, up, edge))
            late = jnp.where(item == 2, turned_late, late)
            stack = [jnp.where(item == i, plane, 0.0).astype(BF16) for i in range(4)]
            stack += [jnp.where(item == i, late, 0.0).astype(BF16) for i in range(2, 4)]
            ghost[...] = dot(jnp.concatenate(stack, axis=0), spread[side])
            for i, d in enumerate(enter):
                moved[slot, d] += ghost[S * i:S * i + S, :].astype(BF16)
            grads[slot, 0] += diffusivity * ghost[5 * S:6 * S, :]
            grads[slot, 3] += sign * ghost[5 * S:6 * S, :]

    def moments(slot, lanes):
        def f(d):
            return moved[slot, d, :, lanes].astype(F32)

        straight, slanted = 0.0, 0.0
        along = [0.0, 0.0, 0.0]
        for d in range(1, 19, 2):
            one, two = f(d), f(d + 1)
            both, diff = one + two, one - two
            if d < 7:
                straight = both + straight
                along[d // 2] = diff + diff
            else:
                slanted = both + slanted
                for axis in range(3):
                    if VELOCITY[d][axis]:
                        along[axis] = along[axis] + diff if VELOCITY[d][axis] == 1 else along[axis] - diff
        density = f(0) * (1.0 / 3.0) + straight * (1.0 / 18.0) + slanted * (1.0 / 36.0)
        over36 = (1.0 / 36.0) / density
        ux, uy, uz = (part * over36 for part in along)
        mixed = grads[slot, 0, :, lanes] - 0.5 * (
            ux * grads[slot, 1, :, lanes] + uy * grads[slot, 2, :, lanes] + uz * grads[slot, 3, :, lanes])
        return density, ux, uy, uz, mixed

    @pl.loop(0, GROUPS - 1)
    def _(step):
        slot = front_slot(step, front, redeal)

        @pl.loop(0, CELLS // WIDE)
        def _(part):
            lanes = pl.ds(pl.multiple_of(part * WIDE, WIDE), WIDE)
            out_mixed[step, :, lanes] = moments(slot, lanes)[4]

        mixed_out(step + 1).start()

    @pl.loop(0, SLOTS - 3)
    def _(step):
        slot = rest_slot(step, front)

        @pl.loop(0, CELLS // WIDE)
        def _(part):
            lanes = pl.ds(pl.multiple_of(part * WIDE, WIDE), WIDE)
            *now, mixed = moments(slot, lanes)
            for i in range(4):
                flow[step, i, :, lanes] = now[i]
            fresh[step, 0, :, lanes], fresh[step, 1, :, lanes] = react(mixed, solid_ref[slot, :, lanes])

    all_of(s1, r1, 0).wait_send()
    all_of(s2, r2, 1).wait_send()
    all_of(s3, r3, 2).wait_send()
    for k in range(1, GROUPS):
        table_copy(k).wait()
        solid_out(k).wait()
        mixed_out(k).wait()


def exchange(populations, solute, solid_fraction, neighbours, front_list, redeal_list):
    vmem, hbm = (pl.BlockSpec(memory_space=m) for m in (pltpu.VMEM, pltpu.HBM))
    operands = (populations, solute, solid_fraction, neighbours, front_list, redeal_list)
    return pl.pallas_call(
        exchange_kernel,
        out_shape=(
            jax.ShapeDtypeStruct(populations.shape, BF16),
            jax.ShapeDtypeStruct((SLOTS - 3, 4, S, CELLS), F32),
            jax.ShapeDtypeStruct((SLOTS - 3, 2, S, CELLS), F32),
            jax.ShapeDtypeStruct((GROUPS - 1, S, CELLS), F32),
            jax.ShapeDtypeStruct((GROUPS - 1, S, CELLS), F32),
            jax.ShapeDtypeStruct((GROUPS - 1, 1, 128), I32),
        ),
        in_specs=[hbm] * 6,
        out_specs=(vmem,) * 6,
        scratch_shapes=[
            pltpu.VMEM((SLOTS, S, CELLS), F32),
            pltpu.VMEM((SLOTS, S, CELLS), F32),
            pltpu.VMEM((SLOTS, 16, CELLS), BF16),
            pltpu.VMEM((2 * SLOTS, 16, 512), BF16),
            pltpu.VMEM((2 * SLOTS, S, 256), BF16),
            pltpu.VMEM((2 * SLOTS, S, 256), BF16),
            pltpu.VMEM((2 * SLOTS, 16, 128), BF16),
            pltpu.VMEM((2 * SLOTS, 16, 128), BF16),
            pltpu.VMEM((2 * SLOTS, 16, 128), F32),
            pltpu.VMEM((2 * SLOTS, 16, 128), F32),
            pltpu.VMEM((PEERS, 16, 128), BF16),
            pltpu.VMEM((PEERS, S, 384), BF16),
            pltpu.VMEM((PEERS, 16, 512), BF16),
            pltpu.VMEM((PEERS, 16, 128), BF16),
            pltpu.VMEM((PEERS, S, 384), BF16),
            pltpu.VMEM((PEERS, 16, 512), BF16),
            pltpu.VMEM((1, 128), I32),
            pltpu.VMEM((8, 128), I32),
            pltpu.VMEM((len(TURNS), 8, CELLS), F32),
            pltpu.VMEM((2, 128, CELLS), BF16),
            pltpu.VMEM((6 * S, CELLS), F32),
            pltpu.VMEM((SLOTS, 4, S, CELLS), F32),
            pltpu.VMEM((GROUPS - 1, S, CELLS), F32),
            pltpu.VMEM((GROUPS - 1, S, CELLS), F32),
            pltpu.SMEM((SLOTS, 6), I32),
            pltpu.SMEM((8, 128), I32),
            pltpu.SMEM((3,), I32),
            pltpu.SMEM((3,), I32),
            pltpu.SemaphoreType.DMA((19,)),
            pltpu.SemaphoreType.DMA((6,)),
            pltpu.SemaphoreType.DMA((3,)),
            pltpu.SemaphoreType.DMA((3,)),
            pltpu.SemaphoreType.DMA((3, GROUPS)),
            pltpu.SemaphoreType.DMA((3, GROUPS)),
        ],
        compiler_params=pltpu.CompilerParams(collective_id=0, has_side_effects=True, vmem_limit_bytes=28 * 2**20),
        cost_estimate=pl.CostEstimate(flops=10**9, bytes_accessed=12 * 10**6, transcendentals=0),
        name="exchange",
    )(*(pltpu.with_memory_space_constraint(operand, pltpu.HBM) for operand in operands))


def collide(f, flow, amount, put):
    density, ux, uy, uz = flow
    pair_sum = [f[i] + f[i + 1] for i in range(1, 19, 2)]
    pair_dif = [f[i] - f[i + 1] for i in range(1, 19, 2)]
    share = 1.0 - amount
    scale = (1.0 / relax_time) * share * density
    base = scale - (1.5 * scale) * (ux * ux + uy * uy + uz * uz)
    curve, slope = 4.5 * scale, 3.0 * scale
    rest = (1.0 / relax_time - 1.0) * share
    even_part, odd_part = 0.5 * (amount - rest), 0.5 * (amount + rest)
    put(0, base + (amount - rest) * f[0])
    along_all = (ux, uy, uz, ux + uy, ux - uy, ux + uz, ux - uz, uy + uz, uy - uz)
    for pair in range(9):
        along = along_all[pair]
        even = base + (curve * along) * along + even_part * pair_sum[pair]
        odd = slope * along - odd_part * pair_dif[pair]
        put(2 * pair + 1, even + odd)
        put(2 * pair + 2, even - odd)


def collide_kernel(front, table, moved, flow, fresh, got_mixed, got_solid, solid, new_pop, new_sol, new_solid,
                   ones, done, placed, sems, pop_sems):
    ones[...] = jnp.ones(ones.shape, BF16)
    copies = []
    for k in range(3):
        slot = place_slot(k, front, table)
        placed[0, k], placed[1, k] = react(got_mixed[k], got_solid[k])
        copies.append(pltpu.make_async_copy(ones, new_pop.at[slot], sems.at[0, k]))
        copies.append(pltpu.make_async_copy(placed.at[0, k], new_sol.at[slot], sems.at[1, k]))
        copies.append(pltpu.make_async_copy(placed.at[1, k], new_solid.at[slot], sems.at[2, k]))
    for k in range(SLOTS - 3):
        slot = rest_slot(k, front)
        copies.append(pltpu.make_async_copy(fresh.at[k, 0], new_sol.at[slot], sems.at[1, 3 + k]))
        copies.append(pltpu.make_async_copy(fresh.at[k, 1], new_solid.at[slot], sems.at[2, 3 + k]))
    for copy in copies:
        copy.start()

    def out(index):
        return pltpu.make_async_copy(done.at[index], new_pop.at[rest_slot(index, front)], pop_sems.at[index])

    @pl.loop(0, SLOTS - 3)
    def _(index):
        slot = rest_slot(index, front)
        for row in range(0, S, 16):
            for lane in range(0, CELLS, 128):
                rows, lanes = slice(row, row + 16), slice(lane, lane + 128)

                def put(direction, value):
                    done[index, direction, rows, lanes] = value.astype(BF16)

                f = [moved[slot, d, rows, lanes].astype(F32) for d in range(19)]
                collide(f, [flow[index, i, rows, lanes] for i in range(4)], solid[slot, rows, lanes], put)
        out(index).start()

    for copy in copies:
        copy.wait()
    for index in range(SLOTS - 3):
        out(index).wait()


def collide_all(front, table, moved, flow, fresh, got_mixed, got_solid, solid_fraction):
    smem, vmem, anywhere = (pl.BlockSpec(memory_space=m) for m in (pltpu.SMEM, pltpu.VMEM, pl.ANY))
    return pl.pallas_call(
        collide_kernel,
        out_shape=(
            jax.ShapeDtypeStruct(moved.shape, BF16),
            jax.ShapeDtypeStruct(solid_fraction.shape, F32),
            jax.ShapeDtypeStruct(solid_fraction.shape, F32),
        ),
        in_specs=[smem] * 2 + [vmem] * 6,
        out_specs=(anywhere,) * 3,
        scratch_shapes=[
            pltpu.VMEM((19, S, CELLS), BF16),
            pltpu.VMEM((SLOTS - 3, 19, S, CELLS), BF16),
            pltpu.VMEM((2, 3, S, CELLS), F32),
            pltpu.SemaphoreType.DMA((3, SLOTS)),
            pltpu.SemaphoreType.DMA((SLOTS - 3,)),
        ],
        compiler_params=pltpu.CompilerParams(vmem_limit_bytes=16 * 2**20),
        cost_estimate=pl.CostEstimate(flops=10**8, bytes_accessed=16 * 10**6, transcendentals=0),
        name="collide",
    )(front, table, moved, flow, fresh, got_mixed, got_solid, solid_fraction)


def body(populations, solute, solid_fraction, neighbours, front_list, redeal_list):
    moved, flow, fresh, got_mixed, got_solid, table = exchange(
        populations, solute, solid_fraction, neighbours, front_list, redeal_list)
    return collide_all(front_list, table, moved, flow, fresh, got_mixed, got_solid, solid_fraction)


def solution(mesh):
    deal = ("blk", "grp")
    return jax.shard_map(
        body,
        mesh=mesh,
        in_specs=(P(deal, None, None, None), P(deal, None, None), P(deal, None, None), P(deal, None), P(deal), P(deal)),
        out_specs=(P(deal, None, None, None), P(deal, None, None), P(deal, None, None)),
        check_vma=False,
    )
```

time: 55.6 us -> 49.8 us (0.90)
  starting transfers between devices: 5.68 us -> 0 us
  Pallas kernels: 47.8 us -> 49.1 us
  local copies, waits for them, and re-layouts: 1.24 us -> 0.01 us
    ppermute x3 -> x0, starting transfers between devices: 5.68 us -> none  [body(): lax.ppermute(sent[k], 'grp', [(g, (g + k + 1) % GROUPS) for g in range(GR...]
    unnamed x10 -> x4, local copies, waits for them, and re-layouts: 1.24 us -> 0.01 us
    pallas_call x4 -> x2, Pallas kernels: 47.8 us -> 49.1 us  [the longest x1 43.2 us: exchange(): pl.pallas_call(exchange_kernel, out_shape=(jax.ShapeDtypeStruct(populatio...]
  transfers between devices with their start and end apart: 3 -> 0, of which waited for: 0 -> 0; matrix products, arithmetic and copies ran while one was open for 0% -> 0% of each run, Pallas kernels for 20% -> 0%
where the time goes in v3:
time: 49.8 us; the launch traced here: 49.7 us
  Pallas kernels  49.1 us (99%)
  between operations  0.67 us (1%)
    pallas_call x1, Pallas kernels, exchange(): pl.pallas_call(exchange_kernel, out_shape=(jax.ShapeDtypeStruct(populatio...  43.2 us
    pallas_call x1, Pallas kernels, collide_all(): pl.pallas_call(collide_kernel, out_shape=(jax.ShapeDtypeStruct(moved.shap...  5.84 us

profile of v3, /device:TPU:1, one launch (start us, length us, event | category | flops | bytes accessed | tf_op | source)
XLA Modules:
  0.0 49.7 jit_solution(10624131340119168722)
XLA Ops:
  0.6 0.0 copy-start.1
  0.6 0.0 copy-start
  0.7 43.2 %exchange.1 = (bf16[8,19,32,1024]{3,2,1,0:T(8,128)(2,1)S(1)}, f32[5,4,32,1024]{3,2,1,0:T(8,128)S(1)}, f32[5,2,32,1024]{3,2,1,0:T(8,128)S(1)}, f32[3,32,1024]{2,1...) custom-call(bf16[8,19,32,1024]{3,2,1,0:T(8,128)(2,1)} %pop_hbm.1, f32[8,32,1024]{2,1,0:T(8,128)} %sol_hbm.1, ...), custom_call_target="tpu_custom_call" | custom-call | flops 1000000000 | bytes 12000000 | tf_op jit(solution)/shard_map/exchange/pallas_call | solution.py:482
  43.9 0.0 copy-done.1
  43.9 0.0 copy-done
  43.9 5.8 %collide.1 = (bf16[8,19,32,1024]{3,2,1,0:T(8,128)(2,1)}, f32[8,32,1024]{2,1,0:T(8,128)}, f32[8,32,1024]{2,1,0:T(8,128)}) custom-call(s32[3]{0:T(128)S(1)} %copy-done.1, s32[3,1,128]{2,1,0:T(1,128)S(1)} %get-tuple-element.9.table, bf16[8,19,32,1024]{3,2,1,0:T(8,128)(2,1)S(1)} %get-tuple-element.10.moved, f32[5,4,32,1024]{3,2,1,0:T(8,128)S(1)} %get-tuple-element.11.flow, ...), custom_call_target="tpu_custom_call" | custom-call | flops 100000000 | bytes 16000000 | tf_op jit(solution)/shard_map/collide/pallas_call | solution.py:598
Async XLA Ops:
  0.6 43.2 %copy-start.1 = (s32[3]{0:T(128)S(1)}, s32[3]{0:T(128)}, u32[]{:S(2)}) copy-start(s32[3]{0:T(128)} %front.1) | copy-start | bytes 40
  0.6 43.2 %copy-start = (f32[8,32,1024]{2,1,0:T(8,128)S(1)}, f32[8,32,1024]{2,1,0:T(8,128)}, u32[]{:S(2)}) copy-start(f32[8,32,1024]{2,1,0:T(8,128)} %solid.1) | copy-start | bytes 3145732

commit v4 on v3

--- a/solution.py
+++ b/solution.py
@@ -48,16 +48,16 @@
 
 
 def front_slot(step, front, redeal):
-    group = front[0] // SLOTS % GROUPS
-    slot = front[0] % SLOTS
+    group = (front[0] >> 3) & (GROUPS - 1)
+    slot = front[0] & (SLOTS - 1)
     for entry in range(1, 3):
-        ahead = (redeal[entry] // SLOTS % GROUPS - group + GROUPS) % GROUPS
-        slot = jnp.where(ahead == step + 1, front[entry] % SLOTS, slot)
+        ahead = ((redeal[entry] >> 3) - group) & (GROUPS - 1)
+        slot = jnp.where(ahead == step + 1, front[entry] & (SLOTS - 1), slot)
     return slot
 
 
 def rest_slot(step, front):
-    a, b, c = (front[entry] % SLOTS for entry in range(3))
+    a, b, c = (front[entry] & (SLOTS - 1) for entry in range(3))
     low, high = jnp.minimum(a, b), jnp.maximum(a, b)
     mid, high = jnp.minimum(high, c), jnp.maximum(high, c)
     low, mid = jnp.minimum(low, mid), jnp.maximum(low, mid)
@@ -68,18 +68,18 @@
 
 
 def place_slot(step, front, table):
-    group = front[0] // SLOTS % GROUPS
-    slot = table[step, 0, 0] % SLOTS
+    group = (front[0] >> 3) & (GROUPS - 1)
+    slot = table[step, 0, 0] & (SLOTS - 1)
     for entry in range(1, 3):
         place = table[step, 0, entry]
-        slot = jnp.where(place // SLOTS % GROUPS == group, place % SLOTS, slot)
+        slot = jnp.where((place >> 3) & (GROUPS - 1) == group, place & (SLOTS - 1), slot)
     return slot
 
 
 def exchange_kernel(pop_hbm, sol_hbm, solid_hbm, nbr_hbm, front_hbm, redeal_hbm,
-                    moved, flow, fresh, got_mixed, got_solid, table_ref,
+                    moved, flow, fresh, got_mixed, got_base, got_solid, table_ref,
                     sol_ref, solid_ref, xr, fx, fy, fz, lx, ly, ey, ez, s1, s2, s3, r1, r2, r3, mine, inv_vmem,
-                    keep, spread, ghost, grads, out_mixed, out_solid,
+                    keep, spread, ghost, grads, edge_in, edge_rows, out_mixed, out_base, out_solid,
                     nbr, inv, front, redeal, fetch_sem, small_sem, send_sem, recv_sem, grp_send, grp_recv):
     me = lax.axis_index("blk")
     grp = lax.axis_index("grp")
@@ -110,9 +110,9 @@
     for k in range(1, GROUPS):
         pl.semaphore_signal(barrier, inc=1, device_id={"grp": (grp + k) % GROUPS}, device_id_type=pl.DeviceIdType.MESH)
 
-    deep, lane = iota((CELLS, 128), 0), iota((CELLS, 128), 1) % S
+    deep, lane = iota((CELLS, 128), 0), iota((CELLS, 128), 1) & (S - 1)
     pick = [jnp.where(deep == lane * S + z, 1.0, 0.0).astype(BF16) for z in (0, S - 1)]
-    wide, lane = iota((128, 128), 0), iota((128, 128), 1) % S
+    wide, lane = iota((128, 128), 0), iota((128, 128), 1) & (S - 1)
     pick_y = [jnp.where(wide == lane + first, 1.0, 0.0).astype(BF16) for first in (0, 128 - S)]
 
     nbr_copy.wait()
@@ -120,7 +120,7 @@
     front_copy.wait()
 
     def owner(slot, face):
-        return nbr[slot, face] // (SLOTS * GROUPS)
+        return nbr[slot, face] >> 5
 
     row8, lane8 = iota((8, 128), 0), iota((8, 128), 1)
     found = jnp.zeros((8, 128), I32)
@@ -161,7 +161,7 @@
     faces = xr[...].reshape(SLOTS * 16, CELLS)
     z_low, z_top = dot(faces, pick[0]), dot(faces, pick[1])
     y_low, y_top = dot(faces[:, 0:128], pick_y[0]), dot(faces[:, CELLS - 128:], pick_y[1])
-    quarter1 = lane1 // S
+    quarter1 = lane1 >> 5
     ready((15, 16, 17, 18))
     high = slice(CELLS - 128, CELLS)
     lane16 = iota((16, 128), 1)
@@ -213,6 +213,9 @@
     def solid_out(k):
         return grp_copy(out_solid.at[k - 1], got_solid.at[k - 1], 1, k)
 
+    def base_out(k):
+        return grp_copy(out_base.at[k - 1], got_base.at[k - 1], 3, k)
+
     def mixed_out(k):
         return grp_copy(out_mixed.at[k - 1], got_mixed.at[k - 1], 2, k)
 
@@ -227,7 +230,7 @@
     for k in range(1, GROUPS):
         table_copy(k).start()
 
-    quarter = iota((SLOTS * S, 128), 1) // S
+    quarter = iota((SLOTS * S, 128), 1) >> 5
 
     def place_items(into, side, parts, later):
         low = jnp.where(quarter == 0, parts[0], jnp.where(quarter == 1, parts[1], jnp.where(quarter == 2, parts[2], parts[3])))
@@ -266,7 +269,7 @@
         if cy:
             hold = hold & ((lane8w >= S) if cy == 1 else (lane8w < CELLS - S))
         if cz:
-            hold = hold & (lane8w % S != (0 if cz == 1 else S - 1))
+            hold = hold & ((lane8w & (S - 1)) != (0 if cz == 1 else S - 1))
         keep[i] = jnp.where(hold, 1.0, 0.0)
 
     @pl.loop(0, SLOTS)
@@ -286,7 +289,7 @@
         return jnp.concatenate([r1[owner(slot, face)].astype(F32)[row:row + 1] for slot in range(SLOTS)], axis=0)
 
     x_lo, x_hi, y_lo, y_hi = lines(0, 0), lines(1, 0), lines(2, 8), lines(3, 8)
-    quarter8 = lane8 // S
+    quarter8 = lane8 >> 5
     back = [pltpu.roll(part, 128 - S, 1) for part in (x_lo, x_hi, y_lo, y_hi)]
     x_lo, x_hi = pltpu.roll(x_lo, S, 1), pltpu.roll(x_hi, S, 1)
 
@@ -317,9 +320,8 @@
         solid_out(k).start()
     deep, lane = iota((128, CELLS), 0), iota((128, CELLS), 1)
     for side in range(2):
-        spread[side] = jnp.where((deep % S == lane // S) & (lane % S == (S - 1) * side), 1.0, 0.0).astype(BF16)
+        spread[side] = jnp.where(((deep & (S - 1)) == lane >> 5) & ((lane & (S - 1)) == (S - 1) * side), 1.0, 0.0).astype(BF16)
     row8w = iota((8, CELLS), 0)
-    depth8w = lane8w % S
 
     def without_row(block, step):
         if step == 1:
@@ -352,37 +354,28 @@
         grads[slot, 3] = above - below
         grads[slot, 0] = here + diffusivity * (total + below + above - 6.0 * here)
 
+    for k in range(1, GROUPS):
+        out_base[k - 1] = grads[front_slot(k - 1, front, redeal), 0]
+        base_out(k).start()
+    row32, lane32 = iota((S, 128), 0), iota((S, 128), 1)
+    item = lane32 >> 5
+    depth32 = lane32 & (S - 1)
+    row16w = iota((16, CELLS), 0)
     all_of(s2, r2, 1).wait_recv()
-    all_of(s3, r3, 2).wait_recv()
-    row32, lane32 = iota((S, 128), 0), iota((S, 128), 1)
-    item = lane32 // S
-    depth32 = lane32 % S
-    row16w = iota((16, CELLS), 0)
-
-    def shift_rows(plane, down, up, edge):
-        from_low = jnp.where(row32 == 0, edge, pltpu.roll(plane, 1, 0))
-        from_high = jnp.where(row32 == S - 1, edge, pltpu.roll(plane, S - 1, 0))
+
+    def shift_rows(plane, down, up):
+        from_low = jnp.where(row32 == 0, 0.0, pltpu.roll(plane, 1, 0))
+        from_high = jnp.where(row32 == S - 1, 0.0, pltpu.roll(plane, S - 1, 0))
         return jnp.where(item == down, from_low, jnp.where(item == up, from_high, plane))
 
     @pl.loop(0, SLOTS)
     def _(slot):
         for side in range(2):
-            enter = LEAVES[0][1 - side]
-            part = r3[owner(slot, side)].astype(F32)
-            rows = jnp.concatenate([part[0:8], part[8:16]], axis=1)
-            at, hit = (0, row16w == 0) if side == 0 else (16, row16w == 15)
-            for i, d in enumerate(enter):
-                moved[slot, d, at:at + 16, :] += jnp.where(hit, rows[i:i + 1], 0.0).astype(BF16)
-            at, hit, sign = (0, row8w == 0, -1.0) if side == 0 else (S - 8, row8w == 7, 1.0)
-            extra = jnp.where(hit, rows[5:6], 0.0)
-            grads[slot, 0, at:at + 8, :] += diffusivity * extra
-            grads[slot, 1, at:at + 8, :] += sign * extra
-
+            sign = -1.0 if side == 0 else 1.0
             enter = LEAVES[1][1 - side]
             down, up = (1, 2) if side == 0 else (2, 1)
             peer = owner(slot, 2 + side)
-            edge = r3[peer, :, 0:128].astype(F32)[6:7]
-            tiles = (shift_rows(r2[peer, :, 0:128].astype(F32), down, up, edge), r2[peer, :, 128:256].astype(F32))
+            tiles = (shift_rows(r2[peer, :, 0:128].astype(F32), down, up), r2[peer, :, 128:256].astype(F32))
             first = 0 if side == 0 else 128 - S
             at = 0 if side == 0 else CELLS - 128
             for i in range(6):
@@ -403,14 +396,11 @@
 
             enter = LEAVES[2][1 - side]
             peer = owner(slot, 4 + side)
-            edge = r3[peer, :, 0:128].astype(F32)[7:8]
-            third = jnp.sum(jnp.where(lane32 == row32 + 96, edge, 0.0), axis=1, keepdims=True)
-            fourth = jnp.sum(jnp.where(lane32 == row32, edge, 0.0), axis=1, keepdims=True)
             plane, late = r2[peer, :, 256:384].astype(F32), r2[peer, :, 128:256].astype(F32)
             turn, at3, at4 = (1, 96, 95) if side == 0 else (127, 127, 64)
-            turned = jnp.where(lane32 == at3, third, pltpu.roll(plane, turn, 1))
-            turned_late = jnp.where(lane32 == at4, fourth, pltpu.roll(late, 128 - turn, 1))
-            plane = jnp.where(item == 3, turned, shift_rows(plane, down, up, edge))
+            turned = jnp.where(lane32 == at3, 0.0, pltpu.roll(plane, turn, 1))
+            turned_late = jnp.where(lane32 == at4, 0.0, pltpu.roll(late, 128 - turn, 1))
+            plane = jnp.where(item == 3, turned, shift_rows(plane, down, up))
             late = jnp.where(item == 2, turned_late, late)
             stack = [jnp.where(item == i, plane, 0.0).astype(BF16) for i in range(4)]
             stack += [jnp.where(item == i, late, 0.0).astype(BF16) for i in range(2, 4)]
@@ -419,6 +409,51 @@
                 moved[slot, d] += ghost[S * i:S * i + S, :].astype(BF16)
             grads[slot, 0] += diffusivity * ghost[5 * S:6 * S, :]
             grads[slot, 3] += sign * ghost[5 * S:6 * S, :]
+
+    all_of(s3, r3, 2).wait_recv()
+    item16 = lane16 >> 5
+
+    @pl.loop(0, SLOTS)
+    def _(slot):
+        for side in range(2):
+            edge = r3[owner(slot, 4 + side), :, 0:128].astype(F32)[7:8]
+            one, two = (3, 12) if side == 0 else (11, 4)
+            hit = ((row16 == one) & (item16 == 1)) | ((row16 == two) & (item16 == 2))
+            edge_in[side, slot] = jnp.where(hit, edge, 0.0).astype(BF16)
+
+    z_edges = [dot(edge_in[side].reshape(SLOTS * 16, 128), spread[side]) for side in range(2)]
+    edge_rows[...] = (z_edges[0] + z_edges[1]).reshape(SLOTS, 16, CELLS)
+
+    @pl.loop(0, SLOTS)
+    def _(slot):
+        halves = []
+        for side in range(2):
+            part = r3[owner(slot, side)].astype(F32)
+            halves.append(jnp.concatenate([part[0:8], part[8:16]], axis=1))
+        rows = jnp.concatenate(halves, axis=0) + edge_rows[slot]
+        low, top = (jnp.broadcast_to(r3[owner(slot, 2 + side), :, 0:128].astype(F32)[6:7], (16, 128)) for side in range(2))
+        low = jnp.where(row16 == 1, pltpu.roll(low, 96, 1), jnp.where(row16 == 10, pltpu.roll(low, 64, 1), 0.0))
+        top = jnp.where(row16 == 2, pltpu.roll(top, 32, 1), jnp.where(row16 == 9, pltpu.roll(top, 64, 1), 0.0))
+        low, top = jnp.where(item16 == 0, low, 0.0), jnp.where(item16 == 3, top, 0.0)
+        rows = jnp.concatenate([rows[:, 0:128] + low, rows[:, 128:CELLS - 128], rows[:, CELLS - 128:] + top], axis=1)
+        for side in range(2):
+            at, hit = (0, row16w == 0) if side == 0 else (16, row16w == 15)
+            for i, d in enumerate(LEAVES[0][1 - side]):
+                row = rows[8 * side + i:8 * side + i + 1]
+                moved[slot, d, at:at + 16, :] += jnp.where(hit, row, 0.0).astype(BF16)
+            at, hit, sign = (0, row8w == 0, -1.0) if side == 0 else (S - 8, row8w == 7, 1.0)
+            extra = jnp.where(hit, rows[8 * side + 5:8 * side + 6], 0.0)
+            grads[slot, 0, at:at + 8, :] += diffusivity * extra
+            grads[slot, 1, at:at + 8, :] += sign * extra
+
+            edge = r3[owner(slot, 4 + side), :, 0:128].astype(F32)[7:8]
+            third = jnp.sum(jnp.where(lane32 == row32 + 96, edge, 0.0), axis=1, keepdims=True)
+            fourth = jnp.sum(jnp.where(lane32 == row32, edge, 0.0), axis=1, keepdims=True)
+            third = jnp.where(lane32 == (0 if side == 0 else 127), third, 0.0).astype(BF16)
+            fourth = jnp.where(lane32 == (96 if side == 0 else 31), fourth, 0.0).astype(BF16)
+            starts, ends = (third, fourth) if side == 0 else (fourth, third)
+            moved[slot, 15 if side == 0 else 17, :, 0:128] += starts
+            moved[slot, 18 if side == 0 else 16, :, CELLS - 128:] += ends
 
     def moments(slot, lanes):
         def f(d):
@@ -451,7 +486,7 @@
         @pl.loop(0, CELLS // WIDE)
         def _(part):
             lanes = pl.ds(pl.multiple_of(part * WIDE, WIDE), WIDE)
-            out_mixed[step, :, lanes] = moments(slot, lanes)[4]
+            out_mixed[step, :, lanes] = (moments(slot, lanes)[4] - out_base[step, :, lanes]).astype(BF16)
 
         mixed_out(step + 1).start()
 
@@ -473,6 +508,7 @@
     for k in range(1, GROUPS):
         table_copy(k).wait()
         solid_out(k).wait()
+        base_out(k).wait()
         mixed_out(k).wait()
 
 
@@ -485,12 +521,13 @@
             jax.ShapeDtypeStruct(populations.shape, BF16),
             jax.ShapeDtypeStruct((SLOTS - 3, 4, S, CELLS), F32),
             jax.ShapeDtypeStruct((SLOTS - 3, 2, S, CELLS), F32),
+            jax.ShapeDtypeStruct((GROUPS - 1, S, CELLS), BF16),
             jax.ShapeDtypeStruct((GROUPS - 1, S, CELLS), F32),
             jax.ShapeDtypeStruct((GROUPS - 1, S, CELLS), F32),
             jax.ShapeDtypeStruct((GROUPS - 1, 1, 128), I32),
         ),
         in_specs=[hbm] * 6,
-        out_specs=(vmem,) * 6,
+        out_specs=(vmem,) * 7,
         scratch_shapes=[
             pltpu.VMEM((SLOTS, S, CELLS), F32),
             pltpu.VMEM((SLOTS, S, CELLS), F32),
@@ -514,6 +551,9 @@
             pltpu.VMEM((2, 128, CELLS), BF16),
             pltpu.VMEM((6 * S, CELLS), F32),
             pltpu.VMEM((SLOTS, 4, S, CELLS), F32),
+            pltpu.VMEM((2, SLOTS, 16, 128), BF16),
+            pltpu.VMEM((SLOTS, 16, CELLS), F32),
+            pltpu.VMEM((GROUPS - 1, S, CELLS), BF16),
             pltpu.VMEM((GROUPS - 1, S, CELLS), F32),
             pltpu.VMEM((GROUPS - 1, S, CELLS), F32),
             pltpu.SMEM((SLOTS, 6), I32),
@@ -524,8 +564,8 @@
             pltpu.SemaphoreType.DMA((6,)),
             pltpu.SemaphoreType.DMA((3,)),
             pltpu.SemaphoreType.DMA((3,)),
-            pltpu.SemaphoreType.DMA((3, GROUPS)),
-            pltpu.SemaphoreType.DMA((3, GROUPS)),
+            pltpu.SemaphoreType.DMA((4, GROUPS)),
+            pltpu.SemaphoreType.DMA((4, GROUPS)),
         ],
         compiler_params=pltpu.CompilerParams(collective_id=0, has_side_effects=True, vmem_limit_bytes=28 * 2**20),
         cost_estimate=pl.CostEstimate(flops=10**9, bytes_accessed=12 * 10**6, transcendentals=0),
@@ -553,13 +593,13 @@
         put(2 * pair + 2, even - odd)
 
 
-def collide_kernel(front, table, moved, flow, fresh, got_mixed, got_solid, solid, new_pop, new_sol, new_solid,
+def collide_kernel(front, table, moved, flow, fresh, got_mixed, got_base, got_solid, solid, new_pop, new_sol, new_solid,
                    ones, done, placed, sems, pop_sems):
     ones[...] = jnp.ones(ones.shape, BF16)
     copies = []
     for k in range(3):
         slot = place_slot(k, front, table)
-        placed[0, k], placed[1, k] = react(got_mixed[k], got_solid[k])
+        placed[0, k], placed[1, k] = react(got_base[k] + got_mixed[k].astype(F32), got_solid[k])
         copies.append(pltpu.make_async_copy(ones, new_pop.at[slot], sems.at[0, k]))
         copies.append(pltpu.make_async_copy(placed.at[0, k], new_sol.at[slot], sems.at[1, k]))
         copies.append(pltpu.make_async_copy(placed.at[1, k], new_solid.at[slot], sems.at[2, k]))
@@ -593,7 +633,7 @@
         out(index).wait()
 
 
-def collide_all(front, table, moved, flow, fresh, got_mixed, got_solid, solid_fraction):
+def collide_all(front, table, moved, flow, fresh, got_mixed, got_base, got_solid, solid_fraction):
     smem, vmem, anywhere = (pl.BlockSpec(memory_space=m) for m in (pltpu.SMEM, pltpu.VMEM, pl.ANY))
     return pl.pallas_call(
         collide_kernel,
@@ -602,7 +642,7 @@
             jax.ShapeDtypeStruct(solid_fraction.shape, F32),
             jax.ShapeDtypeStruct(solid_fraction.shape, F32),
         ),
-        in_specs=[smem] * 2 + [vmem] * 6,
+        in_specs=[smem] * 2 + [vmem] * 7,
         out_specs=(anywhere,) * 3,
         scratch_shapes=[
             pltpu.VMEM((19, S, CELLS), BF16),
@@ -614,13 +654,13 @@
         compiler_params=pltpu.CompilerParams(vmem_limit_bytes=16 * 2**20),
         cost_estimate=pl.CostEstimate(flops=10**8, bytes_accessed=16 * 10**6, transcendentals=0),
         name="collide",
-    )(front, table, moved, flow, fresh, got_mixed, got_solid, solid_fraction)
+    )(front, table, moved, flow, fresh, got_mixed, got_base, got_solid, solid_fraction)
 
 
 def body(populations, solute, solid_fraction, neighbours, front_list, redeal_list):
-    moved, flow, fresh, got_mixed, got_solid, table = exchange(
+    moved, flow, fresh, got_mixed, got_base, got_solid, table = exchange(
         populations, solute, solid_fraction, neighbours, front_list, redeal_list)
-    return collide_all(front_list, table, moved, flow, fresh, got_mixed, got_solid, solid_fraction)
+    return collide_all(front_list, table, moved, flow, fresh, got_mixed, got_base, got_solid, solid_fraction)
 
 
 def solution(mesh):

time: 49.8 us -> 46.4 us (0.932)
  the two profiles are of different devices: /device:TPU:1 before, /device:TPU:7 now
where the time goes in v4:
time: 46.4 us; the launch traced here: 46.3 us
  Pallas kernels  45.6 us (98%)
  between operations  0.67 us (1%)
    pallas_call x1, Pallas kernels, exchange(): pl.pallas_call(exchange_kernel, out_shape=(jax.ShapeDtypeStruct(populatio...  39.8 us
    pallas_call x1, Pallas kernels, collide_all(): pl.pallas_call(collide_kernel, out_shape=(jax.ShapeDtypeStruct(moved.shap...  5.8 us

profile of v4, /device:TPU:7, one launch (start us, length us, event | category | flops | bytes accessed | tf_op | source)
XLA Modules:
  0.0 46.3 jit_solution(11757249769383087974)
XLA Ops:
  0.6 0.0 copy-start.1
  0.6 0.0 copy-start
  0.7 39.8 %exchange.1 = (bf16[8,19,32,1024]{3,2,1,0:T(8,128)(2,1)S(1)}, f32[5,4,32,1024]{3,2,1,0:T(8,128)S(1)}, f32[5,2,32,1024]{3,2,1,0:T(8,128)S(1)}, bf16[3,32,1024]{2,...) custom-call(bf16[8,19,32,1024]{3,2,1,0:T(8,128)(2,1)} %pop_hbm.1, ...), custom_call_target="tpu_custom_call" | custom-call | flops 1000000000 | bytes 12000000 | tf_op jit(solution)/shard_map/exchange/pallas_call | solution.py:518
  40.5 0.0 copy-done.1
  40.5 0.0 copy-done
  40.5 5.8 %collide.1 = (bf16[8,19,32,1024]{3,2,1,0:T(8,128)(2,1)}, f32[8,32,1024]{2,1,0:T(8,128)}, f32[8,32,1024]{2,1,0:T(8,128)}) custom-call(s32[3]{0:T(128)S(1)} %copy-done.1, s32[3,1,128]{2,1,0:T(1,128)S(1)} %get-tuple-element.10.table, bf16[8,19,32,1024]{3,2,1,0:T(8,128)(2,1)S(1)} %get-tuple-element.11.moved, f32[5,4,32,1024]{3,2,1,0:T(8,128)S(1)} %get-tuple-element.12.flow, ...), custom_call_target="tpu_custom_call" | custom-call | flops 100000000 | bytes 16000000 | tf_op jit(solution)/shard_map/collide/pallas_call | solution.py:638
Async XLA Ops:
  0.6 39.8 %copy-start.1 = (s32[3]{0:T(128)S(1)}, s32[3]{0:T(128)}, u32[]{:S(2)}) copy-start(s32[3]{0:T(128)} %front.1) | copy-start | bytes 40
  0.6 39.8 %copy-start = (f32[8,32,1024]{2,1,0:T(8,128)S(1)}, f32[8,32,1024]{2,1,0:T(8,128)}, u32[]{:S(2)}) copy-start(f32[8,32,1024]{2,1,0:T(8,128)} %solid.1) | copy-start | bytes 3145732

commit v5 on v4

--- a/solution.py
+++ b/solution.py
@@ -77,8 +77,8 @@
 
 
 def exchange_kernel(pop_hbm, sol_hbm, solid_hbm, nbr_hbm, front_hbm, redeal_hbm,
-                    moved, flow, fresh, got_mixed, got_base, got_solid, table_ref,
-                    sol_ref, solid_ref, xr, fx, fy, fz, lx, ly, ey, ez, s1, s2, s3, r1, r2, r3, mine, inv_vmem,
+                    done, fresh, got_mixed, got_base, got_solid, table_ref,
+                    moved, flow, sol_ref, solid_ref, xr, fx, fy, fz, lx, ly, ey, ez, s1, s2, s3, s4, r1, r2, r3, r4, mine, inv_vmem,
                     keep, spread, ghost, grads, edge_in, edge_rows, out_mixed, out_base, out_solid,
                     nbr, inv, front, redeal, fetch_sem, small_sem, send_sem, recv_sem, grp_send, grp_recv):
     me = lax.axis_index("blk")
@@ -144,6 +144,7 @@
                 fetched.add(direction)
                 fetch(direction).wait()
 
+    high = slice(CELLS - 128, CELLS)
     ready(LEAVES[0][0] + LEAVES[0][1])
 
     @pl.loop(0, SLOTS)
@@ -163,7 +164,6 @@
     y_low, y_top = dot(faces[:, 0:128], pick_y[0]), dot(faces[:, CELLS - 128:], pick_y[1])
     quarter1 = lane1 >> 5
     ready((15, 16, 17, 18))
-    high = slice(CELLS - 128, CELLS)
     lane16 = iota((16, 128), 1)
 
     def across(d, at, z):
@@ -179,7 +179,7 @@
             four = (y_top, y_low, z_top, z_low) if side else (y_low, y_top, z_low, z_top)
             four = [part[row + 1 + i:row + 2 + i] for i, part in enumerate(four)]
             line = jnp.where(quarter1 == 0, four[0], jnp.where(quarter1 == 1, four[1], jnp.where(quarter1 == 2, four[2], four[3])))
-            lx[2 * slot + side] = jnp.broadcast_to(line, (16, 128)).astype(BF16)
+            lx[2 * slot + side] = line
             tiles = [part[:, 128 * (slot // 4):128 * (slot // 4) + 128] for part in y_lines[side]]
             shift = (128 - S * (slot % 4)) % 128
             if shift:
@@ -187,7 +187,7 @@
             shift = (shift + S) % 128
             if shift:
                 tiles[1] = pltpu.roll(tiles[1], shift, 1)
-            ly[2 * slot + side] = jnp.where(lane16 < S, tiles[0], tiles[1]).astype(BF16)
+            ly[2 * slot + side] = jnp.where(lane16 < S, tiles[0], tiles[1])[0:1]
 
     inv_copy.wait()
     pl.semaphore_wait(barrier, PEERS - 1 + GROUPS - 1)
@@ -219,12 +219,11 @@
     def mixed_out(k):
         return grp_copy(out_mixed.at[k - 1], got_mixed.at[k - 1], 2, k)
 
-    upper8 = iota((16, 128), 0) < 8
-
     @pl.loop(1, PEERS)
     def _(k):
         peer = (me + k) % PEERS
-        s1[peer] = jnp.where(upper8, lx[inv[0, peer]].astype(F32), ly[inv[1, peer]].astype(F32)).astype(BF16)
+        s1[peer, :, 0:128] = lx[inv[0, peer]]
+        s1[peer, :, 128:256] = ly[inv[1, peer]]
         send(s1, r1, 0, peer).start()
 
     for k in range(1, GROUPS):
@@ -285,10 +284,10 @@
 
     all_of(s1, r1, 0).wait_recv()
 
-    def lines(face, row):
-        return jnp.concatenate([r1[owner(slot, face)].astype(F32)[row:row + 1] for slot in range(SLOTS)], axis=0)
-
-    x_lo, x_hi, y_lo, y_hi = lines(0, 0), lines(1, 0), lines(2, 8), lines(3, 8)
+    def lines(face, at):
+        return jnp.concatenate([r1[owner(slot, face), :, at:at + 128] for slot in range(SLOTS)], axis=0)
+
+    x_lo, x_hi, y_lo, y_hi = lines(0, 0), lines(1, 0), lines(2, 128), lines(3, 128)
     quarter8 = lane8 >> 5
     back = [pltpu.roll(part, 128 - S, 1) for part in (x_lo, x_hi, y_lo, y_hi)]
     x_lo, x_hi = pltpu.roll(x_lo, S, 1), pltpu.roll(x_hi, S, 1)
@@ -300,17 +299,21 @@
     z_rows = (four_of(back[1], back[0], back[3], back[2]), four_of(back[0], back[1], back[2], back[3]))
     for slot in range(SLOTS):
         for side in range(2):
-            ey[2 * slot + side] = jnp.broadcast_to(y_rows[side][slot:slot + 1], (16, 128))
-            ez[2 * slot + side] = jnp.broadcast_to(z_rows[side][slot:slot + 1], (16, 128))
+            ey[2 * slot + side] = y_rows[side][slot:slot + 1]
+            ez[2 * slot + side] = z_rows[side][slot:slot + 1]
     row16 = iota((16, 128), 0)
 
     @pl.loop(1, PEERS)
     def _(k):
         peer = (me + k) % PEERS
-        part = fx[inv[0, peer]]
-        first = jnp.where(row16 == 6, ey[inv[1, peer]], jnp.where(row16 == 7, ez[inv[2, peer]], part[:, 0:128].astype(F32)))
-        s3[peer, :, 0:128] = first.astype(BF16)
-        s3[peer, :, 128:512] = part[:, 128:512]
+        s4[peer, :, 0:128] = ey[inv[1, peer]]
+        s4[peer, :, 128:256] = ez[inv[2, peer]]
+        send(s4, r4, 3, peer).start()
+
+    @pl.loop(1, PEERS)
+    def _(k):
+        peer = (me + k) % PEERS
+        s3[peer] = fx[inv[0, peer]]
         send(s3, r3, 2, peer).start()
 
     ready((0,))
@@ -411,12 +414,13 @@
             grads[slot, 3] += sign * ghost[5 * S:6 * S, :]
 
     all_of(s3, r3, 2).wait_recv()
+    all_of(s4, r4, 3).wait_recv()
     item16 = lane16 >> 5
 
     @pl.loop(0, SLOTS)
     def _(slot):
         for side in range(2):
-            edge = r3[owner(slot, 4 + side), :, 0:128].astype(F32)[7:8]
+            edge = r4[owner(slot, 4 + side), :, 128:256]
             one, two = (3, 12) if side == 0 else (11, 4)
             hit = ((row16 == one) & (item16 == 1)) | ((row16 == two) & (item16 == 2))
             edge_in[side, slot] = jnp.where(hit, edge, 0.0).astype(BF16)
@@ -431,7 +435,7 @@
             part = r3[owner(slot, side)].astype(F32)
             halves.append(jnp.concatenate([part[0:8], part[8:16]], axis=1))
         rows = jnp.concatenate(halves, axis=0) + edge_rows[slot]
-        low, top = (jnp.broadcast_to(r3[owner(slot, 2 + side), :, 0:128].astype(F32)[6:7], (16, 128)) for side in range(2))
+        low, top = (jnp.broadcast_to(r4[owner(slot, 2 + side), :, 0:128], (16, 128)) for side in range(2))
         low = jnp.where(row16 == 1, pltpu.roll(low, 96, 1), jnp.where(row16 == 10, pltpu.roll(low, 64, 1), 0.0))
         top = jnp.where(row16 == 2, pltpu.roll(top, 32, 1), jnp.where(row16 == 9, pltpu.roll(top, 64, 1), 0.0))
         low, top = jnp.where(item16 == 0, low, 0.0), jnp.where(item16 == 3, top, 0.0)
@@ -446,7 +450,7 @@
             grads[slot, 0, at:at + 8, :] += diffusivity * extra
             grads[slot, 1, at:at + 8, :] += sign * extra
 
-            edge = r3[owner(slot, 4 + side), :, 0:128].astype(F32)[7:8]
+            edge = r4[owner(slot, 4 + side), :, 128:256]
             third = jnp.sum(jnp.where(lane32 == row32 + 96, edge, 0.0), axis=1, keepdims=True)
             fourth = jnp.sum(jnp.where(lane32 == row32, edge, 0.0), axis=1, keepdims=True)
             third = jnp.where(lane32 == (0 if side == 0 else 127), third, 0.0).astype(BF16)
@@ -502,9 +506,26 @@
                 flow[step, i, :, lanes] = now[i]
             fresh[step, 0, :, lanes], fresh[step, 1, :, lanes] = react(mixed, solid_ref[slot, :, lanes])
 
+    @pl.loop(0, SLOTS - 3)
+    def _(index):
+        slot = rest_slot(index, front)
+
+        @pl.loop(0, CELLS // 128)
+        def _(part):
+            lanes = pl.ds(pl.multiple_of(part * 128, 128), 128)
+            for row in range(0, S, 16):
+                rows = slice(row, row + 16)
+
+                def put(direction, value):
+                    done[index, direction, rows, lanes] = value.astype(BF16)
+
+                f = [moved[slot, d, rows, lanes].astype(F32) for d in range(19)]
+                collide(f, [flow[index, i, rows, lanes] for i in range(4)], solid_ref[slot, rows, lanes], put)
+
     all_of(s1, r1, 0).wait_send()
     all_of(s2, r2, 1).wait_send()
     all_of(s3, r3, 2).wait_send()
+    all_of(s4, r4, 3).wait_send()
     for k in range(1, GROUPS):
         table_copy(k).wait()
         solid_out(k).wait()
@@ -518,8 +539,7 @@
     return pl.pallas_call(
         exchange_kernel,
         out_shape=(
-            jax.ShapeDtypeStruct(populations.shape, BF16),
-            jax.ShapeDtypeStruct((SLOTS - 3, 4, S, CELLS), F32),
+            jax.ShapeDtypeStruct((SLOTS - 3, 19, S, CELLS), BF16),
             jax.ShapeDtypeStruct((SLOTS - 3, 2, S, CELLS), F32),
             jax.ShapeDtypeStruct((GROUPS - 1, S, CELLS), BF16),
             jax.ShapeDtypeStruct((GROUPS - 1, S, CELLS), F32),
@@ -527,24 +547,28 @@
             jax.ShapeDtypeStruct((GROUPS - 1, 1, 128), I32),
         ),
         in_specs=[hbm] * 6,
-        out_specs=(vmem,) * 7,
+        out_specs=(vmem,) * 6,
         scratch_shapes=[
+            pltpu.VMEM((SLOTS, 19, S, CELLS), BF16),
+            pltpu.VMEM((SLOTS - 3, 4, S, CELLS), F32),
             pltpu.VMEM((SLOTS, S, CELLS), F32),
             pltpu.VMEM((SLOTS, S, CELLS), F32),
             pltpu.VMEM((SLOTS, 16, CELLS), BF16),
             pltpu.VMEM((2 * SLOTS, 16, 512), BF16),
             pltpu.VMEM((2 * SLOTS, S, 256), BF16),
             pltpu.VMEM((2 * SLOTS, S, 256), BF16),
-            pltpu.VMEM((2 * SLOTS, 16, 128), BF16),
-            pltpu.VMEM((2 * SLOTS, 16, 128), BF16),
-            pltpu.VMEM((2 * SLOTS, 16, 128), F32),
-            pltpu.VMEM((2 * SLOTS, 16, 128), F32),
-            pltpu.VMEM((PEERS, 16, 128), BF16),
+            pltpu.VMEM((2 * SLOTS, 1, 128), F32),
+            pltpu.VMEM((2 * SLOTS, 1, 128), F32),
+            pltpu.VMEM((2 * SLOTS, 1, 128), F32),
+            pltpu.VMEM((2 * SLOTS, 1, 128), F32),
+            pltpu.VMEM((PEERS, 1, 256), F32),
             pltpu.VMEM((PEERS, S, 384), BF16),
             pltpu.VMEM((PEERS, 16, 512), BF16),
-            pltpu.VMEM((PEERS, 16, 128), BF16),
+            pltpu.VMEM((PEERS, 1, 256), F32),
+            pltpu.VMEM((PEERS, 1, 256), F32),
             pltpu.VMEM((PEERS, S, 384), BF16),
             pltpu.VMEM((PEERS, 16, 512), BF16),
+            pltpu.VMEM((PEERS, 1, 256), F32),
             pltpu.VMEM((1, 128), I32),
             pltpu.VMEM((8, 128), I32),
             pltpu.VMEM((len(TURNS), 8, CELLS), F32),
@@ -562,12 +586,12 @@
             pltpu.SMEM((3,), I32),
             pltpu.SemaphoreType.DMA((19,)),
             pltpu.SemaphoreType.DMA((6,)),
-            pltpu.SemaphoreType.DMA((3,)),
-            pltpu.SemaphoreType.DMA((3,)),
+            pltpu.SemaphoreType.DMA((4,)),
+            pltpu.SemaphoreType.DMA((4,)),
             pltpu.SemaphoreType.DMA((4, GROUPS)),
             pltpu.SemaphoreType.DMA((4, GROUPS)),
         ],
-        compiler_params=pltpu.CompilerParams(collective_id=0, has_side_effects=True, vmem_limit_bytes=28 * 2**20),
+        compiler_params=pltpu.CompilerParams(collective_id=0, has_side_effects=True, vmem_limit_bytes=44 * 2**20),
         cost_estimate=pl.CostEstimate(flops=10**9, bytes_accessed=12 * 10**6, transcendentals=0),
         name="exchange",
     )(*(pltpu.with_memory_space_constraint(operand, pltpu.HBM) for operand in operands))
@@ -593,74 +617,56 @@
         put(2 * pair + 2, even - odd)
 
 
-def collide_kernel(front, table, moved, flow, fresh, got_mixed, got_base, got_solid, solid, new_pop, new_sol, new_solid,
-                   ones, done, placed, sems, pop_sems):
-    ones[...] = jnp.ones(ones.shape, BF16)
+def deal_kernel(front, table, done, fresh, got_mixed, got_base, got_solid, new_pop, new_sol, new_solid, ones, placed, sems):
     copies = []
-    for k in range(3):
-        slot = place_slot(k, front, table)
-        placed[0, k], placed[1, k] = react(got_base[k] + got_mixed[k].astype(F32), got_solid[k])
-        copies.append(pltpu.make_async_copy(ones, new_pop.at[slot], sems.at[0, k]))
-        copies.append(pltpu.make_async_copy(placed.at[0, k], new_sol.at[slot], sems.at[1, k]))
-        copies.append(pltpu.make_async_copy(placed.at[1, k], new_solid.at[slot], sems.at[2, k]))
     for k in range(SLOTS - 3):
         slot = rest_slot(k, front)
+        copies.append(pltpu.make_async_copy(done.at[k], new_pop.at[slot], sems.at[0, 3 + k]))
         copies.append(pltpu.make_async_copy(fresh.at[k, 0], new_sol.at[slot], sems.at[1, 3 + k]))
         copies.append(pltpu.make_async_copy(fresh.at[k, 1], new_solid.at[slot], sems.at[2, 3 + k]))
     for copy in copies:
         copy.start()
-
-    def out(index):
-        return pltpu.make_async_copy(done.at[index], new_pop.at[rest_slot(index, front)], pop_sems.at[index])
-
-    @pl.loop(0, SLOTS - 3)
-    def _(index):
-        slot = rest_slot(index, front)
-        for row in range(0, S, 16):
-            for lane in range(0, CELLS, 128):
-                rows, lanes = slice(row, row + 16), slice(lane, lane + 128)
-
-                def put(direction, value):
-                    done[index, direction, rows, lanes] = value.astype(BF16)
-
-                f = [moved[slot, d, rows, lanes].astype(F32) for d in range(19)]
-                collide(f, [flow[index, i, rows, lanes] for i in range(4)], solid[slot, rows, lanes], put)
-        out(index).start()
+    ones[...] = jnp.ones(ones.shape, BF16)
+    for k in range(3):
+        slot = place_slot(k, front, table)
+        placed[0, k], placed[1, k] = react(got_base[k] + got_mixed[k].astype(F32), got_solid[k])
+        late = [pltpu.make_async_copy(ones, new_pop.at[slot], sems.at[0, k]),
+                pltpu.make_async_copy(placed.at[0, k], new_sol.at[slot], sems.at[1, k]),
+                pltpu.make_async_copy(placed.at[1, k], new_solid.at[slot], sems.at[2, k])]
+        for copy in late:
+            copy.start()
+        copies += late
 
     for copy in copies:
         copy.wait()
-    for index in range(SLOTS - 3):
-        out(index).wait()
-
-
-def collide_all(front, table, moved, flow, fresh, got_mixed, got_base, got_solid, solid_fraction):
+
+
+def deal(front, table, done, fresh, got_mixed, got_base, got_solid):
     smem, vmem, anywhere = (pl.BlockSpec(memory_space=m) for m in (pltpu.SMEM, pltpu.VMEM, pl.ANY))
     return pl.pallas_call(
-        collide_kernel,
+        deal_kernel,
         out_shape=(
-            jax.ShapeDtypeStruct(moved.shape, BF16),
-            jax.ShapeDtypeStruct(solid_fraction.shape, F32),
-            jax.ShapeDtypeStruct(solid_fraction.shape, F32),
+            jax.ShapeDtypeStruct((SLOTS, 19, S, CELLS), BF16),
+            jax.ShapeDtypeStruct((SLOTS, S, CELLS), F32),
+            jax.ShapeDtypeStruct((SLOTS, S, CELLS), F32),
         ),
-        in_specs=[smem] * 2 + [vmem] * 7,
+        in_specs=[smem] * 2 + [vmem] * 5,
         out_specs=(anywhere,) * 3,
         scratch_shapes=[
             pltpu.VMEM((19, S, CELLS), BF16),
-            pltpu.VMEM((SLOTS - 3, 19, S, CELLS), BF16),
             pltpu.VMEM((2, 3, S, CELLS), F32),
             pltpu.SemaphoreType.DMA((3, SLOTS)),
-            pltpu.SemaphoreType.DMA((SLOTS - 3,)),
         ],
-        compiler_params=pltpu.CompilerParams(vmem_limit_bytes=16 * 2**20),
+        compiler_params=pltpu.CompilerParams(vmem_limit_bytes=8 * 2**20),
         cost_estimate=pl.CostEstimate(flops=10**8, bytes_accessed=16 * 10**6, transcendentals=0),
-        name="collide",
-    )(front, table, moved, flow, fresh, got_mixed, got_base, got_solid, solid_fraction)
+        name="deal",
+    )(front, table, done, fresh, got_mixed, got_base, got_solid)
 
 
 def body(populations, solute, solid_fraction, neighbours, front_list, redeal_list):
-    moved, flow, fresh, got_mixed, got_base, got_solid, table = exchange(
+    done, fresh, got_mixed, got_base, got_solid, table = exchange(
         populations, solute, solid_fraction, neighbours, front_list, redeal_list)
-    return collide_all(front_list, table, moved, flow, fresh, got_mixed, got_base, got_solid, solid_fraction)
+    return deal(front_list, table, done, fresh, got_mixed, got_base, got_solid)
 
 
 def solution(mesh):

time: 46.4 us -> 45.4 us (0.978)
  Pallas kernels: 45.6 us -> 44.6 us
    pallas_call x2, Pallas kernels: 45.6 us -> 44.6 us  [the longest x1 39.5 us: exchange(): pl.pallas_call(exchange_kernel, out_shape=(jax.ShapeDtypeStruct((SLOTS -...]
where the time goes in v5:
time: 45.4 us; the launch traced here: 45.3 us
  Pallas kernels  44.6 us (98%)
  between operations  0.66 us (1%)
    pallas_call x1, Pallas kernels, exchange(): pl.pallas_call(exchange_kernel, out_shape=(jax.ShapeDtypeStruct((SLOTS -...  39.5 us
    pallas_call x1, Pallas kernels, deal(): pl.pallas_call(deal_kernel, out_shape=(jax.ShapeDtypeStruct((SLOTS, 19, S...  5.15 us

profile of v5, /device:TPU:7, one launch (start us, length us, event | category | flops | bytes accessed | tf_op | source)
XLA Modules:
  0.0 45.3 jit_solution(153705699277962956)
XLA Ops:
  0.6 0.0 copy-start
  0.6 39.5 %exchange.1 = (bf16[5,19,32,1024]{3,2,1,0:T(8,128)(2,1)S(1)}, f32[5,2,32,1024]{3,2,1,0:T(8,128)S(1)}, bf16[3,32,1024]{2,1,0:T(8,128)(2,1)S(1)}, f32[3,32,1024]{2...) custom-call(bf16[8,19,32,1024]{3,2,1,0:T(8,128)(2,1)} %pop_hbm.1, f32[8,32,1024]{2,1,0:T(8,128)} %sol_hbm.1, ...), custom_call_target="tpu_custom_call" | custom-call | flops 1000000000 | bytes 12000000 | tf_op jit(solution)/shard_map/exchange/pallas_call | solution.py:539
  40.1 0.0 copy-done
  40.1 5.1 %deal.1 = (bf16[8,19,32,1024]{3,2,1,0:T(8,128)(2,1)}, f32[8,32,1024]{2,1,0:T(8,128)}, f32[8,32,1024]{2,1,0:T(8,128)}) custom-call(s32[3]{0:T(128)S(1)} %copy-done, s32[3,1,128]{2,1,0:T(1,128)S(1)} %get-tuple-element.9.table, bf16[5,19,32,1024]{3,2,1,0:T(8,128)(2,1)S(1)} %get-tuple-element.10.done, f32[5,2,32,1024]{3,2,1,0:T(8,128)S(1)} %get-tuple-element.11.fresh, ...), custom_call_target="tpu_custom_call" | custom-call | flops 100000000 | bytes 16000000 | tf_op jit(solution)/shard_map/deal/pallas_call | solution.py:646
Async XLA Ops:
  0.6 39.5 %copy-start = (s32[3]{0:T(128)S(1)}, s32[3]{0:T(128)}, u32[]{:S(2)}) copy-start(s32[3]{0:T(128)} %front.1) | copy-start | bytes 40
